TPU v7x, 32 devices: a whole 2x2x4 slice. The times are simulated.
32 devices in a mesh: blk: 8 (over z, y), sp: 4 (over x, core).
Axes of the slice: x: 2, y: 2, z: 4, core: 2. Of those that a mesh axis runs over, the one named last changes fastest.
Arguments:
- species: float32 [8, 256, 4096], P('sp', 'blk'), may hold values from 0 to 0.25
- interface_normal_flow: float32 [3, 256, 4096], P(None, 'blk'), may hold values from -6 to 6
- face_diffusion: float32 [3, 256, 4096], P(None, 'blk'), may hold values from 0.3 to 3
- inv_volume: float32 [256, 4096], P('blk'), may hold values from 0.5 to 2
- diffusivity: float32 [8], P('sp'), may hold values from 0.2 to 2
- low_partner: int32 [8, 64], P('blk'), may hold values from 0 to 7, as said below
- high_partner: int32 [8, 64], P('blk'), may hold values from 0 to 7, as said below
- low_orient: int32 [8, 64], P('blk'), may hold values from 0 to 7
- high_orient: int32 [8, 64], P('blk'), may hold values from 0 to 7, as said below
- droplet_table: float32 [8192, 128], P(('blk', 'sp')), may hold values from -6 to 6
- parcel_block: int32 [8192, 1], P(('blk', 'sp')), may hold values from 0 to 7; in each aligned block of 256 rows (0 to 255, 256 to 511, ...) at most 48 rows name the same one
- parcel_cell: int32 [8192], P(('blk', 'sp')), may hold values from 0 to 131071
- parcel_live: int32 [8192], P(('blk', 'sp')), may hold values 0 or 1
Outputs:
- new_species: float32 [8, 256, 4096], P('sp', 'blk')
- arrived: float32 [12288, 128], P(('blk', 'sp'))
Inputs may be any that keep to these rules, and one draw needn't show every extreme that they name: low_partner: in each row no block appears more than 8 times and some block appears exactly 8 times; high_partner[c, t] = b exactly when low_partner[b, t] = c. high_partner: in each row no block appears more than 8 times and some block appears exactly 8 times. high_orient[c, t] = low_orient[high_partner[c, t], t]. parcel_block: among the slots of one device no block is named more than 48 times.
All inputs are finite; a program needn't handle non-finite values. No bound on the sum of `parcel_live` on one device may be relied on, other than what follows from the above.
Results may differ from a plain program's by a relative error of at most 0.00002.
Values sent between devices are 32-bit elements; how exact they have to be, the bound alone decides.
No kernel may reach another device: no remote copies, remote signals or barrier semaphores. Data moves between devices by JAX's collectives and lax.ppermute only.
A program may use at most 192 MiB of HBM per device.

v0:
```python
import jax
import jax.numpy as jnp
from jax import lax
from jax.sharding import PartitionSpec as P

PV = 128
BJ = 64
BK = 64
TILE_SIDE = 8
TILES = 64


section_step = 0.5
friction_timescale = 0.3


def spread(value, axis, source):
    kept = jnp.where(lax.axis_index(axis) == source, value, 0).astype(value.dtype)
    return lax.psum(kept, axis)


def face_tiles(face):
    leading = face.shape[:-1]
    levels = len(leading)
    blocked = face.reshape(leading + (BJ // TILE_SIDE, TILE_SIDE, BK // TILE_SIDE, TILE_SIDE))
    axes_order = tuple(range(levels)) + (levels, levels + 2, levels + 1, levels + 3)
    return jnp.transpose(blocked, axes_order).reshape(leading + (TILES, TILE_SIDE * TILE_SIDE))


def tile_face(tiles):
    leading = tiles.shape[:-2]
    levels = len(leading)
    blocked = tiles.reshape(leading + (BJ // TILE_SIDE, BK // TILE_SIDE, TILE_SIDE, TILE_SIDE))
    axes_order = tuple(range(levels)) + (levels, levels + 2, levels + 1, levels + 3)
    return jnp.transpose(blocked, axes_order).reshape(leading + (BJ * BK,))


def orient(tiles, codes, inverse):
    square = tiles.reshape(tiles.shape[:-1] + (TILE_SIDE, TILE_SIDE))
    selector = codes[..., None, None, None]
    transposed = selector // 4 % 2 == 1
    flip_rows = selector % 2 == 1
    flip_columns = selector // 2 % 2 == 1
    if not inverse:
        square = jnp.where(transposed, jnp.swapaxes(square, -1, -2), square)
    square = jnp.where(flip_rows, jnp.flip(square, -2), square)
    square = jnp.where(flip_columns, jnp.flip(square, -1), square)
    if inverse:
        square = jnp.where(transposed, jnp.swapaxes(square, -1, -2), square)
    return square.reshape(tiles.shape)


def droplet_motion_update(droplet_table, evaporate_component, ambient_flow_speed, alive_indicator):
    boiled_off_quantity = (
        jax.nn.softplus(droplet_table[:, 1])
        * (jax.nn.sigmoid(droplet_table[:, 2]) - evaporate_component)
        * alive_indicator
    )
    shifted_droplet_list = droplet_table.at[:, 0].add(-boiled_off_quantity)
    shifted_droplet_list = shifted_droplet_list.at[:, 3:6].add(
        friction_timescale * (jnp.transpose(ambient_flow_speed) - droplet_table[:, 3:6])
    )
    return (boiled_off_quantity, shifted_droplet_list * alive_indicator[:, None])


def matched_rank(targets, blocks):
    onehot = (targets[:, None] == jnp.arange(blocks)[None, :]).astype(jnp.int32)
    return jnp.sum((jnp.cumsum(onehot, axis=0) - onehot) * onehot, axis=1)


def face_flux(velocity, diffusion, scaled, difference, middle, weight):
    return velocity * middle - diffusion * (scaled * difference - middle * weight)


def body(
    species,
    interface_normal_flow,
    face_diffusion,
    inv_volume,
    diffusivity,
    low_partner,
    high_partner,
    low_orient,
    high_orient,
    droplet_table,
    parcel_block,
    parcel_cell,
    parcel_live,
):
    blocks = lax.axis_size("blk")
    layers = species.shape[1]
    local_species = species.shape[0]
    low_face = jnp.concatenate(
        [species[:, 0], interface_normal_flow[0:1, 0], face_diffusion[0:1, 0]], axis=0
    )
    low_pack = jnp.transpose(face_tiles(low_face), (1, 0, 2))
    high_pack = jnp.transpose(face_tiles(species[:, layers - 1]), (1, 0, 2))
    low_source = low_partner[0]
    high_source = high_partner[0]
    tile_cap = max(1, TILES // blocks)
    low_rank = matched_rank(low_source, blocks)
    high_rank = matched_rank(high_source, blocks)
    send_high = (
        jnp.zeros((blocks, tile_cap) + high_pack.shape[1:], jnp.float32)
        .at[high_source, high_rank]
        .set(high_pack)
    )
    send_low = (
        jnp.zeros((blocks, tile_cap) + low_pack.shape[1:], jnp.float32)
        .at[low_source, low_rank]
        .set(low_pack)
    )
    got_high, got_low = (
        lax.all_to_all(send_high, "blk", split_axis=0, concat_axis=0, tiled=True),
        lax.all_to_all(send_low, "blk", split_axis=0, concat_axis=0, tiled=True),
    )
    picked_high = got_high[low_source, low_rank]
    picked_low = got_low[high_source, high_rank]
    ghost_low = tile_face(jnp.transpose(orient(picked_high, low_orient[0], False), (1, 0, 2)))
    ghost_high = tile_face(jnp.transpose(orient(picked_low, high_orient[0], True), (1, 0, 2)))
    parcel_rows = droplet_table.shape[0]
    parcel_cap = 3 * parcel_rows // (2 * blocks)
    target_block = parcel_block[:, 0]
    active_rows = parcel_live == 1
    onehot = ((target_block[:, None] == jnp.arange(blocks)[None, :]) & active_rows[:, None]).astype(
        jnp.int32
    )
    rank_before = jnp.sum((jnp.cumsum(onehot, axis=0) - onehot) * onehot, axis=1)
    slot_index = jnp.where(
        active_rows, target_block * parcel_cap + rank_before, blocks * parcel_cap
    )
    send_rows = (
        jnp.zeros((blocks * parcel_cap, PV), jnp.float32)
        .at[slot_index]
        .set(droplet_table, mode="drop")
        .reshape(blocks, parcel_cap, PV)
    )
    send_cells = (
        jnp.zeros((blocks * parcel_cap,), jnp.int32)
        .at[slot_index]
        .set(parcel_cell, mode="drop")
        .reshape(blocks, parcel_cap)
    )
    send_flags = (
        jnp.zeros((blocks * parcel_cap,), jnp.int32)
        .at[slot_index]
        .set(parcel_live, mode="drop")
        .reshape(blocks, parcel_cap)
    )
    got_rows, got_cells, received_flags = (
        lax.all_to_all(send_rows, "blk", split_axis=0, concat_axis=0, tiled=True),
        lax.all_to_all(send_cells, "blk", split_axis=0, concat_axis=0, tiled=True),
        lax.all_to_all(send_flags, "blk", split_axis=0, concat_axis=0, tiled=True),
    )
    inbound_droplet_list = got_rows.reshape(blocks * parcel_cap, PV)
    landing_grid_points = got_cells.reshape(-1)
    alive_indicator = received_flags.reshape(-1).astype(jnp.float32)
    fuel_local = species[0].reshape(-1)
    fuel_field = spread(fuel_local, "sp", 0)
    evaporate_component = fuel_field[landing_grid_points]
    ambient_flow_speed = interface_normal_flow.reshape(3, -1)[:, landing_grid_points]
    boiled_off_quantity, shifted_droplet_list = droplet_motion_update(
        inbound_droplet_list, evaporate_component, ambient_flow_speed, alive_indicator
    )
    source = (
        jnp.zeros((layers * BJ * BK,), jnp.float32).at[landing_grid_points].add(boiled_off_quantity)
    )
    total_source = lax.psum(source, "sp").reshape(layers, BJ * BK)
    scaled_face = diffusivity[:, None]
    scaled_field = diffusivity[:, None, None]
    ghost_top = ghost_high[:local_species]
    bottom_layer = species[:, 0]
    top_layer = species[:, layers - 1]
    bottom_diff = bottom_layer - ghost_low
    bottom_mean = 0.5 * (bottom_layer + ghost_low)
    inner_diff = species[:, 1:] - species[:, :-1]
    inner_mean = 0.5 * (species[:, 1:] + species[:, :-1])
    top_diff = ghost_top - top_layer
    top_mean = 0.5 * (ghost_top + top_layer)
    previous_row = jnp.roll(species, BK, axis=-1)
    previous_column = jnp.roll(species, 1, axis=-1)
    row_diff = species - previous_row
    row_mean = 0.5 * (species + previous_row)
    column_diff = species - previous_column
    column_mean = 0.5 * (species + previous_column)
    partial_terms = (
        jnp.sum(scaled_face * bottom_diff, axis=0),
        jnp.sum(scaled_field * inner_diff, axis=0),
        jnp.sum(scaled_face * top_diff, axis=0),
        jnp.sum(scaled_field * row_diff, axis=0),
        jnp.sum(scaled_field * column_diff, axis=0),
    )
    weight_bottom, weight_inner, weight_top, weight_row, weight_column = lax.psum(
        (partial_terms[0], partial_terms[1], partial_terms[2], partial_terms[3], partial_terms[4]),
        "sp",
    )
    flux_bottom = face_flux(
        interface_normal_flow[0, 0],
        face_diffusion[0, 0],
        scaled_face,
        bottom_diff,
        bottom_mean,
        weight_bottom,
    )
    flux_inner = face_flux(
        interface_normal_flow[0, 1:],
        face_diffusion[0, 1:],
        scaled_field,
        inner_diff,
        inner_mean,
        weight_inner,
    )
    flux_top = face_flux(
        ghost_high[local_species],
        ghost_high[local_species + 1],
        scaled_face,
        top_diff,
        top_mean,
        weight_top,
    )
    cell_index = jnp.arange(BJ * BK)
    wall_rows = cell_index // BK == 0
    wall_columns = cell_index % BK == 0
    flux_row = jnp.where(
        wall_rows,
        0.0,
        face_flux(
            interface_normal_flow[1],
            face_diffusion[1],
            scaled_field,
            row_diff,
            row_mean,
            weight_row,
        ),
    )
    flux_column = jnp.where(
        wall_columns,
        0.0,
        face_flux(
            interface_normal_flow[2],
            face_diffusion[2],
            scaled_field,
            column_diff,
            column_mean,
            weight_column,
        ),
    )
    divergence = (
        jnp.roll(flux_row, -BK, axis=-1)
        - flux_row
        + (jnp.roll(flux_column, -1, axis=-1) - flux_column)
    )
    divergence = divergence.at[:, : layers - 1].add(flux_inner)
    divergence = divergence.at[:, 1:].add(-flux_inner)
    divergence = divergence.at[:, 0].add(-flux_bottom)
    divergence = divergence.at[:, layers - 1].add(flux_top)
    global_index = lax.axis_index("sp") * local_species + jnp.arange(local_species)
    is_fuel = (global_index == 0).astype(jnp.float32)[:, None, None]
    tendency = inv_volume * (total_source * (is_fuel - species) - divergence)
    new_species = species + section_step * tendency
    return (new_species, shifted_droplet_list)


def solution(mesh):
    placed = (
        P("sp", "blk", None),
        P(None, "blk", None),
        P(None, "blk", None),
        P("blk", None),
        P("sp"),
        P("blk", None),
        P("blk", None),
        P("blk", None),
        P("blk", None),
        P(("blk", "sp"), None),
        P(("blk", "sp"), None),
        P(("blk", "sp")),
        P(("blk", "sp")),
    )
    return jax.shard_map(
        body,
        mesh=mesh,
        in_specs=placed,
        out_specs=(P("sp", "blk", None), P(("blk", "sp"), None)),
        check_vma=False,
    )
```

profile of v0, /device:TPU:0, one launch (start us, length us, event | category | flops | bytes accessed | tf_op | source)
XLA Modules:
  0.0 248.9 jit_solution(10332376365897104924)
XLA Ops:
  13.8 7.3 %all-to-all-start = ((s32[8,1,48]{2,1,0:T(1,128)}), s32[8,1,48]{2,1,0:T(1,128)S(1)}, u32[]{:S(2)}, u32[]{:S(2)}) async-start(s32[8,1,48]{2,1,0:T(1,128)} %all_to_all.21), calls=%async_computation | async-start | bytes 8192 | tf_op jit(solution)/shard_map/all_to_all | solution.py:152
  24.8 2.9 %slice_bitcast_fusion.1 = (f32[32,4096]{1,0:T(8,128)}, f32[32,4096]{1,0:T(8,128)}, f32[32,4096]{1,0:T(8,128)}, f32[32,4096]{1,0:T(8,128)}) fusion(f32[3,32,4096]{2,1,0:T(8,128)} %param.27, f32[3,32,4096]{2,1,0:T(8,128)} %param.26), kind=kLoop, calls=%fused_computation.31 | loop fusion | flops 262144 | bytes 4194304 | tf_op jit(solution)/shard_map/mul | solution.py:72
  27.7 2.3 slice_bitcast_fusion
  31.7 2.7 %fusion.61 = (f32[31,4096]{1,0:T(8,128)}, f32[2,31,4096]{2,0,1:T(2,128)}) fusion(f32[2,32,4096]{2,0,1:T(2,128)S(1)} %copy.103, f32[2]{0:T(128)S(1)} %copy-done.26), kind=kLoop, calls=%fused_computation.180 | loop fusion | flops 634880 | bytes 3555336 | tf_op jit(solution)/shard_map/reduce_sum | solution.py:188
  39.8 5.2 %fusion.58 = (f32[32,4096]{1,0:T(8,128)}, f32[32,4096]{1,0:T(8,128)}) fusion(f32[2,32,4095]{2,0,1:T(2,128)S(1)} %bitcast.174, f32[2,32,1]{2,0,1:T(2,128)S(1)} %slice.289, f32[2]{0:T(128)S(1)} %copy-done.26, f32[2,32,4096]{2,1,0:T(8,128)S(1)} %copy-done, f32[2,32,4032]{2,0,1:T(2,128)S(1)} %bitcast.175, f32[2,32,64]{2,0,1:T(2,128)S(1)} %slice.285), kind=kLoop, calls=%fused_computation.179 | loop fusion | flops 1835008 | bytes 4194312 | tf_op jit(solution)/shard_map/reduce_sum | solution.py:191
  47.2 32.0 %copy.106 = f32[3,32,4096]{0,2,1:T(8,128)} copy(f32[3,32,4096]{2,1,0:T(8,128)} %param.26) | data formatting | bytes 3145728 | tf_op args[1]
  82.6 2.2 scatter_custom_fusion.1
  84.8 3.1 %scatter_fusion.1 = f32[8,8,4,64]{3,2,1,0:T(4,128)S(1)} fusion(f32[8,8,4,64]{3,2,1,0:T(4,128)S(1)} %broadcast_in_dim.113, s32[64]{0:T(128)S(1)} %get-tuple-element.124, f32[64,4,64]{2,1,0:T(4,128)S(1)} %copy.98), kind=kCustom, calls=%fused_computation.9 | custom fusion | bytes 197120 | tf_op jit(solution)/shard_map/scatter | solution.py:111
  89.4 3.1 %scatter_fusion = f32[8,8,2,64]{3,2,1,0:T(2,128)S(1)} fusion(f32[8,8,2,64]{3,2,1,0:T(2,128)S(1)} %broadcast_in_dim.109, s32[64]{0:T(128)S(1)} %get-tuple-element.92, f32[64,2,64]{2,1,0:T(2,128)S(1)} %copy.91), kind=kCustom, calls=%fused_computation.8 | custom fusion | bytes 98816 | tf_op jit(solution)/shard_map/scatter | solution.py:106
  94.7 5.9 %all-to-all-start.2 = ((s32[8,1,48]{2,1,0:T(1,128)}), s32[8,1,48]{2,1,0:T(1,128)S(1)}, u32[]{:S(2)}, u32[]{:S(2)}) async-start(s32[8,1,48]{2,1,0:T(1,128)} %all_to_all.24), calls=%async_computation.2 | async-start | bytes 8192 | tf_op jit(solution)/shard_map/all_to_all | solution.py:153
  101.9 5.2 %all-to-all-done.2 = s32[8,1,48]{2,1,0:T(1,128)S(1)} async-done(((s32[8,1,48]{2,1,0:T(1,128)}), s32[8,1,48]{2,1,0:T(1,128)S(1)}, u32[]{:S(2)}, u32[]{:S(2)}) %all-to-all-start.2) | async-done | bytes 1568 | tf_op jit(solution)/shard_map/all_to_all | solution.py:153
  107.1 3.3 %all-to-all-start.3 = ((f32[8,1,1024]{2,1,0:T(1,128)}), f32[8,1,1024]{2,1,0:T(1,128)S(1)}, u32[]{:S(2)}, u32[]{:S(2)}) async-start(f32[8,1,1024]{2,1,0:T(1,128)} %reshape.943), calls=%async_computation.3 | async-start | bytes 65536 | tf_op jit(solution)/shard_map/all_to_all | solution.py:114
  110.7 11.1 %gather_fusion.3 = f32[384,3]{1,0:T(8,128)} fusion(f32[3,131072]{0,1:T(8,128)} %bitcast.43, s32[1024]{0:T(1024)S(1)} %pad_clamp_fusion), kind=kCustom, calls=%fused_computation.3 | custom fusion | bytes 10752 | tf_op jit(solution)/shard_map/gather | solution.py:161
  121.8 5.3 %all-to-all-start.4 = ((f32[8,1,2048]{2,1,0:T(1,128)}), f32[8,1,2048]{2,1,0:T(1,128)}, u32[]{:S(2)}, u32[]{:S(2)}) async-start(f32[8,1,2048]{2,1,0:T(1,128)} %reshape.945), calls=%async_computation.4 | async-start | bytes 131072 | tf_op jit(solution)/shard_map/all_to_all | solution.py:115
  134.7 6.0 %all-to-all-start.1 = ((f32[8,48,128]{2,1,0:T(8,128)}), f32[8,48,128]{2,1,0:T(8,128)S(1)}, u32[]{:S(2)}, u32[]{:S(2)}) async-start(f32[8,48,128]{2,1,0:T(8,128)} %bitcast.190), calls=%async_computation.1 | async-start | bytes 393216 | tf_op jit(solution)/shard_map/all_to_all | solution.py:151
  146.7 2.6 %copy.102 = f32[4,8,8,8,8]{4,2,3,1,0:T(8,128)} copy(f32[4,8,8,8,8]{2,1,4,3,0:T(8,128)} %reshape.901) | data formatting | bytes 131072 | tf_op jit(solution)/shard_map/reshape | solution.py:33
  149.3 2.7 %fusion.63 = (f32[2,8,8,8,8]{4,3,2,1,0:T(8,128)}, f32[8,8,8,8]{3,2,1,0:T(8,128)}) fusion(f32[4,8,8,8,8]{4,3,2,1,0:T(8,128)} %bitcast.182, f32[2,8,8,8,8]{4,3,2,1,0:T(8,128)S(1)} %reshape_squeeze.4, f32[2]{0:T(128)S(1)} %copy-done.26), kind=kLoop, calls=%fused_computation.182 | loop fusion | flops 20480 | bytes 114696 | tf_op jit(solution)/shard_map/slice | solution.py:171
  151.9 11.6 %gather_fusion = f32[384]{0:T(512)S(1)} fusion(f32[131072]{0:T(1024)} %all-reduce.5.cloned.1.call-done, s32[1024]{0:T(1024)S(1)} %pad_clamp_fusion), kind=kCustom, calls=%fused_computation | custom fusion | bytes 4608 | tf_op jit(solution)/shard_map/gather | solution.py:160
  165.2 4.5 %scatter_custom_fusion.3 = f32[131072]{0:T(1024)} fusion(s32[384]{0:T(512)} %copy-done.31, f32[384]{0:T(512)S(1)} %fusion.37, f32[]{:T(128)} %constant.289.clone.1), kind=kCustom, calls=%fused_computation.42 | custom fusion | flops 384 | bytes 524800 | tf_op jit(solution)/shard_map/scatter-add | solution.py:166
  169.7 2.0 mul.324
  178.5 12.3 %all-reduce = (f32[4096]{0:T(1024)S(1)}, f32[4096]{0:T(1024)S(1)}) all-reduce(f32[4096]{0:T(1024)S(1)} %copy-done.20, f32[4096]{0:T(1024)S(1)} %reduce_sum.88), channel_id=1, replica_groups=mesh['blk'=8,'sp'=4] {'sp'}, use_global_device_ids=true, to_apply=%region_21.22 | all-reduce | flops 8192 | bytes 65536 | tf_op jit(solution)/shard_map/psum | solution.py:193
  198.0 27.1 %all-reduce.7.cloned.1.call-done = (f32[32,4096]{1,0:T(8,128)}, f32[32,4096]{1,0:T(8,128)}, f32[31,4096]{1,0:T(8,128)}, f32[32,4096]{1,0:T(8,128)}) async-done(((f32[32,4096]{1,0:T(8,128)}, f32[32,4096]{1,0:T(8,128)}, f32[31,4096]{1,0:T(8,128)}, f32[32,4096]{1,0:T(8,128)}), (f32[32,4096]{1,0:T(8,128)}, f32[32,4096]{1,0:T(8,128)}, f32[31,4096]{1,0:T(8,128)}, ...) | async-done | bytes 2080784 | tf_op jit(solution)/shard_map/psum | solution.py:193
  226.6 4.3 %subtract_select_fusion = (f32[2,32,4096]{2,0,1:T(2,128)S(1)}, f32[2,32,4096]{2,0,1:T(2,128)S(1)}) fusion(pred[4096]{0:T(1024)(128)(4,1)S(1)} %copy-done.30, f32[32,4096]{1,0:T(8,128)S(1)} %get-tuple-element.128, f32[32,4096]{1,0:T(8,128)S(1)} %copy-done.3, f32[32,4096]{1,0:T(8,128)S(1)} %copy-done.6, f32[2,32,4095]{2,0,1:T(2,128)S(1)} %bitcast.176, ...), kind=kLoop, calls=%fused_computation.17 | loop fusion | flops 5242880 | bytes 8396808 | tf_op jit(solution)/shard_map/jit(_where)/select_n | solution.py:236
  235.3 2.1 fusion.2
  (189 shorter events, 67.4 us)
Async XLA Ops:
  7.2 16.0 %copy-start = (f32[2,32,4096]{2,1,0:T(8,128)S(1)}, f32[2,32,4096]{2,1,0:T(8,128)}, u32[]{:S(2)}) copy-start(f32[2,32,4096]{2,1,0:T(8,128)} %param.25) | copy-start | bytes 3145732
  13.8 80.9 %all-to-all-start = ((s32[8,1,48]{2,1,0:T(1,128)}), s32[8,1,48]{2,1,0:T(1,128)S(1)}, u32[]{:S(2)}, u32[]{:S(2)}) async-start(s32[8,1,48]{2,1,0:T(1,128)} %all_to_all.21), calls=%async_computation | async-start | bytes 8192 | tf_op jit(solution)/shard_map/all_to_all | solution.py:152
  21.1 130.8 %all-reduce.5.cloned.1.call-start = ((), (), s32[]{:S(2)}) async-start(), calls=%async_computation.5 | async-start | bytes 1048576 | tf_op jit(solution)/shard_map/psum | solution.py:19
  24.1 15.7 %copy-start.13 = (f32[2,32,64]{2,0,1:T(2,128)}, f32[2,32,64]{2,0,1:T(2,128)S(1)}, u32[]{:S(2)}) copy-start(f32[2,32,64]{2,0,1:T(2,128)S(1)} %slice.285) | copy-start | bytes 49156
  24.2 15.6 %copy-start.15 = (f32[2,32,1]{2,0,1:T(2,128)}, f32[2,32,1]{2,0,1:T(2,128)S(1)}, u32[]{:S(2)}) copy-start(f32[2,32,1]{2,0,1:T(2,128)S(1)} %slice.289) | copy-start | bytes 772
  31.6 6.3 %copy-start.35 = (s32[1,64]{1,0:T(1,128)S(1)}, s32[1,64]{1,0:T(1,128)}, u32[]{:S(2)}) copy-start(s32[1,64]{1,0:T(1,128)} %param.32) | copy-start | bytes 772
  31.7 6.3 %copy-start.36 = (s32[1,64]{1,0:T(1,128)S(1)}, s32[1,64]{1,0:T(1,128)}, u32[]{:S(2)}) copy-start(s32[1,64]{1,0:T(1,128)} %param.33) | copy-start | bytes 772
  94.7 12.4 %all-to-all-start.2 = ((s32[8,1,48]{2,1,0:T(1,128)}), s32[8,1,48]{2,1,0:T(1,128)S(1)}, u32[]{:S(2)}, u32[]{:S(2)}) async-start(s32[8,1,48]{2,1,0:T(1,128)} %all_to_all.24), calls=%async_computation.2 | async-start | bytes 8192 | tf_op jit(solution)/shard_map/all_to_all | solution.py:153
  101.9 25.8 %copy-start.31 = (s32[384]{0:T(512)}, s32[384]{0:T(512)S(1)}, u32[]{:S(2)}) copy-start(s32[384]{0:T(512)S(1)} %fusion.38) | copy-start | bytes 4612
  107.1 14.7 %all-to-all-start.3 = ((f32[8,1,1024]{2,1,0:T(1,128)}), f32[8,1,1024]{2,1,0:T(1,128)S(1)}, u32[]{:S(2)}, u32[]{:S(2)}) async-start(f32[8,1,1024]{2,1,0:T(1,128)} %reshape.943), calls=%async_computation.3 | async-start | bytes 65536 | tf_op jit(solution)/shard_map/all_to_all | solution.py:114
  110.7 54.5 %copy-start.28 = (f32[384]{0:T(512)}, f32[384]{0:T(512)S(1)}, u32[]{:S(2)}) copy-start(f32[384]{0:T(512)S(1)} %convert_element_type.43) | copy-start | bytes 4612
  121.8 12.9 %all-to-all-start.4 = ((f32[8,1,2048]{2,1,0:T(1,128)}), f32[8,1,2048]{2,1,0:T(1,128)}, u32[]{:S(2)}, u32[]{:S(2)}) async-start(f32[8,1,2048]{2,1,0:T(1,128)} %reshape.945), calls=%async_computation.4 | async-start | bytes 131072 | tf_op jit(solution)/shard_map/all_to_all | solution.py:115
  134.7 28.9 %all-to-all-start.1 = ((f32[8,48,128]{2,1,0:T(8,128)}), f32[8,48,128]{2,1,0:T(8,128)S(1)}, u32[]{:S(2)}, u32[]{:S(2)}) async-start(f32[8,48,128]{2,1,0:T(8,128)} %bitcast.190), calls=%async_computation.1 | async-start | bytes 393216 | tf_op jit(solution)/shard_map/all_to_all | solution.py:151
  140.7 84.4 %all-reduce.7.cloned.1.call-start = ((), (), s32[]{:S(2)}) async-start(), calls=%async_computation.6 | async-start | bytes 4194304 | tf_op jit(solution)/shard_map/psum | solution.py:193
  171.8 6.7 %copy-start.20 = (f32[4096]{0:T(1024)S(1)}, f32[4096]{0:T(1024)}, u32[]{:S(2)}) copy-start(f32[4096]{0:T(1024)} %fusion.19) | copy-start | bytes 49156
  172.6 19.4 %copy-start.9 = (f32[384,1]{1,0:T(8,128)S(1)}, f32[384,1]{1,0:T(8,128)}, u32[]{:S(2)}) copy-start(f32[384,1]{1,0:T(8,128)} %get-tuple-element.114) | copy-start | bytes 4612
  172.7 20.3 %copy-start.17 = (f32[384,3]{1,0:T(8,128)S(1)}, f32[384,3]{1,0:T(8,128)}, u32[]{:S(2)}) copy-start(f32[384,3]{1,0:T(8,128)} %gather_fusion.3) | copy-start | bytes 13828
  194.5 31.9 %copy-start.3 = (f32[32,4096]{1,0:T(8,128)S(1)}, f32[32,4096]{1,0:T(8,128)}, u32[]{:S(2)}) copy-start(f32[32,4096]{1,0:T(8,128)} %get-tuple-element.104) | copy-start | bytes 1572868
  194.5 32.0 %copy-start.4 = (f32[32,4096]{1,0:T(8,128)S(1)}, f32[32,4096]{1,0:T(8,128)}, u32[]{:S(2)}) copy-start(f32[32,4096]{1,0:T(8,128)} %get-tuple-element.105) | copy-start | bytes 1572868
  194.5 32.0 %copy-start.14 = (f32[2,32,64]{2,0,1:T(2,128)S(1)}, f32[2,32,64]{2,0,1:T(2,128)}, u32[]{:S(2)}) copy-start(f32[2,32,64]{2,0,1:T(2,128)} %copy-done.13) | copy-start | bytes 49156
  194.5 32.0 %copy-start.16 = (f32[2,32,1]{2,0,1:T(2,128)S(1)}, f32[2,32,1]{2,0,1:T(2,128)}, u32[]{:S(2)}) copy-start(f32[2,32,1]{2,0,1:T(2,128)} %copy-done.15) | copy-start | bytes 772
  194.5 32.0 %copy-start.27 = (f32[2]{0:T(128)S(1)}, f32[2]{0:T(128)}, u32[]{:S(2)}) copy-start(f32[2]{0:T(128)} %param.29) | copy-start | bytes 28
  194.5 32.0 %copy-start.29 = (pred[4096]{0:T(1024)(128)(4,1)S(1)}, pred[4096]{0:T(1024)(128)(4,1)}, u32[]{:S(2)}) copy-start(pred[4096]{0:T(1024)(128)(4,1)} %get-tuple-element.132) | copy-start | bytes 12292
  194.6 32.0 %copy-start.30 = (pred[4096]{0:T(1024)(128)(4,1)S(1)}, pred[4096]{0:T(1024)(128)(4,1)}, u32[]{:S(2)}) copy-start(pred[4096]{0:T(1024)(128)(4,1)} %get-tuple-element.133) | copy-start | bytes 12292
  (20 other events, 40.0 us)
Sparse Core Ops, SparseCore 0:
  24.3 34.5 all-reduce.4
  171.9 53.1 all-reduce.6
where the time goes:
time: 253 us; the launch traced here: 249 us
  local copies, waits for them, and re-layouts  103 us (41%)
  other arithmetic  58.6 us (23%)
  waiting for transfers between devices  32.3 us (13%)
  starting transfers between devices  27.9 us (11%)
  between operations  14.9 us (6%)
  blocking collectives  12.3 us (5%)
    unnamed x83, local copies, waits for them, and re-layouts  37.2 us
    psum x1, waiting for transfers between devices, body(): lax.psum((partial_terms[0], partial_terms[1], partial_terms[2], partial_t...  27.1 us
    psum x1, blocking collectives, body(): lax.psum((partial_terms[0], partial_terms[1], partial_terms[2], partial_t...  12.3 us
    gather x1, local copies, waits for them, and re-layouts, body(): evaporate_component = fuel_field[landing_grid_points]  11.6 us
    gather x1, local copies, waits for them, and re-layouts, body(): interface_normal_flow.reshape(3, -1)[:, landing_grid_points]  11.1 us
    all_to_all x1, starting transfers between devices, body(): lax.all_to_all(send_cells, 'blk', split_axis=0, concat_axis=0, tiled=True)  7.28 us
    all_to_all x1, starting transfers between devices, body(): lax.all_to_all(send_rows, 'blk', split_axis=0, concat_axis=0, tiled=True)  6 us
    all_to_all x1, starting transfers between devices, body(): lax.all_to_all(send_flags, 'blk', split_axis=0, concat_axis=0, tiled=True)  5.92 us
  transfers between devices with their start and end apart: 7, of which 2 were waited for; matrix products, arithmetic and copies ran while one was open for 52% of the time, Pallas kernels for 0%

commit v1 on v0

v1 whole, which is shorter than its diff:
```python
import functools

import jax
import jax.numpy as jnp
import ml_dtypes
import numpy as np
from jax import lax
from jax.experimental import pallas as pl
from jax.experimental.pallas import tpu as pltpu
from jax.sharding import PartitionSpec as P

PV = 128
BJ = 64
BK = 64
TILE_SIDE = 8
TILES = 64
LANES = 128
FACE = BJ * BK
STRIP = TILE_SIDE * BK
PAIRS = 4

section_step = 0.5
friction_timescale = 0.3

F32 = jnp.float32
BF16 = jnp.bfloat16
VMEM_LIMIT = 63 * 1024 * 1024


def orient_table(inverse):
    table = np.zeros((8, 64, 64), np.float32)
    for code in range(8):
        for r in range(8):
            for c in range(8):
                if inverse:
                    r0, c0 = (c, r) if code // 4 else (r, c)
                    r0 = 7 - r0 if code % 2 else r0
                    c0 = 7 - c0 if code // 2 % 2 else c0
                else:
                    r0 = 7 - r if code % 2 else r
                    c0 = 7 - c if code // 2 % 2 else c
                    r0, c0 = (c0, r0) if code // 4 else (r0, c0)
                table[code, r0 * 8 + c0, r * 8 + c] = 1
    return table.reshape(512, 64)


def tables():
    tile, lane, cell = np.arange(64), np.arange(STRIP), np.arange(64)
    strip_of = (tile[:, None] // 8 == np.arange(8)[None]).astype(np.float32)
    column_of = (tile[:, None] % 8 == (lane[None] // 8) % 8).astype(np.float32)
    inside = ((lane // 64) * 8 + lane % 8)[:, None] == cell[None]
    inside = inside.astype(np.float32)
    code_of = (np.arange(8)[:, None] == lane[None] // 64).astype(np.float32)
    there, back = orient_table(False), orient_table(True)
    zero = np.zeros_like(there)

    def pair(first, second):
        return np.concatenate(
            [np.concatenate([first, zero], 1), np.concatenate([zero, second], 1)], 0
        )

    zero_cells = np.zeros_like(inside)
    return dict(
        strip_of=strip_of,
        column_of=column_of,
        inside2=np.concatenate([inside, inside], 1),
        code_of=code_of,
        pair_high=pair(there, there),
        pair_low=pair(back, back),
        pair_mixed=pair(there, back),
        spread_first=np.concatenate([inside, zero_cells], 1).T,
        spread_second=np.concatenate([zero_cells, inside], 1).T,
    )


def iota(shape, dim):
    return lax.broadcasted_iota(jnp.int32, shape, dim)


def mm(a, b):
    return lax.dot_general(a, b, (((1,), (0,)), ((), ())), preferred_element_type=F32)


def mm_nt(a, b):
    return lax.dot_general(a, b, (((1,), (1,)), ((), ())), preferred_element_type=F32)


def split(value, parts):
    out = []
    for _ in range(parts - 1):
        head = value.astype(BF16)
        out.append(head)
        value = value - head.astype(F32)
    out.append(value.astype(BF16))
    return out


def place_matrix(partner, blocks, cap):
    onehot = (iota((blocks, TILES), 0) == partner).astype(F32)
    earlier = (iota((TILES, TILES), 0) < iota((TILES, TILES), 1)).astype(BF16)
    rank = jnp.sum(onehot * mm(onehot.astype(BF16), earlier), axis=0, keepdims=True)
    slot = partner * cap + rank.astype(jnp.int32)
    return (iota((TILES, TILES), 0) == slot).astype(BF16)


def to_strips(row):
    return jnp.concatenate([row[:, i * STRIP : (i + 1) * STRIP] for i in range(8)], axis=0)


def from_strips(strips):
    return jnp.concatenate([strips[i : i + 1] for i in range(8)], axis=1)


def take_tiles(faces, place, codes, t):
    rows = mm(place, t["strip_of"][...]).astype(BF16)
    column = mm(place, t["column_of"][...])
    code = (iota((8, TILES), 0) == codes).astype(BF16)
    code = mm(mm_nt(place, code).astype(BF16), t["code_of"][...])
    parts = [part for face in faces for part in split(face, 3)]
    wide = mm(rows, jnp.concatenate(parts, axis=1))
    tall = jnp.concatenate(
        [(wide[:, i * STRIP : (i + 1) * STRIP] * column).astype(BF16) for i in range(len(parts))],
        axis=0,
    )
    cells = mm(tall, t["inside2"][...])
    out = []
    for i in range(len(parts)):
        one = cells[i * TILES : (i + 1) * TILES]
        out.append((jnp.concatenate([one] * 4, axis=1) * code).astype(BF16))
    return [out[3 * i : 3 * i + 3] for i in range(len(faces))]


def pair_tiles(first, second, table):
    total = None
    for part in (2, 1, 0):
        one = mm(jnp.concatenate([first[part], second[part]], axis=1), table)
        total = one if total is None else total + one
    return total


def pack_kernel(
    names,
    blocks,
    tile_cap,
    parcel_cap,
    bottom_ref,
    top_ref,
    flow_ref,
    diff_ref,
    d_ref,
    low_partner,
    high_partner,
    low_orient,
    high_orient,
    table_ref,
    block_ref,
    cell_ref,
    live_ref,
    *rest,
):
    t = dict(zip(names, rest[: len(names)]))
    out_ref, m_ref = rest[len(names) :]
    me = lax.axis_index("blk")
    d0, d1 = d_ref[0], d_ref[1]
    place_high = place_matrix(high_partner[...], blocks, tile_cap)
    place_low = place_matrix(low_partner[...], blocks, tile_cap)
    top0, top1 = to_strips(top_ref[0, 7:8, :]), to_strips(top_ref[1, 7:8, :])
    low0, low1 = to_strips(bottom_ref[0, 0:1, :]), to_strips(bottom_ref[1, 0:1, :])
    vel, dif = to_strips(flow_ref[0, 0:1, :]), to_strips(diff_ref[0, 0:1, :])
    high = take_tiles([top0, top1, d0 * top0 + d1 * top1], place_high, high_orient[...], t)
    low = take_tiles(
        [low0, low1, vel, dif, d0 * low0 + d1 * low1], place_low, low_orient[...], t
    )
    pairs = [
        pair_tiles(high[0], high[1], t["pair_high"][...]),
        pair_tiles(low[0], low[1], t["pair_low"][...]),
        pair_tiles(low[2], low[3], t["pair_low"][...]),
    ]
    m_ref[4 * blocks : 4 * blocks + TILES, :] = pair_tiles(high[2], low[4], t["pair_mixed"][...])
    rows = table_ref.shape[0]
    target = block_ref[...]
    live = live_ref[...] == 1
    onehot = ((iota((blocks, rows), 0) == target) & live).astype(F32)
    earlier = (iota((rows, rows), 0) < iota((rows, rows), 1)).astype(BF16)
    rank = jnp.sum(onehot * mm(onehot.astype(BF16), earlier), axis=0, keepdims=True)
    rank = rank.astype(jnp.int32)
    slot = jnp.where(live, target * parcel_cap + rank, -1)
    send = (iota((blocks * parcel_cap, rows), 0) == slot).astype(BF16)
    table = split(table_ref[...], 3)
    sent = mm(send, table[2]) + mm(send, table[1]) + mm(send, table[0])
    for b in range(blocks):
        out_ref[b, 0:parcel_cap, :] = sent[b * parcel_cap : (b + 1) * parcel_cap]
        for k in range(PAIRS - 1):
            at = parcel_cap + k * tile_cap
            out_ref[b, at : at + tile_cap, :] = pairs[k][b * tile_cap : (b + 1) * tile_cap]
    pick = (iota((8, PV), 1) == iota((8, PV), 0) + 1).astype(BF16)
    columns = mm_nt(pick, table[2]) + mm_nt(pick, table[1]) + mm_nt(pick, table[0])
    p1, p2 = columns[0:1], columns[1:2]
    soft = jnp.maximum(p1, 0.0) + jnp.log1p(jnp.exp(-jnp.abs(p1)))
    sig = 1.0 / (1.0 + jnp.exp(-p2))
    fields = jnp.concatenate(
        [(cell_ref[...] + 1).astype(F32), soft, sig, jnp.zeros((5, rows), F32)], axis=0
    )
    share = 48 // parcel_cap
    lane = rank + lax.rem(me, share) * parcel_cap + 64 * (lax.div(me, share) & 1)
    goal = jnp.where(live, target * LANES + lane, -1)
    spots = (iota((blocks * LANES, rows), 0) == goal).astype(BF16)
    meta = mm_nt(jnp.concatenate(split(fields, 3), axis=0), spots)
    meta = meta[16:24] + meta[8:16] + meta[0:8]
    for b in range(blocks):
        m_ref[4 * b : 4 * b + 4, :] = meta[0:4, b * LANES : (b + 1) * LANES]


def assemble_kernel(blocks, tile_cap, parcel_cap, buf_ref, m0, m1, m2, m3, out_ref):
    ghost = parcel_cap + (PAIRS - 1) * tile_cap
    z = slice(4 * blocks, 4 * blocks + TILES)
    total = (m0[z, :] + m1[z, :]) + (m2[z, :] + m3[z, :])
    near = m0[0 : 4 * blocks, :] + pltpu.roll(m1[0 : 4 * blocks, :], 64, 1)
    far = m2[0 : 4 * blocks, :] + pltpu.roll(m3[0 : 4 * blocks, :], 64, 1)
    for b in range(blocks):
        out_ref[b, 0:ghost, :] = buf_ref[b, 0:ghost, :]
        out_ref[b, ghost : ghost + tile_cap, :] = total[b * tile_cap : (b + 1) * tile_cap]
        at = ghost + tile_cap
        out_ref[b, at : at + 3, :] = near[4 * b : 4 * b + 3]
        out_ref[b, at + 3 : at + 6, :] = far[4 * b : 4 * b + 3]
        if at + 6 < out_ref.shape[1]:
            out_ref[b, at + 6 :, :] = jnp.zeros((out_ref.shape[1] - at - 6, LANES), F32)


def sum_kernel(own_ref, other_ref, d_ref, e_ref, z_ref, zh_ref, fh_ref):
    half = zh_ref.shape[0]
    core = lax.axis_index("sp") & 1
    z_ref[...] = (
        d_ref[0] * own_ref[0]
        + d_ref[1] * own_ref[1]
        + (e_ref[0] * other_ref[0] + e_ref[1] * other_ref[1])
    )

    @pl.when(core == 0)
    def _():
        zh_ref[...] = z_ref[0:half, :]
        fh_ref[...] = own_ref[0, 0:half, :]

    @pl.when(core == 1)
    def _():
        zh_ref[...] = z_ref[half:, :]
        fh_ref[...] = other_ref[0, half:, :]


def flux(velocity, diffusion, d, upper, lower, weight):
    middle = 0.5 * (upper + lower)
    return velocity * middle - diffusion * (d * (upper - lower) - middle * weight)


def inner_kernel(species_ref, flow_ref, diff_ref, vol_ref, zc_ref, za_ref, zb_ref, d_ref, base_ref, z_ref):
    layers = species_ref.shape[1]
    half = layers // 2
    core = lax.axis_index("sp") & 1
    first = core == 0
    z_ref[0:half, :] = zc_ref[0:half, :] + jnp.where(first, za_ref[...], zb_ref[...])
    z_ref[half:, :] = zc_ref[half:, :] + jnp.where(first, zb_ref[...], za_ref[...])
    shape = (layers, LANES)
    row, lane = iota(shape, 0), iota(shape, 1)
    left = lane < 64
    inner = row > 0
    not_last = row < layers - 1
    off_wall = (lane & 63) != 0
    tiles = FACE // LANES

    def step(i, carry):
        j = tiles - 1 - i
        here = pl.ds(pl.multiple_of(j * LANES, LANES), LANES)
        before = pl.ds(pl.multiple_of(jnp.maximum(j - 1, 0) * LANES, LANES), LANES)
        off_floor = (lane >= 64) | (j > 0)
        z, zb = z_ref[:, here], z_ref[:, before]
        w_layer = z - pltpu.roll(z, 1, 0)
        w_row = z - pltpu.roll(jnp.where(left, z, zb), 64, 1)
        w_column = z - pltpu.roll(z, 1, 1)
        vol = section_step * vol_ref[:, here]
        flows = [flow_ref[k, :, here] for k in range(3)]
        diffs = [diff_ref[k, :, here] for k in range(3)]
        out = []
        for s in range(2):
            y, yb, d = species_ref[s, :, here], species_ref[s, :, before], d_ref[s]
            f_layer = flux(flows[0], diffs[0], d, y, pltpu.roll(y, 1, 0), w_layer)
            f_layer = jnp.where(inner, f_layer, 0.0)
            under = pltpu.roll(jnp.where(left, y, yb), 64, 1)
            f_row = jnp.where(off_floor, flux(flows[1], diffs[1], d, y, under, w_row), 0.0)
            f_col = flux(flows[2], diffs[2], d, y, pltpu.roll(y, 1, 1), w_column)
            f_col = jnp.where(off_wall, f_col, 0.0)
            divergence = (
                (pltpu.roll(f_layer, layers - 1, 0) - f_layer)
                + (pltpu.roll(jnp.where(left, carry[s], f_row), 64, 1) - f_row)
                + (pltpu.roll(f_col, LANES - 1, 1) - f_col)
            )
            base_ref[s, :, here] = y - vol * divergence
            out.append(f_row)
        return tuple(out)

    zero = jnp.zeros(shape, F32)
    lax.fori_loop(0, tiles, step, (zero, zero))


def transposed_parts(get, out_ref, at, parts):
    for g in range(FACE // LANES // 4):
        square = jnp.concatenate([get(4 * g + i) for i in range(4)], axis=0).T
        for k, part in enumerate(split(square, parts)):
            out_ref[at + k * LANES : at + (k + 1) * LANES, g * LANES : (g + 1) * LANES] = part


def velocity_kernel(flow_ref, out_ref):
    for f in range(3):
        transposed_parts(
            lambda j: flow_ref[f, :, j * LANES : (j + 1) * LANES], out_ref, 2 * f * LANES, 2
        )


def fuel_kernel(own_ref, other_ref, fa_ref, fb_ref, out_ref, fuel):
    half = fa_ref.shape[0]
    q = lax.axis_index("sp")

    @pl.when(q == 0)
    def _():
        fuel[...] = own_ref[0]

    @pl.when(q == 1)
    def _():
        fuel[...] = other_ref[0]

    @pl.when(q == 2)
    def _():
        fuel[0:half, :] = fa_ref[...]
        fuel[half:, :] = fb_ref[...]

    @pl.when(q == 3)
    def _():
        fuel[0:half, :] = fb_ref[...]
        fuel[half:, :] = fa_ref[...]

    transposed_parts(lambda j: fuel[:, j * LANES : (j + 1) * LANES], out_ref, 0, 2)


def ghost_faces(pairs, place, t):
    column = mm(place, t["column_of"][...])
    strip = mm(place, t["strip_of"][...])
    parts = []
    for pair, name in pairs:
        for part in split(pair, 3):
            parts.append((mm(part, t[name][...]) * column).astype(BF16))
    wide = lax.dot_general(
        strip.astype(BF16),
        jnp.concatenate(parts, axis=1),
        (((0,), (0,)), ((), ())),
        preferred_element_type=F32,
    )
    wide = [wide[:, i * STRIP : (i + 1) * STRIP] for i in range(len(parts))]
    return [wide[3 * i + 2] + wide[3 * i + 1] + wide[3 * i] for i in range(len(pairs))]


def final_kernel(
    names,
    blocks,
    tile_cap,
    parcel_cap,
    got_ref,
    fuel_ref,
    velocity_ref,
    base_ref,
    species_ref,
    vol_ref,
    z_ref,
    flow_ref,
    diff_ref,
    d_ref,
    low_partner,
    high_partner,
    *rest,
):
    t = dict(zip(names, rest[: len(names)]))
    new_ref, arrived_ref, spots, loads, edge = rest[len(names) :]
    layers = species_ref.shape[1]
    cells = layers * FACE // LANES
    share = 48 // parcel_cap
    groups = blocks // share
    ghost = parcel_cap
    at = parcel_cap + PAIRS * tile_cap

    def pair(k):
        lo = ghost + k * tile_cap
        return jnp.concatenate([got_ref[b, lo : lo + tile_cap, :] for b in range(blocks)], axis=0)

    def meta(f):
        rows = []
        for h in range(2):
            for g in range(groups):
                total = None
                for i in range(share):
                    one = got_ref[g * share + i, at + 3 * h + f : at + 3 * h + f + 1, :]
                    total = one if total is None else total + one
                rows.append(total)
        return jnp.concatenate(rows, axis=0)

    chunks = 2 * groups
    number = meta(0).astype(jnp.int32) - 1
    soft, sig = meta(1), meta(2)
    cell_layer = lax.shift_right_arithmetic(number, 12)
    cell_row = (lax.shift_right_arithmetic(number, 7) & 31) * layers + cell_layer
    cell_row = jnp.where(number >= 0, cell_row, -1)
    cell_lane = number & (LANES - 1)
    sublane = iota((LANES, LANES), 0)
    tall = iota((cells, LANES), 0)
    for c in range(chunks):
        spots[:, c * LANES : (c + 1) * LANES] = (tall == cell_row[c : c + 1]).astype(BF16)
    place_low = place_matrix(low_partner[...], blocks, tile_cap)
    place_high = place_matrix(high_partner[...], blocks, tile_cap)
    p0, p1, p2, p3 = (pair(k) for k in range(PAIRS))
    below0, below1, below_z = ghost_faces(
        [(p0, "spread_first"), (p0, "spread_second"), (p3, "spread_first")], place_low, t
    )
    above0, above1, top_v, top_d, above_z = ghost_faces(
        [
            (p1, "spread_first"),
            (p1, "spread_second"),
            (p2, "spread_first"),
            (p2, "spread_second"),
            (p3, "spread_second"),
        ],
        place_high,
        t,
    )
    z_bottom = to_strips(z_ref[0:1, :])
    z_top = to_strips(z_ref[layers - 1 : layers, :])
    bottom_v, bottom_d = to_strips(flow_ref[0, 0:1, :]), to_strips(diff_ref[0, 0:1, :])
    for s, (below, above) in enumerate(((below0, above0), (below1, above1))):
        low = to_strips(species_ref[s, 0:1, :])
        high = to_strips(species_ref[s, layers - 1 : layers, :])
        f_low = flux(bottom_v, bottom_d, d_ref[s], low, below, z_bottom - below_z)
        f_high = flux(top_v, top_d, d_ref[s], above, high, above_z - z_top)
        edge[2 * s : 2 * s + 1, :] = from_strips(f_low)
        edge[2 * s + 1 : 2 * s + 2, :] = from_strips(f_high)
    width = 2 * LANES
    lefts = iota((1, LANES), 1) < 64
    evaporated = []
    for c in range(0, chunks, 2):
        both = mm(fuel_ref[...], spots[:, c * LANES : c * LANES + width])
        both = both[0:LANES] + both[LANES:]
        for i in range(2):
            mask = sublane == cell_lane[c + i : c + i + 1]
            fuel = jnp.sum(
                jnp.where(mask, both[:, i * LANES : (i + 1) * LANES], 0.0), axis=0, keepdims=True
            )
            gone = soft[c + i : c + i + 1] * (sig[c + i : c + i + 1] - fuel)
            evaporated.append(gone)
            for k, part in enumerate(split(jnp.where(mask, gone, 0.0), 2)):
                loads[k * LANES : (k + 1) * LANES, (c + i) * LANES : (c + i + 1) * LANES] = part
    column = iota((8, PV), 1)
    index = iota((8, PV), 0)
    target = ((index == 0) & (column == 0)) | (
        (index >= 1) & (index <= 3) & (column == index + 2)
    )
    target = target.astype(F32)
    drag = (iota((parcel_cap * share, PV), 1) >= 3) & (iota((parcel_cap * share, PV), 1) <= 5)
    keep = jnp.where(drag, 1.0 - friction_timescale, 1.0)
    for h in range(groups // 2):
        a, b = 2 * h, 2 * h + 1
        own = jnp.where(
            iota((cells, LANES), 1) < 64,
            spots[:, a * LANES : (a + 1) * LANES].astype(F32),
            spots[:, b * LANES : (b + 1) * LANES].astype(F32),
        ).astype(BF16)
        mask = sublane == jnp.where(lefts, cell_lane[a : a + 1], cell_lane[b : b + 1])
        u = mm(velocity_ref[...], own)
        rows = [-jnp.where(lefts, evaporated[a], evaporated[b])]
        for f in range(3):
            field = u[2 * f * LANES : (2 * f + 1) * LANES] + u[(2 * f + 1) * LANES : (2 * f + 2) * LANES]
            rows.append(
                friction_timescale * jnp.sum(jnp.where(mask, field, 0.0), axis=0, keepdims=True)
            )
        rows.append(jnp.zeros((4, LANES), F32))
        change = lax.dot_general(
            jnp.concatenate(rows, axis=0),
            target,
            (((0,), (0,)), ((), ())),
            precision=lax.Precision.HIGHEST,
            preferred_element_type=F32,
        )
        for i in range(2):
            g = 2 * h + i
            size = share * parcel_cap
            table = jnp.concatenate(
                [got_ref[g * share + k, 0:parcel_cap, :] for k in range(share)], axis=0
            )
            arrived_ref[g * size : (g + 1) * size, :] = table * keep + change[64 * i : 64 * i + size]
    source = mm_nt(spots[...], loads[...])
    source = source[:, 0:LANES] + source[:, LANES:]
    row = iota((layers, LANES), 0)
    fuel_group = jnp.where(lax.axis_index("sp") == 0, 1.0, 0.0)
    for j in range(FACE // LANES):
        here = slice(j * LANES, (j + 1) * LANES)
        vol = section_step * vol_ref[:, here]
        here_source = source[j * layers : (j + 1) * layers]
        for s in range(2):
            y = species_ref[s, :, here]
            delta = fuel_group if s == 0 else 0.0
            term = here_source * (delta - y)
            term = term + jnp.where(row == 0, edge[2 * s : 2 * s + 1, here], 0.0)
            term = term - jnp.where(row == layers - 1, edge[2 * s + 1 : 2 * s + 2, here], 0.0)
            new_ref[s, :, here] = base_ref[s, :, here] + vol * term


def whole(memory=pltpu.VMEM):
    return pl.BlockSpec(memory_space=memory)


def part(shape, index):
    return pl.BlockSpec(shape, lambda i: index)


def params(semantics=None):
    return pltpu.CompilerParams(vmem_limit_bytes=VMEM_LIMIT)


def body(
    species,
    interface_normal_flow,
    face_diffusion,
    inv_volume,
    diffusivity,
    low_partner,
    high_partner,
    low_orient,
    high_orient,
    droplet_table,
    parcel_block,
    parcel_cell,
    parcel_live,
):
    blocks = lax.axis_size("blk")
    local_species, layers, cells = species.shape
    parcels = droplet_table.shape[0]
    tile_cap = max(1, TILES // blocks)
    parcel_cap = 3 * parcels // (2 * blocks)
    last = layers // 8 - 1
    constants = tables()

    def use(*names):
        return names, [jnp.asarray(constants[n].astype(ml_dtypes.bfloat16)) for n in names]

    def swap(value, bit):
        return lax.ppermute(value, "sp", [(i, i ^ bit) for i in range(lax.axis_size("sp"))])

    other_species = swap(species, 1)
    other_diffusivity = swap(diffusivity, 1)

    names, values = use(
        "strip_of", "column_of", "inside2", "code_of", "pair_high", "pair_low", "pair_mixed"
    )
    rows = -(-(parcel_cap + PAIRS * tile_cap + 6) // 8) * 8
    meta_rows = 4 * blocks + TILES
    face = (1, 8, cells)

    def full(a):
        return pl.BlockSpec(a.shape, lambda i: (0,) * a.ndim)

    small = [low_partner, high_partner, low_orient, high_orient, droplet_table]
    small += [parcel_block.reshape(1, parcels), parcel_cell.reshape(1, parcels)]
    small += [parcel_live.reshape(1, parcels)] + values
    packed, m0 = pl.pallas_call(
        functools.partial(pack_kernel, names, blocks, tile_cap, parcel_cap),
        grid=(1,),
        out_shape=(
            jax.ShapeDtypeStruct((blocks, rows, LANES), F32),
            jax.ShapeDtypeStruct((meta_rows, LANES), F32),
        ),
        in_specs=[
            part((local_species, 8, cells), (0, 0, 0)),
            part((local_species, 8, cells), (0, last, 0)),
            part(face, (0, 0, 0)),
            part(face, (0, 0, 0)),
            whole(pltpu.SMEM),
        ]
        + [full(a) for a in small],
        out_specs=(
            pl.BlockSpec((blocks, rows, LANES), lambda i: (0, 0, 0)),
            pl.BlockSpec((meta_rows, LANES), lambda i: (0, 0)),
        ),
        compiler_params=params(),
        name="pack",
    )(species, species, interface_normal_flow, face_diffusion, diffusivity, *small)
    m1, m2, m3 = swap(m0, 1), swap(m0, 2), swap(m0, 3)

    z_chip, z_half, fuel_half = pl.pallas_call(
        sum_kernel,
        out_shape=(
            jax.ShapeDtypeStruct((layers, cells), F32),
            jax.ShapeDtypeStruct((layers // 2, cells), F32),
            jax.ShapeDtypeStruct((layers // 2, cells), F32),
        ),
        in_specs=[whole(), whole(), whole(pltpu.SMEM), whole(pltpu.SMEM)],
        out_specs=(whole(), whole(), whole()),
        compiler_params=params(),
        name="chip_sum",
    )(species, other_species, diffusivity, other_diffusivity)
    z_far = swap(z_half, 2)
    fuel_far = swap(fuel_half, 2)
    z_far_other = swap(z_far, 1)
    fuel_far_other = swap(fuel_far, 1)

    ready = pl.pallas_call(
        functools.partial(assemble_kernel, blocks, tile_cap, parcel_cap),
        out_shape=jax.ShapeDtypeStruct((blocks, rows, LANES), F32),
        in_specs=[whole()] * 5,
        out_specs=whole(),
        compiler_params=params(),
        name="assemble",
    )(packed, m0, m1, m2, m3)
    got = lax.all_to_all(ready, "blk", split_axis=0, concat_axis=0, tiled=True)

    velocity_parts = pl.pallas_call(
        velocity_kernel,
        out_shape=jax.ShapeDtypeStruct((6 * LANES, layers * cells // LANES), BF16),
        in_specs=[whole()],
        out_specs=whole(),
        compiler_params=params(),
        name="velocity_parts",
    )(interface_normal_flow)

    base, z_total = pl.pallas_call(
        inner_kernel,
        out_shape=(
            jax.ShapeDtypeStruct(species.shape, F32),
            jax.ShapeDtypeStruct((layers, cells), F32),
        ),
        in_specs=[whole()] * 7 + [whole(pltpu.SMEM)],
        out_specs=(whole(), whole()),
        compiler_params=params(),
        name="inner_flux",
    )(species, interface_normal_flow, face_diffusion, inv_volume, z_chip, z_far, z_far_other, diffusivity)

    fuel_parts = pl.pallas_call(
        fuel_kernel,
        out_shape=jax.ShapeDtypeStruct((2 * LANES, layers * cells // LANES), BF16),
        in_specs=[whole()] * 4,
        out_specs=whole(),
        scratch_shapes=[pltpu.VMEM((layers, cells), F32)],
        compiler_params=params(),
        name="fuel_parts",
    )(species, other_species, fuel_far, fuel_far_other)

    names, values = use("strip_of", "column_of", "spread_first", "spread_second")
    groups = blocks * parcel_cap // 48
    small = [low_partner, high_partner] + values
    return pl.pallas_call(
        functools.partial(final_kernel, names, blocks, tile_cap, parcel_cap),
        grid=(1,),
        out_shape=(
            jax.ShapeDtypeStruct(species.shape, F32),
            jax.ShapeDtypeStruct((blocks * parcel_cap, PV), F32),
        ),
        in_specs=[full(got), full(fuel_parts), full(velocity_parts), full(base), full(species)]
        + [full(inv_volume), full(z_total), part(face, (0, 0, 0)), part(face, (0, 0, 0))]
        + [whole(pltpu.SMEM)]
        + [full(a) for a in small],
        out_specs=(
            pl.BlockSpec(species.shape, lambda i: (0, 0, 0)),
            pl.BlockSpec((blocks * parcel_cap, PV), lambda i: (0, 0)),
        ),
        scratch_shapes=[
            pltpu.VMEM((layers * cells // LANES, 2 * groups * LANES), BF16),
            pltpu.VMEM((2 * LANES, 2 * groups * LANES), BF16),
            pltpu.VMEM((8, cells), F32),
        ],
        compiler_params=params(),
        name="final",
    )(
        got,
        fuel_parts,
        velocity_parts,
        base,
        species,
        inv_volume,
        z_total,
        interface_normal_flow,
        face_diffusion,
        diffusivity,
        *small,
    )


def solution(mesh):
    placed = (
        P("sp", "blk", None),
        P(None, "blk", None),
        P(None, "blk", None),
        P("blk", None),
        P("sp"),
        P("blk", None),
        P("blk", None),
        P("blk", None),
        P("blk", None),
        P(("blk", "sp"), None),
        P(("blk", "sp"), None),
        P(("blk", "sp")),
        P(("blk", "sp")),
    )
    return jax.shard_map(
        body,
        mesh=mesh,
        in_specs=placed,
        out_specs=(P("sp", "blk", None), P(("blk", "sp"), None)),
        check_vma=False,
    )
```

time: 253 us -> 68.7 us (0.27); the launches traced: 249 us -> 68.3 us
  local copies, waits for them, and re-layouts: 103 us -> 1.89 us
  other arithmetic: 58.6 us -> 0 us
  Pallas kernels: 0 us -> 37 us
  starting transfers between devices: 27.9 us -> 11.3 us
  waiting for transfers between devices: 32.3 us -> 17.4 us
  between operations: 14.9 us -> 0.68 us
  blocking collectives: 12.3 us -> 0 us
    pallas_call x0 -> x7, Pallas kernels: none -> 37 us  [the longest x1 12.2 us: body(): pl.pallas_call(functools.partial(final_kernel, names, blocks, tile_cap, p...]
    unnamed x83 -> x16, local copies, waits for them, and re-layouts: 37.2 us -> 1.89 us
    psum x2 -> x0, waiting for transfers between devices: 27.1 us -> none  [the longest x1 27.1 us: body(): lax.psum((partial_terms[0], partial_terms[1], partial_terms[2], partial_t...]
    gather x6 -> x0, local copies, waits for them, and re-layouts: 24.4 us -> none  [the longest x1 11.6 us: body(): evaporate_component = fuel_field[landing_grid_points]]
    all_to_all x5 -> x1, starting transfers between devices: 27.9 us -> 5.84 us  [body(): got = lax.all_to_all(ready, 'blk', split_axis=0, concat_axis=0, tiled=True)]
    ppermute x0 -> x9, waiting for transfers between devices: none -> 17.4 us  [swap(): lax.ppermute(value, 'sp', [(i, i ^ bit) for i in range(lax.axis_size('sp'...]
    psum x1 -> x0, blocking collectives: 12.3 us -> none  [body(): lax.psum((partial_terms[0], partial_terms[1], partial_terms[2], partial_t...]
    mul x10 -> x0, other arithmetic: 11.7 us -> none  [the longest x2 5.18 us: face_flux(): diffusion * (scaled * difference - middle * weight)]
  transfers between devices with their start and end apart: 7 -> 10, of which waited for: 2 -> 5; matrix products, arithmetic and copies ran while one was open for 52% -> 0% of each run, Pallas kernels for 0% -> 36%
where the time goes in v1:
time: 68.7 us; the launch traced here: 68.3 us
  Pallas kernels  37 us (54%)
  waiting for transfers between devices  17.4 us (25%)
  starting transfers between devices  11.3 us (16%)
  local copies, waits for them, and re-layouts  1.89 us (3%)
    ppermute x9, waiting for transfers between devices, swap(): lax.ppermute(value, 'sp', [(i, i ^ bit) for i in range(lax.axis_size('sp'...  17.4 us
    pallas_call x1, Pallas kernels, body(): pl.pallas_call(functools.partial(final_kernel, names, blocks, tile_cap, p...  12.2 us
    pallas_call x1, Pallas kernels, body(): pl.pallas_call(inner_kernel, out_shape=(jax.ShapeDtypeStruct(species.shap...  9.66 us
    all_to_all x1, starting transfers between devices, body(): got = lax.all_to_all(ready, 'blk', split_axis=0, concat_axis=0, tiled=True)  5.84 us
    ppermute x9, starting transfers between devices, swap(): lax.ppermute(value, 'sp', [(i, i ^ bit) for i in range(lax.axis_size('sp'...  5.47 us
    pallas_call x1, Pallas kernels, body(): pl.pallas_call(functools.partial(pack_kernel, names, blocks, tile_cap, pa...  4.75 us
    pallas_call x1, Pallas kernels, body(): pl.pallas_call(velocity_kernel, out_shape=jax.ShapeDtypeStruct((6 * LANES...  3.15 us
    pallas_call x1, Pallas kernels, body(): pl.pallas_call(fuel_kernel, out_shape=jax.ShapeDtypeStruct((2 * LANES, la...  2.71 us
  transfers between devices with their start and end apart: 10, of which 5 were waited for; matrix products, arithmetic and copies ran while one was open for 0% of the time, Pallas kernels for 36%

profile of v1, /device:TPU:0, one launch (start us, length us, event | category | flops | bytes accessed | tf_op | source)
XLA Modules:
  0.0 68.3 jit_solution(16881381549588508182)
XLA Ops:
  0.6 0.5 collective-permute-start.3
  1.1 4.8 %pack.1 = (f32[8,88,128]{2,1,0:T(8,128)}, f32[96,128]{1,0:T(8,128)}) custom-call(f32[2,32,4096]{2,1,0:T(8,128)} %species_ref.3, f32[2,32,4096]{2,1,0:T(8,128)} %species_ref.3, f32[3,32,4096]{2,1,0:T(8,128)} %flow_ref.7, f32[3,32,4096]{2,1,0:T(8,128)} %diff_ref.5, f32[2]{0:T(128)} %d_ref.7, s32[1,64]{1,0:T(1,128)} %low_partner.3, s32[1,64]{1,0:T(1,128)} %high_partner.3, ...), custom_call_target="tpu_custom_call" | custom-call | tf_op jit(solution)/shard_map/pack/pallas_call | solution.py:568
  5.9 2.7 %collective-permute-start.2 = (f32[96,128]{1,0:T(8,128)}, f32[96,128]{1,0:T(8,128)S(1)}, u32[]{:S(2)}, u32[]{:S(2)}) collective-permute-start(f32[96,128]{1,0:T(8,128)} %get-tuple-element.10.m0), channel_id=1, source_target_pairs={{0,3},{1,2},{2,1},{3,0},{4,7},{5,6},{6,5},{7,4},{8,11},{9,10},{10,... | collective-permute-start | bytes 147464 | tf_op jit(solution)/shard_map/ppermute | solution.py:550
  8.6 0.0 collective-permute-start.1
  8.6 0.2 collective-permute-start
  8.8 2.1 %collective-permute-done.2.m3 = f32[96,128]{1,0:T(8,128)S(1)} collective-permute-done((f32[96,128]{1,0:T(8,128)}, f32[96,128]{1,0:T(8,128)S(1)}, u32[]{:S(2)}, u32[]{:S(2)}) %collective-permute-start.2) | collective-permute-done | bytes 49184 | tf_op jit(solution)/shard_map/ppermute | solution.py:550
  10.9 2.0 %collective-permute-done.1.m2 = f32[96,128]{1,0:T(8,128)S(1)} collective-permute-done((f32[96,128]{1,0:T(8,128)}, f32[96,128]{1,0:T(8,128)S(1)}, u32[]{:S(2)}, u32[]{:S(2)}) %collective-permute-start.1) | collective-permute-done | bytes 49184 | tf_op jit(solution)/shard_map/ppermute | solution.py:550
  12.9 0.6 copy-done.4
  13.5 0.0 copy-done.5
  13.5 1.9 %assemble.1 = f32[8,88,128]{2,1,0:T(8,128)} custom-call(f32[8,88,128]{2,1,0:T(8,128)} %get-tuple-element.9.buf_ref, f32[96,128]{1,0:T(8,128)} %get-tuple-element.10.m0, f32[96,128]{1,0:T(8,128)} %copy-done.5, f32[96,128]{1,0:T(8,128)} %copy-done.4, f32[96,128]{1,0:T(8,128)} %copy-done.3), custom_call_target="tpu_custom_call" | custom-call | tf_op jit(solution)/shard_map/assemble/pallas_call | solution.py:609
  15.4 5.8 %all-to-all-start = ((f32[8,88,128]{2,1,0:T(8,128)}), f32[8,88,128]{2,1,0:T(8,128)S(1)}, u32[]{:S(2)}, u32[]{:S(2)}) async-start(f32[8,88,128]{2,1,0:T(8,128)} %assemble.1), calls=%async_computation | async-start | bytes 720896 | tf_op jit(solution)/shard_map/all_to_all | solution.py:617
  21.2 0.1 collective-permute-start.4
  21.3 1.1 %collective-permute-done.4.e_ref = f32[2]{0:T(128)S(1)} collective-permute-done((f32[2]{0:T(128)S(1)}, f32[2]{0:T(128)S(1)}, u32[]{:S(2)}, u32[]{:S(2)}) %collective-permute-start.4) | collective-permute-done | bytes 40 | tf_op jit(solution)/shard_map/ppermute | solution.py:550
  22.4 0.5 copy-done.7
  22.9 2.7 %chip_sum.1 = (f32[32,4096]{1,0:T(8,128)}, f32[16,4096]{1,0:T(8,128)}, f32[16,4096]{1,0:T(8,128)}) custom-call(f32[2,32,4096]{2,1,0:T(8,128)} %species_ref.3, f32[2,32,4096]{2,1,0:T(8,128)} %collective-permute-done.3.other_ref, f32[2]{0:T(128)} %d_ref.7, f32[2]{0:T(128)} %copy-done.7), custom_call_target="tpu_custom_call" | custom-call | tf_op jit(solution)/shard_map/chip_sum/pallas_call | solution.py:592
  25.6 0.9 %collective-permute-start.5 = (f32[16,4096]{1,0:T(8,128)}, f32[16,4096]{1,0:T(8,128)S(1)}, u32[]{:S(2)}, u32[]{:S(2)}) collective-permute-start(f32[16,4096]{1,0:T(8,128)} %get-tuple-element.11), channel_id=1, source_target_pairs={{0,2},{1,3},{2,0},{3,1},{4,6},{5,7},{6,4},{7,5},{8,10},{9,11},{10,... | collective-permute-start | bytes 786440 | tf_op jit(solution)/shard_map/ppermute | solution.py:550
  26.5 1.1 %collective-permute-start.7 = (f32[16,4096]{1,0:T(8,128)}, f32[16,4096]{1,0:T(8,128)S(1)}, u32[]{:S(2)}, u32[]{:S(2)}) collective-permute-start(f32[16,4096]{1,0:T(8,128)} %get-tuple-element.13), channel_id=1, source_target_pairs={{0,2},{1,3},{2,0},{3,1},{4,6},{5,7},{6,4},{7,5},{8,10},{9,11},{10,... | collective-permute-start | bytes 786440 | tf_op jit(solution)/shard_map/ppermute | solution.py:550
  27.6 7.3 %collective-permute-done.5.fa_ref = f32[16,4096]{1,0:T(8,128)S(1)} collective-permute-done((f32[16,4096]{1,0:T(8,128)}, f32[16,4096]{1,0:T(8,128)S(1)}, u32[]{:S(2)}, u32[]{:S(2)}) %collective-permute-start.5) | collective-permute-done | bytes 262176 | tf_op jit(solution)/shard_map/ppermute | solution.py:550
  34.9 4.9 %collective-permute-done.7.za_ref = f32[16,4096]{1,0:T(8,128)S(1)} collective-permute-done((f32[16,4096]{1,0:T(8,128)}, f32[16,4096]{1,0:T(8,128)S(1)}, u32[]{:S(2)}, u32[]{:S(2)}) %collective-permute-start.7) | collective-permute-done | bytes 262176 | tf_op jit(solution)/shard_map/ppermute | solution.py:550
  39.8 3.1 %velocity_parts.1.velocity_ref = bf16[768,1024]{1,0:T(8,128)(2,1)} custom-call(f32[3,32,4096]{2,1,0:T(8,128)} %flow_ref.7), custom_call_target="tpu_custom_call" | custom-call | tf_op jit(solution)/shard_map/velocity_parts/pallas_call | solution.py:619
  43.0 2.7 %fuel_parts.1.fuel_ref = bf16[256,1024]{1,0:T(8,128)(2,1)} custom-call(f32[2,32,4096]{2,1,0:T(8,128)} %species_ref.3, f32[2,32,4096]{2,1,0:T(8,128)} %collective-permute-done.3.other_ref, f32[16,4096]{1,0:T(8,128)} %copy-done.2, f32[16,4096]{1,0:T(8,128)} %collective-permute-done.6.fb_ref), custom_call_target="tpu_custom_call" | custom-call | tf_op jit(solution)/shard_map/fuel_parts/pallas_call | solution.py:640
  45.7 9.7 %inner_flux.1 = (f32[2,32,4096]{2,1,0:T(8,128)}, f32[32,4096]{1,0:T(8,128)}) custom-call(f32[2,32,4096]{2,1,0:T(8,128)} %species_ref.3, f32[3,32,4096]{2,1,0:T(8,128)} %flow_ref.7, f32[3,32,4096]{2,1,0:T(8,128)} %diff_ref.5, f32[32,4096]{1,0:T(8,128)} %vol_ref.3, f32[32,4096]{1,0:T(8,128)} %get-tuple-element.12.zc_ref, f32[16,4096]{1,0:T(8,128)} %copy-done.1, ...), custom_call_target="tpu_custom_call" | custom-call | tf_op jit(solution)/shard_map/inner_flux/pallas_call | solution.py:628
  55.4 0.7 %copy-done = f32[8,88,128]{2,1,0:T(8,128)} copy-done((f32[8,88,128]{2,1,0:T(8,128)}, f32[8,88,128]{2,1,0:T(8,128)S(1)}, u32[]{:S(2)}) %copy-start) | copy-done | bytes 360472
  56.1 12.2 %final.1 = (f32[2,32,4096]{2,1,0:T(8,128)}, f32[384,128]{1,0:T(8,128)}) custom-call(f32[8,88,128]{2,1,0:T(8,128)} %copy-done, bf16[256,1024]{1,0:T(8,128)(2,1)} %fuel_parts.1.fuel_ref, bf16[768,1024]{1,0:T(8,128)(2,1)} %velocity_parts.1.velocity_ref, f32[2,32,4096]{2,1,0:T(8,128)} %get-tuple-element.14.base_ref, f32[2,32,4096]{2,1,0:T(8,128)} %species_ref.3, ...), custom_call_target="tpu_custom_call" | custom-call | tf_op jit(solution)/shard_map/final/pallas_call | solution.py:653
  (19 shorter events, 0.0 us)
Async XLA Ops:
  0.6 21.8 %collective-permute-start.3 = (f32[2,32,4096]{2,1,0:T(8,128)}, f32[2,32,4096]{2,1,0:T(8,128)}, u32[]{:S(2)}, u32[]{:S(2)}) collective-permute-start(f32[2,32,4096]{2,1,0:T(8,128)} %species_ref.3), channel_id=1, source_target_pairs={{0,1},{1,0},{2,3},{3,2},{4,5},{5,4},{6,7},{7,6},{8,9},{9,8},{10,11... | collective-permute-start | bytes 3145736 | tf_op jit(solution)/shard_map/ppermute | solution.py:550
  5.9 15.3 %copy-start.6 = (f32[2]{0:T(128)S(1)}, f32[2]{0:T(128)}, u32[]{:S(2)}) copy-start(f32[2]{0:T(128)} %d_ref.7) | copy-start | bytes 28
  5.9 5.0 %collective-permute-start.2 = (f32[96,128]{1,0:T(8,128)}, f32[96,128]{1,0:T(8,128)S(1)}, u32[]{:S(2)}, u32[]{:S(2)}) collective-permute-start(f32[96,128]{1,0:T(8,128)} %get-tuple-element.10.m0), channel_id=1, source_target_pairs={{0,3},{1,2},{2,1},{3,0},{4,7},{5,6},{6,5},{7,4},{8,11},{9,10},{10,... | collective-permute-start | bytes 147464 | tf_op jit(solution)/shard_map/ppermute | solution.py:550
  8.6 4.3 %collective-permute-start.1 = (f32[96,128]{1,0:T(8,128)}, f32[96,128]{1,0:T(8,128)S(1)}, u32[]{:S(2)}, u32[]{:S(2)}) collective-permute-start(f32[96,128]{1,0:T(8,128)} %get-tuple-element.10.m0), channel_id=1, source_target_pairs={{0,2},{1,3},{2,0},{3,1},{4,6},{5,7},{6,4},{7,5},{8,10},{9,11},{10,... | collective-permute-start | bytes 147464 | tf_op jit(solution)/shard_map/ppermute | solution.py:550
  8.6 4.3 %collective-permute-start = (f32[96,128]{1,0:T(8,128)}, f32[96,128]{1,0:T(8,128)S(1)}, u32[]{:S(2)}, u32[]{:S(2)}) collective-permute-start(f32[96,128]{1,0:T(8,128)} %get-tuple-element.10.m0), channel_id=1, source_target_pairs={{0,1},{1,0},{2,3},{3,2},{4,5},{5,4},{6,7},{7,6},{8,9},{9,8},{10,11... | collective-permute-start | bytes 147464 | tf_op jit(solution)/shard_map/ppermute | solution.py:550
  10.9 2.0 %copy-start.3 = (f32[96,128]{1,0:T(8,128)}, f32[96,128]{1,0:T(8,128)S(1)}, u32[]{:S(2)}) copy-start(f32[96,128]{1,0:T(8,128)S(1)} %collective-permute-done.2.m3) | copy-start | bytes 147460
  12.9 0.6 copy-start.4
  12.9 0.6 copy-start.5
  15.4 40.0 %all-to-all-start = ((f32[8,88,128]{2,1,0:T(8,128)}), f32[8,88,128]{2,1,0:T(8,128)S(1)}, u32[]{:S(2)}, u32[]{:S(2)}) async-start(f32[8,88,128]{2,1,0:T(8,128)} %assemble.1), calls=%async_computation | async-start | bytes 720896 | tf_op jit(solution)/shard_map/all_to_all | solution.py:617
  21.2 1.2 %collective-permute-start.4 = (f32[2]{0:T(128)S(1)}, f32[2]{0:T(128)S(1)}, u32[]{:S(2)}, u32[]{:S(2)}) collective-permute-start(f32[2]{0:T(128)S(1)} %copy-done.6), channel_id=1, source_target_pairs={{0,1},{1,0},{2,3},{3,2},{4,5},{5,4},{6,7},{7,6},{8,9},{9,8},{10,11... | collective-permute-start | bytes 32 | tf_op jit(solution)/shard_map/ppermute | solution.py:550
  22.4 0.5 copy-start.7
  25.6 9.4 %collective-permute-start.5 = (f32[16,4096]{1,0:T(8,128)}, f32[16,4096]{1,0:T(8,128)S(1)}, u32[]{:S(2)}, u32[]{:S(2)}) collective-permute-start(f32[16,4096]{1,0:T(8,128)} %get-tuple-element.11), channel_id=1, source_target_pairs={{0,2},{1,3},{2,0},{3,1},{4,6},{5,7},{6,4},{7,5},{8,10},{9,11},{10,... | collective-permute-start | bytes 786440 | tf_op jit(solution)/shard_map/ppermute | solution.py:550
  26.5 13.3 %collective-permute-start.7 = (f32[16,4096]{1,0:T(8,128)}, f32[16,4096]{1,0:T(8,128)S(1)}, u32[]{:S(2)}, u32[]{:S(2)}) collective-permute-start(f32[16,4096]{1,0:T(8,128)} %get-tuple-element.13), channel_id=1, source_target_pairs={{0,2},{1,3},{2,0},{3,1},{4,6},{5,7},{6,4},{7,5},{8,10},{9,11},{10,... | collective-permute-start | bytes 786440 | tf_op jit(solution)/shard_map/ppermute | solution.py:550
  34.9 8.0 %copy-start.2 = (f32[16,4096]{1,0:T(8,128)}, f32[16,4096]{1,0:T(8,128)S(1)}, u32[]{:S(2)}) copy-start(f32[16,4096]{1,0:T(8,128)S(1)} %collective-permute-done.5.fa_ref) | copy-start | bytes 786436
  34.9 8.0 %collective-permute-start.6 = (f32[16,4096]{1,0:T(8,128)S(1)}, f32[16,4096]{1,0:T(8,128)}, u32[]{:S(2)}, u32[]{:S(2)}) collective-permute-start(f32[16,4096]{1,0:T(8,128)S(1)} %collective-permute-done.5.fa_ref), channel_id=1, source_target_pairs={{0,1},{1,0},{2,3},{3,2},{4,5},{5,4},{6,7},{7,6},{8,9},{9,8},{10,11... | collective-permute-start | bytes 786440 | tf_op jit(solution)/shard_map/ppermute | solution.py:550
  39.8 3.2 %copy-start.1 = (f32[16,4096]{1,0:T(8,128)}, f32[16,4096]{1,0:T(8,128)S(1)}, u32[]{:S(2)}) copy-start(f32[16,4096]{1,0:T(8,128)S(1)} %collective-permute-done.7.za_ref) | copy-start | bytes 786436
  39.8 5.9 %collective-permute-start.8 = (f32[16,4096]{1,0:T(8,128)S(1)}, f32[16,4096]{1,0:T(8,128)}, u32[]{:S(2)}, u32[]{:S(2)}) collective-permute-start(f32[16,4096]{1,0:T(8,128)S(1)} %collective-permute-done.7.za_ref), channel_id=1, source_target_pairs={{0,1},{1,0},{2,3},{3,2},{4,5},{5,4},{6,7},{7,6},{8,9},{9,8},{10,11... | collective-permute-start | bytes 786440 | tf_op jit(solution)/shard_map/ppermute | solution.py:550
  55.4 0.7 %copy-start = (f32[8,88,128]{2,1,0:T(8,128)}, f32[8,88,128]{2,1,0:T(8,128)S(1)}, u32[]{:S(2)}) copy-start(f32[8,88,128]{2,1,0:T(8,128)S(1)} %all-to-all-done.got_ref) | copy-start | bytes 1081348

commit v2 on v0

v2 whole, which is shorter than its diff:
```python
import functools

import jax
import jax.numpy as jnp
from jax import lax
from jax.experimental import pallas as pl
from jax.experimental.pallas import tpu as pltpu
from jax.sharding import PartitionSpec as P

PV = 128
BJ = 64
BK = 64
TILE_SIDE = 8
TILES = 64
LANES = 128
FACE = BJ * BK
STRIP = TILE_SIDE * BK
PAIRS = 4

section_step = 0.5
friction_timescale = 0.3

F32 = jnp.float32
BF16 = jnp.bfloat16
VMEM_LIMIT = 16 * 1024 * 1024


def iota(shape, dim):
    return lax.broadcasted_iota(jnp.int32, shape, dim)


def mm(a, b):
    return lax.dot_general(a, b, (((1,), (0,)), ((), ())), preferred_element_type=F32)


def mm_nt(a, b):
    return lax.dot_general(a, b, (((1,), (1,)), ((), ())), preferred_element_type=F32)


def mm_tn(a, b):
    return lax.dot_general(a, b, (((0,), (0,)), ((), ())), preferred_element_type=F32)


def ones(condition, kind=BF16):
    return jnp.where(condition, 1.0, 0.0).astype(kind)


def split(value, parts):
    out = []
    for _ in range(parts - 1):
        head = value.astype(BF16)
        out.append(head)
        value = value - head.astype(F32)
    out.append(value.astype(BF16))
    return out


def inside_table():
    lane, cell = iota((STRIP, LANES), 0), iota((STRIP, LANES), 1) & 63
    return ones(((lane >> 6) == (cell >> 3)) & ((lane & 7) == (cell & 7)))


def orient_table():
    shape = (8 * TILES, LANES)
    code, source = iota(shape, 0) >> 6, iota(shape, 0) & 63
    column = iota(shape, 1)
    r, c = (column >> 3) & 7, column & 7
    back = column >= 64
    turned = code >= 4
    flip_r, flip_c = (code & 1) * 7, ((code >> 1) & 1) * 7
    there = jnp.where(turned, (c ^ flip_c) * 8 + (r ^ flip_r), (r ^ flip_r) * 8 + (c ^ flip_c))
    r0, c0 = jnp.where(turned, c, r), jnp.where(turned, r, c)
    return ones(source == jnp.where(back, (r0 ^ flip_r) * 8 + (c0 ^ flip_c), there))


def place_matrix(partner, blocks, cap):
    onehot = ones(iota((blocks, TILES), 0) == partner, F32)
    earlier = ones(iota((TILES, TILES), 0) < iota((TILES, TILES), 1))
    rank = jnp.sum(onehot * mm(onehot.astype(BF16), earlier), axis=0, keepdims=True)
    slot = partner * cap + rank.astype(jnp.int32)
    return ones(iota((TILES, TILES), 0) == slot)


def to_strips(row):
    return jnp.concatenate([row[:, i * STRIP : (i + 1) * STRIP] for i in range(8)], axis=0)


def from_strips(strips):
    return jnp.concatenate([strips[i : i + 1] for i in range(8)], axis=1)


def take_tiles(faces, strip, column, code, inside):
    parts = [part for face in faces for part in split(face, 3)]
    wide = mm(strip, jnp.concatenate(parts, axis=1))
    tall = jnp.concatenate(
        [(wide[:, i * STRIP : (i + 1) * STRIP] * column).astype(BF16) for i in range(len(parts))],
        axis=0,
    )
    cells = mm(tall, inside)
    out = []
    for i in range(len(parts)):
        one = cells[i * TILES : (i + 1) * TILES]
        out.append((jnp.concatenate([one] * 4, axis=1) * code).astype(BF16))
    return out


def turn_tiles(tiles, table):
    turned = mm(jnp.concatenate(tiles, axis=0), table)
    turned = [turned[i * TILES : (i + 1) * TILES] for i in range(len(tiles))]
    return [turned[i + 2] + turned[i + 1] + turned[i] for i in range(0, len(tiles), 3)]


def begin(copies, sems):
    started = [pltpu.make_async_copy(a, b, sems.at[i]) for i, (a, b) in enumerate(copies)]
    for one in started:
        one.start()
    return started


def pack_rows_kernel(
    blocks,
    tile_cap,
    parcel_cap,
    species,
    flow,
    diff,
    low_partner,
    high_partner,
    low_orient,
    high_orient,
    table,
    block,
    live,
    out_ref,
    strips_ref,
    edge_ref,
    strip_ref,
    column_ref,
    code_ref,
    rank_ref,
    bottom,
    top,
    vel_in,
    dif_in,
    small,
    table_in,
    parcel,
    sems,
):
    layers = species.shape[1]
    copies = begin(
        [(high_partner, small.at[0]), (low_partner, small.at[1])]
        + [(high_orient, small.at[2]), (low_orient, small.at[3])]
        + [(block, parcel.at[0]), (live, parcel.at[1]), (table, table_in)]
        + [(species.at[:, layers - 8 :], top), (species.at[:, 0:8], bottom)]
        + [(flow.at[0, 0:8], vel_in), (diff.at[0, 0:8], dif_in)],
        sems,
    )
    inside, turn = inside_table(), orient_table()
    tile = iota((TILES, STRIP), 0)
    strip_of = ones((iota((TILES, LANES), 0) >> 3) == iota((TILES, LANES), 1))
    column_of = ones((tile & 7) == ((iota((TILES, STRIP), 1) >> 3) & 7))
    code_of = ones(iota((8, STRIP), 0) == (iota((8, STRIP), 1) >> 6))
    rows = table.shape[0]
    earlier = ones(iota((rows, rows), 0) < iota((rows, rows), 1))
    for copy in copies[0:4]:
        copy.wait()
    for k in range(2):
        place = place_matrix(small[k], blocks, tile_cap)
        strip_ref[k] = mm(place, strip_of)
        column_ref[k] = mm(place, column_of)
        code = ones(iota((8, TILES), 0) == small[2 + k])
        code_ref[k] = mm(mm_nt(place, code).astype(BF16), code_of)
    for copy in copies[4:7]:
        copy.wait()
    target = parcel[0]
    alive = parcel[1] == 1
    onehot = ones((iota((blocks, rows), 0) == target) & alive, F32)
    rank = jnp.sum(onehot * mm(onehot.astype(BF16), earlier), axis=0, keepdims=True)
    rank = rank.astype(jnp.int32)
    rank_ref[...] = jnp.broadcast_to(jnp.where(alive, rank, -1), (8, rows))
    slot = jnp.where(alive, target * parcel_cap + rank, -1)
    send = ones(iota((blocks * parcel_cap, rows), 0) == slot)
    parts = split(table_in[...], 3)
    sent = mm(send, parts[2]) + mm(send, parts[1]) + mm(send, parts[0])
    for copy in copies[7:]:
        copy.wait()
    top0, top1 = to_strips(top[0, 7:8, :]), to_strips(top[1, 7:8, :])
    low0, low1 = to_strips(bottom[0, 0:1, :]), to_strips(bottom[1, 0:1, :])
    strips_ref[...] = jnp.concatenate([top0, top1, low0, low1], axis=0)
    vel, dif = to_strips(vel_in[0:1, :]), to_strips(dif_in[0:1, :])
    edge_ref[...] = jnp.concatenate([vel, dif], axis=0)
    tiles = []
    for k, some in enumerate(([top0, top1], [low0, low1, vel, dif])):
        strip = strip_ref[k][:, 0:8].astype(BF16)
        tiles += take_tiles(some, strip, column_ref[k], code_ref[k], inside)
    high0, high1, low0, low1, vel, dif = turn_tiles(tiles, turn)
    left = iota((TILES, LANES), 1) < 64
    pairs = [
        jnp.where(left, high0, pltpu.roll(high1, 64, 1)),
        jnp.where(left, pltpu.roll(low0, 64, 1), low1),
        jnp.where(left, pltpu.roll(vel, 64, 1), dif),
    ]
    for b in range(blocks):
        out_ref[b, 0:parcel_cap, :] = sent[b * parcel_cap : (b + 1) * parcel_cap]
        for k in range(PAIRS - 1):
            at = parcel_cap + k * tile_cap
            out_ref[b, at : at + tile_cap, :] = pairs[k][b * tile_cap : (b + 1) * tile_cap]


def pack_meta_kernel(
    blocks,
    parcel_cap,
    factors,
    table,
    block,
    cell,
    strips_ref,
    strip_ref,
    column_ref,
    code_ref,
    rank_ref,
    z_half,
    m_ref,
    d_own,
    table_in,
    parcel,
    sems,
):
    copies = begin(
        [(table, table_in), (block, parcel.at[0]), (cell, parcel.at[1]), (factors, d_own)], sems
    )
    rows = table.shape[0]
    me = lax.axis_index("blk")
    inside, turn = inside_table(), orient_table()
    pick = ones(iota((8, PV), 1) == iota((8, PV), 0) + 1)
    for copy in copies:
        copy.wait()
    d0, d1 = d_own[0:1, 0:1], d_own[0:1, 1:2]
    tiles = []
    for k in range(2):
        strip = strip_ref[k][:, 0:8].astype(BF16)
        face = d0 * strips_ref[16 * k : 16 * k + 8, :] + d1 * strips_ref[16 * k + 8 : 16 * k + 16, :]
        tiles += take_tiles([face], strip, column_ref[k], code_ref[k], inside)
    high, low = turn_tiles(tiles, turn)
    lanes = iota((1, LANES), 1)
    m_ref[4 * blocks : 4 * blocks + TILES, :] = jnp.where(lanes < 64, high, low)
    parts = split(table_in[...], 3)
    columns = mm_nt(pick, parts[2]) + mm_nt(pick, parts[1]) + mm_nt(pick, parts[0])
    p1, p2 = columns[0:1], columns[1:2]
    soft = jnp.maximum(p1, 0.0) + jnp.log1p(jnp.exp(-jnp.abs(p1)))
    sig = 1.0 / (1.0 + jnp.exp(-p2))
    fields = jnp.concatenate(
        [(parcel[1] + 1).astype(F32), soft, sig, jnp.zeros((5, rows), F32)], axis=0
    )
    rank = rank_ref[0:1, :]
    share = 48 // parcel_cap
    lane = rank + lax.rem(me, share) * parcel_cap + 64 * (lax.div(me, share) & 1)
    goal = jnp.where(rank >= 0, parcel[0] * LANES + lane, -1)
    spots = ones(iota((blocks * LANES, rows), 0) == goal)
    meta = mm_nt(jnp.concatenate(split(fields, 3), axis=0), spots)
    meta = meta[16:24] + meta[8:16] + meta[0:8]
    own = jnp.where(lanes == 0, d0, jnp.where(lanes == 1, d1, 0.0))
    for b in range(blocks):
        m_ref[4 * b : 4 * b + 3, :] = meta[0:3, b * LANES : (b + 1) * LANES]
        m_ref[4 * b + 3 : 4 * b + 4, :] = own


def assemble_kernel(
    blocks, tile_cap, parcel_cap, buf_ref, m0, m1, m2, m3, z_near, z_far, out_ref, z_ref
):
    z_ref[...] = z_near[...] + z_far[...]
    ghost = parcel_cap + (PAIRS - 1) * tile_cap
    z = slice(4 * blocks, 4 * blocks + TILES)
    total = (m0[z, :] + m1[z, :]) + (m2[z, :] + m3[z, :])
    near = m0[0 : 4 * blocks, :] + pltpu.roll(m1[0 : 4 * blocks, :], 64, 1)
    far = m2[0 : 4 * blocks, :] + pltpu.roll(m3[0 : 4 * blocks, :], 64, 1)
    for b in range(blocks):
        out_ref[b, 0:ghost, :] = buf_ref[b, 0:ghost, :]
        out_ref[b, ghost : ghost + tile_cap, :] = total[b * tile_cap : (b + 1) * tile_cap]
        at = ghost + tile_cap
        out_ref[b, at : at + 3, :] = near[4 * b : 4 * b + 3]
        out_ref[b, at + 3 : at + 6, :] = far[4 * b : 4 * b + 3]
        if at + 6 < out_ref.shape[1]:
            out_ref[b, at + 6 :, :] = jnp.zeros((out_ref.shape[1] - at - 6, LANES), F32)


def sum_kernel(
    species, other_ref, factors, d_other, strip, zh_ref, fh_ref, own_ref, d_own, sems
):
    half, cells = zh_ref.shape
    quarter = cells // 4
    parts = [slice(i * quarter, (i + 1) * quarter) for i in range(4)]
    copies = begin(
        [(factors, d_own)] + [(species.at[:, :, p], own_ref.at[:, :, p]) for p in parts], sems
    )
    first = (lax.axis_index("sp") & 1) == 0
    copies[0].wait()
    d0, d1, e0, e1 = d_own[0:1, 0:1], d_own[0:1, 1:2], d_other[0:1, 0:1], d_other[0:1, 1:2]
    for copy, p in zip(copies[1:], parts):
        copy.wait()
        for lo in range(p.start, p.stop, LANES):
            at = slice(lo, lo + LANES)
            own, other = own_ref[0, :, at], other_ref[0, :, at]
            z = d0 * own + d1 * own_ref[1, :, at] + (e0 * other + e1 * other_ref[1, :, at])
            zh_ref[:, at] = jnp.where(first, z[0:half], z[half:])
            fh_ref[:, at] = jnp.where(first, own[0:half], other[half:])


def flux(velocity, diffusion, d, upper, lower, weight):
    middle = 0.5 * (upper + lower)
    return velocity * middle - diffusion * (d * (upper - lower) - middle * weight)


def transposed_parts(get, out_ref, at, parts, group):
    square = jnp.concatenate([get(4 * group + i) for i in range(4)], axis=0).T
    for k, part in enumerate(split(square, parts)):
        out_ref[at + k * LANES : at + (k + 1) * LANES, group * LANES : (group + 1) * LANES] = part


def inner_kernel(
    flow,
    diff,
    vol,
    species,
    za_ref,
    zb_ref,
    m0,
    base_ref,
    edge_ref,
    flow_ref,
    diff_ref,
    vol_ref,
    species_ref,
    z_ref,
    sems,
):
    layers, cells = vol.shape
    half = layers // 2
    quarter = cells // 4
    parts = [slice(i * quarter, (i + 1) * quarter) for i in range(4)]
    copies = {}
    for n, i in enumerate((3, 2, 1, 0)):
        p = parts[i]
        copies[i] = begin(
            [
                (flow.at[:, :, p], flow_ref.at[:, :, p]),
                (diff.at[:, :, p], diff_ref.at[:, :, p]),
                (vol.at[:, p], vol_ref.at[:, p]),
                (species.at[:, :, p], species_ref.at[:, :, p]),
            ],
            sems.at[n],
        )
    first = (lax.axis_index("sp") & 1) == 0
    z_ref[0:half, :] = jnp.where(first, za_ref[...], zb_ref[...])
    z_ref[half:, :] = jnp.where(first, zb_ref[...], za_ref[...])
    shape = (layers, LANES)
    row, lane = iota(shape, 0), iota(shape, 1)
    left = lane < 64
    inner = row > 0
    off_wall = (lane & 63) != 0
    ds = (m0[3:4, 0:1], m0[3:4, 1:2])
    above = [jnp.zeros(shape, F32)] * 2
    for j in range(cells // LANES - 1, -1, -1):
        here = slice(j * LANES, (j + 1) * LANES)
        before = slice(max(j - 1, 0) * LANES, (max(j - 1, 0) + 1) * LANES)
        if here.stop % quarter == 0:
            for copy in copies[here.start // quarter][0:3]:
                copy.wait()
            if j == cells // LANES - 1:
                copies[here.start // quarter][3].wait()
        if here.start % quarter == 0 and j > 0:
            copies[before.start // quarter][3].wait()
        z = z_ref[:, here]
        unders = (
            lambda y: pltpu.roll(y, 1, 0),
            lambda y: pltpu.roll(y, 64, 1),
            lambda y: pltpu.roll(y, 1, 1),
        )
        z_under = (
            pltpu.roll(z, 1, 0),
            pltpu.roll(jnp.where(left, z, z_ref[:, before]), 64, 1),
            pltpu.roll(z, 1, 1),
        )
        masks = (inner, (lane >= 64) if j == 0 else None, off_wall)
        means, slopes = [], []
        for k in range(3):
            g = diff_ref[k, :, here]
            c = 0.5 * (flow_ref[k, :, here] + g * (z - z_under[k]))
            if masks[k] is not None:
                c, g = jnp.where(masks[k], c, 0.0), jnp.where(masks[k], g, 0.0)
            means.append(c)
            slopes.append(g)
        scale = section_step * vol_ref[:, here]
        for s in range(2):
            y = species_ref[s, :, here]
            under = (
                pltpu.roll(y, 1, 0),
                pltpu.roll(jnp.where(left, y, species_ref[s, :, before]), 64, 1),
                pltpu.roll(y, 1, 1),
            )
            f_layer, f_row, f_column = (
                (y + u) * c - (y - u) * (g * ds[s]) for u, c, g in zip(under, means, slopes)
            )
            divergence = (
                (pltpu.roll(f_layer, layers - 1, 0) - f_layer)
                + (pltpu.roll(jnp.where(left, above[s], f_row), 64, 1) - f_row)
                + (pltpu.roll(f_column, LANES - 1, 1) - f_column)
            )
            base_ref[s, :, here] = y - scale * divergence
            above[s] = f_row
    ends = [ref[i : i + 1, :] for ref in (z_ref, vol_ref) for i in (0, layers - 1)]
    edge_ref[...] = jnp.concatenate([to_strips(end) for end in ends], axis=0)


def fuel_half_kernel(near_ref, far_ref, edge_ref, out_ref):
    out_ref[...] = jnp.where(lax.axis_index("sp") < 2, near_ref[...], far_ref[...])


def fuel_kernel(own_ref, other_ref, out_ref):
    first = (lax.axis_index("sp") & 1) == 0

    def field(j):
        here = slice(j * LANES, (j + 1) * LANES)
        a, b = own_ref[:, here], other_ref[:, here]
        return jnp.concatenate([jnp.where(first, a, b), jnp.where(first, b, a)], axis=0)

    for group in range(FACE // LANES // 4):
        transposed_parts(field, out_ref, 0, 2, group)


def ghost_faces(pairs, strip, column, inside):
    lane = iota((TILES, LANES), 1)
    parts = []
    for pair, right in pairs:
        one = jnp.where((lane >= 64) if right else (lane < 64), pair, 0.0)
        parts += split(one, 3)
    wide = mm_nt(jnp.concatenate(parts, axis=0), inside)
    wide = [
        (wide[i * TILES : (i + 1) * TILES] * column).astype(BF16) for i in range(len(parts))
    ]
    wide = mm_tn(strip, jnp.concatenate(wide, axis=1))
    wide = [wide[:, i * STRIP : (i + 1) * STRIP] for i in range(len(parts))]
    return [wide[3 * i + 2] + wide[3 * i + 1] + wide[3 * i] for i in range(len(pairs))]


def final_kernel(
    blocks,
    tile_cap,
    parcel_cap,
    got_ref,
    fuel_ref,
    base_ref,
    species,
    vol,
    flow,
    zedge_ref,
    fedge_ref,
    strips_ref,
    strip_ref,
    column_ref,
    m0,
    new_hbm,
    arrived_hbm,
    new_ref,
    arrived_ref,
    spots,
    loads,
    edge,
    species_ref,
    vol_ref,
    flow_ref,
    number_ref,
    number_smem,
    rows_ref,
    sems,
    flow_sem,
    number_sem,
):
    layers, cells = base_ref.shape[1:]
    fetch = begin([(species, species_ref), (vol, vol_ref)], sems.at[1])
    fetch_flow = begin(
        [
            (flow.at[:, :, j * LANES : (j + 1) * LANES], flow_ref.at[:, j * layers : (j + 1) * layers])
            for j in range(cells // LANES)
        ],
        flow_sem,
    )
    tall_rows = layers * cells // LANES
    share = 48 // parcel_cap
    groups = blocks // share
    ghost = parcel_cap
    at = parcel_cap + PAIRS * tile_cap

    def pair(k):
        lo = ghost + k * tile_cap
        return jnp.concatenate([got_ref[b, lo : lo + tile_cap, :] for b in range(blocks)], axis=0)

    def meta(f):
        rows = []
        for h in range(2):
            for g in range(groups):
                total = None
                for i in range(share):
                    one = got_ref[g * share + i, at + 3 * h + f : at + 3 * h + f + 1, :]
                    total = one if total is None else total + one
                rows.append(total)
        return jnp.concatenate(rows, axis=0)

    chunks = 2 * groups
    number = meta(0).astype(jnp.int32) - 1
    soft, sig = meta(1), meta(2)
    cell_layer = lax.shift_right_arithmetic(number, 12)
    cell_row = (lax.shift_right_arithmetic(number, 7) & 31) * layers + cell_layer
    cell_row = jnp.where(number >= 0, cell_row, -1)
    number_ref[...] = jnp.maximum(cell_row, 0)
    fetch_number = pltpu.make_async_copy(number_ref, number_smem, number_sem)
    fetch_number.start()
    cell_lane = number & (LANES - 1)
    sublane = iota((LANES, LANES), 0)
    tall = iota((tall_rows, LANES), 0)
    for c in range(chunks):
        spots[:, c * LANES : (c + 1) * LANES] = ones(tall == cell_row[c : c + 1])
    inside = inside_table()
    p0, p1, p2, p3 = (pair(k) for k in range(PAIRS))
    below0, below1, below_z = ghost_faces(
        [(p0, 0), (p0, 1), (p3, 0)], strip_ref[1].astype(BF16)[:, 0:8], column_ref[1], inside
    )
    above0, above1, top_v, top_d, above_z = ghost_faces(
        [(p1, 0), (p1, 1), (p2, 0), (p2, 1), (p3, 1)],
        strip_ref[0].astype(BF16)[:, 0:8],
        column_ref[0],
        inside,
    )
    z_bottom, z_top = zedge_ref[0:8, :], zedge_ref[8:16, :]
    bottom_scale, top_scale = section_step * zedge_ref[16:24, :], section_step * zedge_ref[24:32, :]
    bottom_v, bottom_d = fedge_ref[0:8, :], fedge_ref[8:16, :]
    for s, (below, above) in enumerate(((below0, above0), (below1, above1))):
        d = m0[3:4, s : s + 1]
        high = strips_ref[8 * s : 8 * s + 8, :]
        low = strips_ref[16 + 8 * s : 24 + 8 * s, :]
        f_low = flux(bottom_v, bottom_d, d, low, below, z_bottom - below_z)
        f_high = flux(top_v, top_d, d, above, high, above_z - z_top)
        edge[2 * s : 2 * s + 1, :] = from_strips(bottom_scale * f_low)
        edge[2 * s + 1 : 2 * s + 2, :] = from_strips(top_scale * f_high)
    width = 2 * LANES
    lefts = iota((1, LANES), 1) < 64
    evaporated = []
    for c in range(0, chunks, 2):
        both = mm(fuel_ref[...], spots[:, c * LANES : c * LANES + width])
        both = both[0:LANES] + both[LANES:]
        for i in range(2):
            mask = sublane == cell_lane[c + i : c + i + 1]
            fuel = jnp.sum(
                jnp.where(mask, both[:, i * LANES : (i + 1) * LANES], 0.0), axis=0, keepdims=True
            )
            gone = soft[c + i : c + i + 1] * (sig[c + i : c + i + 1] - fuel)
            evaporated.append(gone)
            for k, part in enumerate(split(jnp.where(mask, gone, 0.0), 2)):
                loads[k * LANES : (k + 1) * LANES, (c + i) * LANES : (c + i + 1) * LANES] = part
    source = mm_nt(spots[...], loads[...])
    source = source[:, 0:LANES] + source[:, LANES:]
    row = iota((8, LANES), 0)
    delta = (jnp.where(lax.axis_index("sp") == 0, 1.0, 0.0), 0.0)
    for copy in fetch:
        copy.wait()
    quarter = cells // 4
    copies = []
    for j in range(cells // LANES):
        here = slice(j * LANES, (j + 1) * LANES)
        part = source[j * layers : (j + 1) * layers] * (section_step * vol_ref[:, here])
        for s in range(2):
            new = base_ref[s, :, here] + part * (delta[s] - species_ref[s, :, here])
            first = jnp.where(row == 0, edge[2 * s : 2 * s + 1, here], 0.0)
            last = jnp.where(row == 7, edge[2 * s + 1 : 2 * s + 2, here], 0.0)
            new_ref[s, 0:8, here] = new[0:8] + first
            new_ref[s, 8 : layers - 8, here] = new[8 : layers - 8]
            new_ref[s, layers - 8 :, here] = new[layers - 8 :] - last
        if here.stop % quarter == 0:
            p = slice(here.stop - quarter, here.stop)
            copies.append(
                pltpu.make_async_copy(
                    new_ref.at[:, :, p], new_hbm.at[:, :, p], sems.at[0, p.start // quarter]
                )
            )
            copies[-1].start()
    size = share * parcel_cap
    fetch_number.wait()
    for copy in fetch_flow:
        copy.wait()

    def group(g, carry):
        for i in range(size):
            where = number_smem[g, 64 * (g & 1) + i]
            for f in range(3):
                rows_ref[f, pl.ds(64 * g + i, 1), :] = flow_ref[f, pl.ds(where, 1), :]
        return carry

    lax.fori_loop(0, groups, group, 0)
    index, column = iota((8, PV), 0), iota((8, PV), 1)
    spread = ones(index == 0)
    take = ones((index < 2) & (column == 0))
    index, column = iota((3 * 2 * LANES, PV), 0), iota((3 * 2 * LANES, PV), 1)
    into = ones(column == 3 + lax.div(index, 2 * LANES))
    drag = (iota((size, PV), 1) >= 3) & (iota((size, PV), 1) <= 5)
    keep = jnp.where(drag, 1.0 - friction_timescale, 1.0)
    lane_of = jnp.where(number >= 0, cell_lane, -1).astype(F32)
    none = jnp.zeros((6, LANES), F32)
    for h in range(groups // 2):
        a, b = 2 * h, 2 * h + 1
        lanes = jnp.where(lefts, lane_of[a : a + 1], lane_of[b : b + 1])
        lanes = jnp.concatenate([lanes, lanes, none], axis=0).astype(BF16)
        mask = mm_tn(lanes, spread) == iota((LANES, PV), 1).astype(F32)
        gone = jnp.where(lefts, evaporated[a], evaporated[b])
        head = gone.astype(BF16).astype(F32)
        change = -mm_tn(jnp.concatenate([head, gone - head, none], axis=0).astype(BF16), take)
        fields = []
        for f in range(3):
            fields += split(jnp.where(mask, rows_ref[f, h * LANES : (h + 1) * LANES, :], 0.0), 2)
        change = change + friction_timescale * mm(jnp.concatenate(fields, axis=1), into)
        for i in range(2):
            g = 2 * h + i
            table = jnp.concatenate(
                [got_ref[g * share + k, 0:parcel_cap, :] for k in range(share)], axis=0
            )
            arrived_ref[g * size : (g + 1) * size, :] = table * keep + change[64 * i : 64 * i + size]
    copies.append(pltpu.make_async_copy(arrived_ref, arrived_hbm, sems.at[1, 2]))
    copies[-1].start()
    for copy in copies:
        copy.wait()


def fast(count=1):
    return [pl.BlockSpec(memory_space=pltpu.VMEM)] * count


def slow(count=1):
    return [pl.BlockSpec(memory_space=pltpu.HBM)] * count


def call(kernel, name, out, in_specs, scratch=(), out_specs=None, kib=1024):
    out_specs = out_specs or fast(len(out))
    run = pl.pallas_call(
        kernel,
        out_shape=tuple(
            (pltpu.HBM if spec.memory_space is pltpu.HBM else pltpu.VMEM)(s, t)
            for (s, t), spec in zip(out, out_specs, strict=True)
        ),
        in_specs=in_specs,
        out_specs=tuple(out_specs),
        scratch_shapes=list(scratch),
        compiler_params=pltpu.CompilerParams(vmem_limit_bytes=VMEM_LIMIT),
        cost_estimate=pl.CostEstimate(flops=0, transcendentals=0, bytes_accessed=kib * 1024),
        name=name,
    )

    def held(*operands):
        return run(
            *(
                pltpu.with_memory_space_constraint(a, spec.memory_space)
                for a, spec in zip(operands, in_specs, strict=True)
            )
        )

    return held


def dma(*count):
    return pltpu.SemaphoreType.DMA(count)


def body(
    species,
    interface_normal_flow,
    face_diffusion,
    inv_volume,
    diffusivity,
    low_partner,
    high_partner,
    low_orient,
    high_orient,
    droplet_table,
    parcel_block,
    parcel_cell,
    parcel_live,
):
    blocks = lax.axis_size("blk")
    local_species, layers, cells = species.shape
    parcels = droplet_table.shape[0]
    tile_cap = max(1, TILES // blocks)
    parcel_cap = 3 * parcels // (2 * blocks)
    sizes = (blocks, tile_cap, parcel_cap)
    tall = layers * cells // LANES
    rows = -(-(parcel_cap + PAIRS * tile_cap + 6) // 8) * 8
    groups = blocks * parcel_cap // 48
    int_row = (1, parcels)
    vmem = pltpu.VMEM

    def swap(value, bit):
        return lax.ppermute(value, "sp", [(i, i ^ bit) for i in range(lax.axis_size("sp"))])

    factors = diffusivity.reshape(1, local_species)
    other_species = swap(species, 1)
    other_factors = swap(factors, 1)

    target, cell = parcel_block.reshape(int_row), parcel_cell.reshape(int_row)
    packed, strips, edge_flow, strip, column, code, rank = call(
        functools.partial(pack_rows_kernel, *sizes),
        "pack_rows",
        [
            ((blocks, rows, LANES), F32),
            ((32, STRIP), F32),
            ((16, STRIP), F32),
            ((2, TILES, LANES), F32),
            ((2, TILES, STRIP), F32),
            ((2, TILES, STRIP), F32),
            ((8, parcels), jnp.int32),
        ],
        slow(10),
        [
            vmem((local_species, 8, cells), F32),
            vmem((local_species, 8, cells), F32),
            vmem((8, cells), F32),
            vmem((8, cells), F32),
            vmem((4, 1, TILES), jnp.int32),
            vmem(droplet_table.shape, F32),
            vmem((2,) + int_row, jnp.int32),
            dma(11),
        ],
        kib=13000,
    )(
        species,
        interface_normal_flow,
        face_diffusion,
        low_partner,
        high_partner,
        low_orient,
        high_orient,
        droplet_table,
        target,
        parcel_live.reshape(int_row),
    )

    z_half, fuel_half = call(
        sum_kernel,
        "chip_sum",
        [((layers // 2, cells), F32), ((layers // 2, cells), F32)],
        slow(1) + fast(1) + slow(1) + fast(2),
        [vmem(species.shape, F32), vmem((1, local_species), F32), dma(5)],
        kib=4680,
    )(species, other_species, factors, other_factors, strip)
    z_far = swap(z_half, 2)

    (m0,) = call(
        functools.partial(pack_meta_kernel, blocks, parcel_cap),
        "pack_meta",
        [((4 * blocks + TILES, LANES), F32)],
        slow(4) + fast(6),
        [
            vmem((1, local_species), F32),
            vmem(droplet_table.shape, F32),
            vmem((2,) + int_row, jnp.int32),
            dma(4),
        ],
        kib=6000,
    )(factors, droplet_table, target, cell, strips, strip, column, code, rank, z_half)
    m1, m2, m3 = swap(m0, 1), swap(m0, 2), swap(m0, 3)
    fuel_far = swap(fuel_half, 2)

    ready, z_own = call(
        functools.partial(assemble_kernel, *sizes),
        "assemble",
        [((blocks, rows, LANES), F32), ((layers // 2, cells), F32)],
        fast(7),
        kib=2880,
    )(packed, m0, m1, m2, m3, z_half, z_far)
    z_other = swap(z_own, 1)
    got = lax.all_to_all(ready, "blk", split_axis=0, concat_axis=0, tiled=True)

    base, edge_z = call(
        inner_kernel,
        "inner_flux",
        [(species.shape, F32), ((32, STRIP), F32)],
        slow(4) + fast(3),
        [
            vmem(interface_normal_flow.shape, F32),
            vmem(face_diffusion.shape, F32),
            vmem((layers, cells), F32),
            vmem(species.shape, F32),
            vmem((layers, cells), F32),
            dma(4, 4),
        ],
        kib=25200,
    )(
        interface_normal_flow,
        face_diffusion,
        inv_volume,
        species,
        z_own,
        z_other,
        m0,
    )

    (fuel_own,) = call(
        fuel_half_kernel,
        "fuel_half",
        [((layers // 2, cells), F32)],
        fast(3),
        kib=360,
    )(fuel_half, fuel_far, edge_z)
    fuel_other = swap(fuel_own, 1)
    (fuel_parts,) = call(
        fuel_kernel, "fuel_parts", [((2 * LANES, tall), BF16)], fast(2), kib=1080
    )(fuel_own, fuel_other)

    return call(
        functools.partial(final_kernel, *sizes),
        "final",
        [(species.shape, F32), ((blocks * parcel_cap, PV), F32)],
        fast(3) + slow(3) + fast(6),
        [
            vmem(species.shape, F32),
            vmem((blocks * parcel_cap, PV), F32),
            vmem((tall, 2 * groups * LANES), BF16),
            vmem((2 * LANES, 2 * groups * LANES), BF16),
            vmem((8, cells), F32),
            vmem(species.shape, F32),
            vmem((layers, cells), F32),
            vmem((3, tall, LANES), F32),
            vmem((2 * groups, LANES), jnp.int32),
            pltpu.SMEM((2 * groups, LANES), jnp.int32),
            vmem((3, 64 * groups, PV), F32),
            dma(2, 4),
            dma(cells // LANES),
            pltpu.SemaphoreType.DMA,
        ],
        slow(2),
        kib=32400,
    )(
        got,
        fuel_parts,
        base,
        species,
        inv_volume,
        interface_normal_flow,
        edge_z,
        edge_flow,
        strips,
        strip,
        column,
        m0,
    )


def solution(mesh):
    placed = (
        P("sp", "blk", None),
        P(None, "blk", None),
        P(None, "blk", None),
        P("blk", None),
        P("sp"),
        P("blk", None),
        P("blk", None),
        P("blk", None),
        P("blk", None),
        P(("blk", "sp"), None),
        P(("blk", "sp"), None),
        P(("blk", "sp")),
        P(("blk", "sp")),
    )
    return jax.shard_map(
        body,
        mesh=mesh,
        in_specs=placed,
        out_specs=(P("sp", "blk", None), P(("blk", "sp"), None)),
        check_vma=False,
    )
```

time: 253 us -> 43.8 us (0.17); the launches traced: 249 us -> 43.5 us
  local copies, waits for them, and re-layouts: 103 us -> 0 us
  other arithmetic: 58.6 us -> 0 us
  waiting for transfers between devices: 32.3 us -> 8.1 us
  Pallas kernels: 0 us -> 21.5 us
  starting transfers between devices: 27.9 us -> 13.2 us
  between operations: 14.9 us -> 0.73 us
  blocking collectives: 12.3 us -> 0 us
    unnamed x83 -> x0, local copies, waits for them, and re-layouts: 37.2 us -> none
    psum x2 -> x0, waiting for transfers between devices: 27.1 us -> none  [the longest x1 27.1 us: body(): lax.psum((partial_terms[0], partial_terms[1], partial_terms[2], partial_t...]
    gather x6 -> x0, local copies, waits for them, and re-layouts: 24.4 us -> none  [the longest x1 11.6 us: body(): evaporate_component = fuel_field[landing_grid_points]]
    all_to_all x5 -> x1, starting transfers between devices: 27.9 us -> 6.08 us  [body(): got = lax.all_to_all(ready, 'blk', split_axis=0, concat_axis=0, tiled=True)]
    pallas_call x0 -> x8, Pallas kernels: none -> 21.5 us  [held(): run(*(pltpu.with_memory_space_constraint(a, spec.memory_space) for a, spe...]
    psum x1 -> x0, blocking collectives: 12.3 us -> none  [body(): lax.psum((partial_terms[0], partial_terms[1], partial_terms[2], partial_t...]
    mul x10 -> x0, other arithmetic: 11.7 us -> none  [the longest x2 5.18 us: face_flux(): diffusion * (scaled * difference - middle * weight)]
    scatter x5 -> x0, local copies, waits for them, and re-layouts: 11.5 us -> none  [the longest x1 3.13 us: body(): send_high = jnp.zeros((blocks, tile_cap) + high_pack.shape[1:], jnp.float...]
  transfers between devices with their start and end apart: 7 -> 10, of which waited for: 2 -> 4; matrix products, arithmetic and copies ran while one was open for 52% -> 0% of each run, Pallas kernels for 0% -> 26%
where the time goes in v2:
time: 43.8 us; the launch traced here: 43.5 us
  Pallas kernels  21.5 us (49%)
  starting transfers between devices  13.2 us (30%)
  waiting for transfers between devices  8.1 us (18%)
  between operations  0.73 us (2%)
    pallas_call x8, Pallas kernels, held(): run(*(pltpu.with_memory_space_constraint(a, spec.memory_space) for a, spe...  21.5 us
    ppermute x9, waiting for transfers between devices, swap(): lax.ppermute(value, 'sp', [(i, i ^ bit) for i in range(lax.axis_size('sp'...  8.1 us
    ppermute x9, starting transfers between devices, swap(): lax.ppermute(value, 'sp', [(i, i ^ bit) for i in range(lax.axis_size('sp'...  7.13 us
    all_to_all x1, starting transfers between devices, body(): got = lax.all_to_all(ready, 'blk', split_axis=0, concat_axis=0, tiled=True)  6.08 us
  transfers between devices with their start and end apart: 10, of which 4 were waited for; matrix products, arithmetic and copies ran while one was open for 0% of the time, Pallas kernels for 26%

profile of v2, /device:TPU:0, one launch (start us, length us, event | category | flops | bytes accessed | tf_op | source)
XLA Modules:
  0.0 43.5 jit_solution(14743804332225475553)
XLA Ops:
  0.6 0.5 %collective-permute-start = (f32[2,32,4096]{2,1,0:T(8,128)}, f32[2,32,4096]{2,1,0:T(8,128)S(1)}, u32[]{:S(2)}, u32[]{:S(2)}) collective-permute-start(f32[2,32,4096]{2,1,0:T(8,128)} %species.7), channel_id=1, source_target_pairs={{0,1},{1,0},{2,3},{3,2},{4,5},{5,4},{6,7},{7,6},{8,9},{9,8},{10,11... | collective-permute-start | bytes 3145736 | tf_op jit(solution)/shard_map/ppermute | solution.py:700
  1.1 0.1 collective-permute-start.1
  1.2 3.7 %pack_rows.1 = (f32[8,88,128]{2,1,0:T(8,128)S(1)}, f32[32,512]{1,0:T(8,128)S(1)}, f32[16,512]{1,0:T(8,128)S(1)}, f32[2,64,128]{2,1,0:T(8,128)S(1)}, f32[2,64,512...) custom-call(f32[2,32,4096]{2,1,0:T(8,128)} %species.7, f32[3,32,4096]{2,1,0:T(8,128)} %flow.5, ...), custom_call_target="tpu_custom_call" | custom-call | bytes 13312000 | tf_op jit(solution)/shard_map/pack_rows/pallas_call | solution.py:658
  4.9 0.0 collective-permute-done.1.d_other
  4.9 1.3 %chip_sum.1 = (f32[16,4096]{1,0:T(8,128)S(1)}, f32[16,4096]{1,0:T(8,128)S(1)}) custom-call(f32[2,32,4096]{2,1,0:T(8,128)} %species.7, f32[2,32,4096]{2,1,0:T(8,128)S(1)} %collective-permute-done.other_ref, f32[1,2]{1,0:T(1,128)} %bitcast.7, f32[1,2]{1,0:T(1,128)S(1)} %collective-permute-done.1.d_other, f32[2,64,128]{2,1,0:T(8,128)S(1)} %get-tuple-element.17.strip.strip_ref), custom_call_target="tpu_custom_call" | custom-call | bytes 4792320 | tf_op jit(solution)/shard_map/chip_sum/pallas_call | solution.py:658
  6.2 3.0 %collective-permute-start.5 = (f32[16,4096]{1,0:T(8,128)S(1)}, f32[16,4096]{1,0:T(8,128)S(1)}, u32[]{:S(2)}, u32[]{:S(2)}) collective-permute-start(f32[16,4096]{1,0:T(8,128)S(1)} %get-tuple-element.21.z_half.z_near), channel_id=1, source_target_pairs={{0,2},{1,3},{2,0},{3,1},{4,6},{5,7},{6,4},{7,5},{8,10},{9,11},{10,... | collective-permute-start | bytes 786440 | tf_op jit(solution)/shard_map/ppermute | solution.py:700
  9.2 1.9 %pack_meta.1.m0 = f32[96,128]{1,0:T(8,128)S(1)} custom-call(f32[1,2]{1,0:T(1,128)} %bitcast.8, f32[256,128]{1,0:T(8,128)} %table.3, s32[1,256]{1,0:T(1,128)} %bitcast.5, s32[1,256]{1,0:T(1,128)} %bitcast.10, f32[32,512]{1,0:T(8,128)S(1)} %get-tuple-element.16.strips_ref, f32[2,64,128]{2,1,0:T(8,128)S(1)} %get-tuple-element.17.strip.strip_ref, ...), custom_call_target="tpu_custom_call" | custom-call | bytes 6144000 | tf_op jit(solution)/shard_map/pack_meta/pallas_call | solution.py:658
  11.1 0.1 collective-permute-start.4
  11.2 1.4 %collective-permute-start.3 = (f32[96,128]{1,0:T(8,128)S(1)}, f32[96,128]{1,0:T(8,128)S(1)}, u32[]{:S(2)}, u32[]{:S(2)}) collective-permute-start(f32[96,128]{1,0:T(8,128)S(1)} %pack_meta.1.m0), channel_id=1, source_target_pairs={{0,2},{1,3},{2,0},{3,1},{4,6},{5,7},{6,4},{7,5},{8,10},{9,11},{10,... | collective-permute-start | bytes 147464 | tf_op jit(solution)/shard_map/ppermute | solution.py:700
  12.6 0.4 collective-permute-start.2
  13.0 3.6 %collective-permute-done.4.m3 = f32[96,128]{1,0:T(8,128)S(1)} collective-permute-done((f32[96,128]{1,0:T(8,128)S(1)}, f32[96,128]{1,0:T(8,128)S(1)}, u32[]{:S(2)}, u32[]{:S(2)}) %collective-permute-start.4) | collective-permute-done | bytes 49184 | tf_op jit(solution)/shard_map/ppermute | solution.py:700
  16.6 1.3 %collective-permute-done.3.m2 = f32[96,128]{1,0:T(8,128)S(1)} collective-permute-done((f32[96,128]{1,0:T(8,128)S(1)}, f32[96,128]{1,0:T(8,128)S(1)}, u32[]{:S(2)}, u32[]{:S(2)}) %collective-permute-start.3) | collective-permute-done | bytes 49184 | tf_op jit(solution)/shard_map/ppermute | solution.py:700
  17.9 0.0 collective-permute-done.2.m1
  17.9 0.8 %assemble.1 = (f32[8,88,128]{2,1,0:T(8,128)}, f32[16,4096]{1,0:T(8,128)S(1)}) custom-call(f32[8,88,128]{2,1,0:T(8,128)S(1)} %get-tuple-element.15.buf_ref, f32[96,128]{1,0:T(8,128)S(1)} %pack_meta.1.m0, f32[96,128]{1,0:T(8,128)S(1)} %collective-permute-done.2.m1, f32[96,128]{1,0:T(8,128)S(1)} %collective-permute-done.3.m2, ...), custom_call_target="tpu_custom_call" | custom-call | bytes 2949120 | tf_op jit(solution)/shard_map/assemble/pallas_call | solution.py:658
  18.7 6.1 %all-to-all-start = ((f32[8,88,128]{2,1,0:T(8,128)}), f32[8,88,128]{2,1,0:T(8,128)S(1)}, u32[]{:S(2)}, u32[]{:S(2)}) async-start(f32[8,88,128]{2,1,0:T(8,128)} %get-tuple-element.22), calls=%async_computation | async-start | bytes 720896 | tf_op jit(solution)/shard_map/all_to_all | solution.py:778
  24.8 0.0 collective-permute-start.7
  24.8 1.6 %collective-permute-start.6 = (f32[16,4096]{1,0:T(8,128)S(1)}, f32[16,4096]{1,0:T(8,128)S(1)}, u32[]{:S(2)}, u32[]{:S(2)}) collective-permute-start(f32[16,4096]{1,0:T(8,128)S(1)} %get-tuple-element.23.near_ref), channel_id=1, source_target_pairs={{0,2},{1,3},{2,0},{3,1},{4,6},{5,7},{6,4},{7,5},{8,10},{9,11},{10,... | collective-permute-start | bytes 786440 | tf_op jit(solution)/shard_map/ppermute | solution.py:700
  26.4 5.5 %inner_flux.1 = (f32[2,32,4096]{2,1,0:T(8,128)S(1)}, f32[32,512]{1,0:T(8,128)S(1)}) custom-call(f32[3,32,4096]{2,1,0:T(8,128)} %flow.5, f32[3,32,4096]{2,1,0:T(8,128)} %diff.3, f32[32,4096]{1,0:T(8,128)} %vol.3, f32[2,32,4096]{2,1,0:T(8,128)} %species.7, f32[16,4096]{1,0:T(8,128)S(1)} %get-tuple-element.24.za_ref, ...), custom_call_target="tpu_custom_call" | custom-call | bytes 25804800 | tf_op jit(solution)/shard_map/inner_flux/pallas_call | solution.py:658
  31.8 1.7 %collective-permute-done.6.far_ref = f32[16,4096]{1,0:T(8,128)S(1)} collective-permute-done((f32[16,4096]{1,0:T(8,128)S(1)}, f32[16,4096]{1,0:T(8,128)S(1)}, u32[]{:S(2)}, u32[]{:S(2)}) %collective-permute-start.6) | collective-permute-done | bytes 262176 | tf_op jit(solution)/shard_map/ppermute | solution.py:700
  33.5 0.1 collective-permute-start.8
  33.6 1.5 %collective-permute-done.8.other_ref = f32[16,4096]{1,0:T(8,128)S(1)} collective-permute-done((f32[16,4096]{1,0:T(8,128)S(1)}, f32[16,4096]{1,0:T(8,128)S(1)}, u32[]{:S(2)}, u32[]{:S(2)}) %collective-permute-start.8) | collective-permute-done | bytes 262176 | tf_op jit(solution)/shard_map/ppermute | solution.py:700
  35.1 0.2 fuel_parts.1.fuel_ref
  35.4 0.0 all-to-all-done.got_ref
  35.4 8.2 %final.1 = (f32[2,32,4096]{2,1,0:T(8,128)}, f32[384,128]{1,0:T(8,128)}) custom-call(f32[8,88,128]{2,1,0:T(8,128)S(1)} %all-to-all-done.got_ref, bf16[256,1024]{1,0:T(8,128)(2,1)S(1)} %fuel_parts.1.fuel_ref, f32[2,32,4096]{2,1,0:T(8,128)S(1)} %get-tuple-element.26.base_ref, f32[2,32,4096]{2,1,0:T(8,128)} %species.7, f32[32,4096]{1,0:T(8,128)} %vol.3, ...), custom_call_target="tpu_custom_call" | custom-call | bytes 33177600 | tf_op jit(solution)/shard_map/final/pallas_call | solution.py:658
  (4 shorter events, 0.0 us)
Async XLA Ops:
  0.6 4.3 %collective-permute-start = (f32[2,32,4096]{2,1,0:T(8,128)}, f32[2,32,4096]{2,1,0:T(8,128)S(1)}, u32[]{:S(2)}, u32[]{:S(2)}) collective-permute-start(f32[2,32,4096]{2,1,0:T(8,128)} %species.7), channel_id=1, source_target_pairs={{0,1},{1,0},{2,3},{3,2},{4,5},{5,4},{6,7},{7,6},{8,9},{9,8},{10,11... | collective-permute-start | bytes 3145736 | tf_op jit(solution)/shard_map/ppermute | solution.py:700
  1.1 3.8 %collective-permute-start.1 = (f32[1,2]{1,0:T(1,128)}, f32[1,2]{1,0:T(1,128)S(1)}, u32[]{:S(2)}, u32[]{:S(2)}) collective-permute-start(f32[1,2]{1,0:T(1,128)} %bitcast.6), channel_id=1, source_target_pairs={{0,1},{1,0},{2,3},{3,2},{4,5},{5,4},{6,7},{7,6},{8,9},{9,8},{10,11... | collective-permute-start | bytes 32 | tf_op jit(solution)/shard_map/ppermute | solution.py:700
  6.2 11.7 %collective-permute-start.5 = (f32[16,4096]{1,0:T(8,128)S(1)}, f32[16,4096]{1,0:T(8,128)S(1)}, u32[]{:S(2)}, u32[]{:S(2)}) collective-permute-start(f32[16,4096]{1,0:T(8,128)S(1)} %get-tuple-element.21.z_half.z_near), channel_id=1, source_target_pairs={{0,2},{1,3},{2,0},{3,1},{4,6},{5,7},{6,4},{7,5},{8,10},{9,11},{10,... | collective-permute-start | bytes 786440 | tf_op jit(solution)/shard_map/ppermute | solution.py:700
  11.1 5.5 %collective-permute-start.4 = (f32[96,128]{1,0:T(8,128)S(1)}, f32[96,128]{1,0:T(8,128)S(1)}, u32[]{:S(2)}, u32[]{:S(2)}) collective-permute-start(f32[96,128]{1,0:T(8,128)S(1)} %pack_meta.1.m0), channel_id=1, source_target_pairs={{0,3},{1,2},{2,1},{3,0},{4,7},{5,6},{6,5},{7,4},{8,11},{9,10},{10,... | collective-permute-start | bytes 147464 | tf_op jit(solution)/shard_map/ppermute | solution.py:700
  11.2 6.7 %collective-permute-start.3 = (f32[96,128]{1,0:T(8,128)S(1)}, f32[96,128]{1,0:T(8,128)S(1)}, u32[]{:S(2)}, u32[]{:S(2)}) collective-permute-start(f32[96,128]{1,0:T(8,128)S(1)} %pack_meta.1.m0), channel_id=1, source_target_pairs={{0,2},{1,3},{2,0},{3,1},{4,6},{5,7},{6,4},{7,5},{8,10},{9,11},{10,... | collective-permute-start | bytes 147464 | tf_op jit(solution)/shard_map/ppermute | solution.py:700
  12.6 5.3 %collective-permute-start.2 = (f32[96,128]{1,0:T(8,128)S(1)}, f32[96,128]{1,0:T(8,128)S(1)}, u32[]{:S(2)}, u32[]{:S(2)}) collective-permute-start(f32[96,128]{1,0:T(8,128)S(1)} %pack_meta.1.m0), channel_id=1, source_target_pairs={{0,1},{1,0},{2,3},{3,2},{4,5},{5,4},{6,7},{7,6},{8,9},{9,8},{10,11... | collective-permute-start | bytes 147464 | tf_op jit(solution)/shard_map/ppermute | solution.py:700
  18.7 16.7 %all-to-all-start = ((f32[8,88,128]{2,1,0:T(8,128)}), f32[8,88,128]{2,1,0:T(8,128)S(1)}, u32[]{:S(2)}, u32[]{:S(2)}) async-start(f32[8,88,128]{2,1,0:T(8,128)} %get-tuple-element.22), calls=%async_computation | async-start | bytes 720896 | tf_op jit(solution)/shard_map/all_to_all | solution.py:778
  24.8 1.6 %collective-permute-start.7 = (f32[16,4096]{1,0:T(8,128)S(1)}, f32[16,4096]{1,0:T(8,128)S(1)}, u32[]{:S(2)}, u32[]{:S(2)}) collective-permute-start(f32[16,4096]{1,0:T(8,128)S(1)} %get-tuple-element.24.za_ref), channel_id=1, source_target_pairs={{0,1},{1,0},{2,3},{3,2},{4,5},{5,4},{6,7},{7,6},{8,9},{9,8},{10,11... | collective-permute-start | bytes 786440 | tf_op jit(solution)/shard_map/ppermute | solution.py:700
  24.8 8.7 %collective-permute-start.6 = (f32[16,4096]{1,0:T(8,128)S(1)}, f32[16,4096]{1,0:T(8,128)S(1)}, u32[]{:S(2)}, u32[]{:S(2)}) collective-permute-start(f32[16,4096]{1,0:T(8,128)S(1)} %get-tuple-element.23.near_ref), channel_id=1, source_target_pairs={{0,2},{1,3},{2,0},{3,1},{4,6},{5,7},{6,4},{7,5},{8,10},{9,11},{10,... | collective-permute-start | bytes 786440 | tf_op jit(solution)/shard_map/ppermute | solution.py:700
  33.5 1.6 %collective-permute-start.8 = (f32[16,4096]{1,0:T(8,128)S(1)}, f32[16,4096]{1,0:T(8,128)S(1)}, u32[]{:S(2)}, u32[]{:S(2)}) collective-permute-start(f32[16,4096]{1,0:T(8,128)S(1)} %fuel_half.1.own_ref), channel_id=1, source_target_pairs={{0,1},{1,0},{2,3},{3,2},{4,5},{5,4},{6,7},{7,6},{8,9},{9,8},{10,11... | collective-permute-start | bytes 786440 | tf_op jit(solution)/shard_map/ppermute | solution.py:700

commit v3 on v2

--- a/solution.py
+++ b/solution.py
@@ -117,31 +117,29 @@
     return started
 
 
-def pack_rows_kernel(
+def pack_meta_kernel(
     blocks,
     tile_cap,
     parcel_cap,
     species,
-    flow,
-    diff,
+    diffusivity,
     low_partner,
     high_partner,
     low_orient,
     high_orient,
     table,
     block,
+    cell,
     live,
-    out_ref,
+    m_ref,
     strips_ref,
-    edge_ref,
     strip_ref,
     column_ref,
     code_ref,
-    rank_ref,
+    slot_ref,
     bottom,
     top,
-    vel_in,
-    dif_in,
+    d_own,
     small,
     table_in,
     parcel,
@@ -151,11 +149,12 @@
     copies = begin(
         [(high_partner, small.at[0]), (low_partner, small.at[1])]
         + [(high_orient, small.at[2]), (low_orient, small.at[3])]
-        + [(block, parcel.at[0]), (live, parcel.at[1]), (table, table_in)]
-        + [(species.at[:, layers - 8 :], top), (species.at[:, 0:8], bottom)]
-        + [(flow.at[0, 0:8], vel_in), (diff.at[0, 0:8], dif_in)],
+        + [(block, parcel.at[0]), (live, parcel.at[1]), (cell, parcel.at[2])]
+        + [(table, table_in), (diffusivity, d_own)]
+        + [(species.at[:, layers - 8 :], top), (species.at[:, 0:8], bottom)],
         sems,
     )
+    me = lax.axis_index("blk")
     inside, turn = inside_table(), orient_table()
     tile = iota((TILES, STRIP), 0)
     strip_of = ones((iota((TILES, LANES), 0) >> 3) == iota((TILES, LANES), 1))
@@ -171,27 +170,80 @@
         column_ref[k] = mm(place, column_of)
         code = ones(iota((8, TILES), 0) == small[2 + k])
         code_ref[k] = mm(mm_nt(place, code).astype(BF16), code_of)
-    for copy in copies[4:7]:
+    for copy in copies[4:8]:
         copy.wait()
     target = parcel[0]
     alive = parcel[1] == 1
     onehot = ones((iota((blocks, rows), 0) == target) & alive, F32)
     rank = jnp.sum(onehot * mm(onehot.astype(BF16), earlier), axis=0, keepdims=True)
     rank = rank.astype(jnp.int32)
-    rank_ref[...] = jnp.broadcast_to(jnp.where(alive, rank, -1), (8, rows))
-    slot = jnp.where(alive, target * parcel_cap + rank, -1)
-    send = ones(iota((blocks * parcel_cap, rows), 0) == slot)
+    slot_ref[...] = jnp.broadcast_to(jnp.where(alive, target * parcel_cap + rank, -1), (8, rows))
+    pick = ones(iota((8, PV), 1) == iota((8, PV), 0) + 1)
     parts = split(table_in[...], 3)
-    sent = mm(send, parts[2]) + mm(send, parts[1]) + mm(send, parts[0])
-    for copy in copies[7:]:
-        copy.wait()
+    columns = mm_nt(pick, parts[2]) + mm_nt(pick, parts[1]) + mm_nt(pick, parts[0])
+    p1, p2 = columns[0:1], columns[1:2]
+    soft = jnp.maximum(p1, 0.0) + jnp.log1p(jnp.exp(-jnp.abs(p1)))
+    sig = 1.0 / (1.0 + jnp.exp(-p2))
+    fields = jnp.concatenate(
+        [(parcel[2] + 1).astype(F32), soft, sig, jnp.zeros((5, rows), F32)], axis=0
+    )
+    share = 48 // parcel_cap
+    lane = rank + lax.rem(me, share) * parcel_cap + 64 * (lax.div(me, share) & 1)
+    goal = jnp.where(alive, target * LANES + lane, -1)
+    spots = ones(iota((blocks * LANES, rows), 0) == goal)
+    meta = mm_nt(jnp.concatenate(split(fields, 3), axis=0), spots)
+    meta = meta[16:24] + meta[8:16] + meta[0:8]
+    copies[8].wait()
+    d0, d1 = d_own[0:1, 0:1], d_own[0:1, 1:2]
+    lanes = iota((1, LANES), 1)
+    own = jnp.where(lanes == 0, d0, jnp.where(lanes == 1, d1, 0.0))
+    for b in range(blocks):
+        m_ref[4 * b : 4 * b + 3, :] = meta[0:3, b * LANES : (b + 1) * LANES]
+        m_ref[4 * b + 3 : 4 * b + 4, :] = own
+    copies[9].wait()
+    copies[10].wait()
     top0, top1 = to_strips(top[0, 7:8, :]), to_strips(top[1, 7:8, :])
     low0, low1 = to_strips(bottom[0, 0:1, :]), to_strips(bottom[1, 0:1, :])
     strips_ref[...] = jnp.concatenate([top0, top1, low0, low1], axis=0)
+    tiles = []
+    for k, face in enumerate((d0 * top0 + d1 * top1, d0 * low0 + d1 * low1)):
+        strip = strip_ref[k][:, 0:8].astype(BF16)
+        tiles += take_tiles([face], strip, column_ref[k], code_ref[k], inside)
+    high, low = turn_tiles(tiles, turn)
+    m_ref[4 * blocks : 4 * blocks + TILES, :] = jnp.where(lanes < 64, high, low)
+
+
+def pack_rows_kernel(
+    blocks,
+    tile_cap,
+    parcel_cap,
+    flow,
+    diff,
+    table,
+    strips_ref,
+    strip_ref,
+    column_ref,
+    code_ref,
+    slot_ref,
+    z_half,
+    out_ref,
+    edge_ref,
+    vel_in,
+    dif_in,
+    table_in,
+    sems,
+):
+    copies = begin(
+        [(flow.at[0, 0:8], vel_in), (diff.at[0, 0:8], dif_in), (table, table_in)], sems
+    )
+    inside, turn = inside_table(), orient_table()
+    faces = [strips_ref[8 * i : 8 * i + 8, :] for i in range(4)]
+    copies[0].wait()
+    copies[1].wait()
     vel, dif = to_strips(vel_in[0:1, :]), to_strips(dif_in[0:1, :])
     edge_ref[...] = jnp.concatenate([vel, dif], axis=0)
     tiles = []
-    for k, some in enumerate(([top0, top1], [low0, low1, vel, dif])):
+    for k, some in enumerate((faces[0:2], faces[2:4] + [vel, dif])):
         strip = strip_ref[k][:, 0:8].astype(BF16)
         tiles += take_tiles(some, strip, column_ref[k], code_ref[k], inside)
     high0, high1, low0, low1, vel, dif = turn_tiles(tiles, turn)
@@ -201,6 +253,11 @@
         jnp.where(left, pltpu.roll(low0, 64, 1), low1),
         jnp.where(left, pltpu.roll(vel, 64, 1), dif),
     ]
+    copies[2].wait()
+    rows = table.shape[0]
+    send = ones(iota((blocks * parcel_cap, rows), 0) == slot_ref[0:1, :])
+    parts = split(table_in[...], 3)
+    sent = mm(send, parts[2]) + mm(send, parts[1]) + mm(send, parts[0])
     for b in range(blocks):
         out_ref[b, 0:parcel_cap, :] = sent[b * parcel_cap : (b + 1) * parcel_cap]
         for k in range(PAIRS - 1):
@@ -208,68 +265,11 @@
             out_ref[b, at : at + tile_cap, :] = pairs[k][b * tile_cap : (b + 1) * tile_cap]
 
 
-def pack_meta_kernel(
-    blocks,
-    parcel_cap,
-    factors,
-    table,
-    block,
-    cell,
-    strips_ref,
-    strip_ref,
-    column_ref,
-    code_ref,
-    rank_ref,
-    z_half,
-    m_ref,
-    d_own,
-    table_in,
-    parcel,
-    sems,
-):
-    copies = begin(
-        [(table, table_in), (block, parcel.at[0]), (cell, parcel.at[1]), (factors, d_own)], sems
-    )
-    rows = table.shape[0]
-    me = lax.axis_index("blk")
-    inside, turn = inside_table(), orient_table()
-    pick = ones(iota((8, PV), 1) == iota((8, PV), 0) + 1)
-    for copy in copies:
-        copy.wait()
-    d0, d1 = d_own[0:1, 0:1], d_own[0:1, 1:2]
-    tiles = []
-    for k in range(2):
-        strip = strip_ref[k][:, 0:8].astype(BF16)
-        face = d0 * strips_ref[16 * k : 16 * k + 8, :] + d1 * strips_ref[16 * k + 8 : 16 * k + 16, :]
-        tiles += take_tiles([face], strip, column_ref[k], code_ref[k], inside)
-    high, low = turn_tiles(tiles, turn)
-    lanes = iota((1, LANES), 1)
-    m_ref[4 * blocks : 4 * blocks + TILES, :] = jnp.where(lanes < 64, high, low)
-    parts = split(table_in[...], 3)
-    columns = mm_nt(pick, parts[2]) + mm_nt(pick, parts[1]) + mm_nt(pick, parts[0])
-    p1, p2 = columns[0:1], columns[1:2]
-    soft = jnp.maximum(p1, 0.0) + jnp.log1p(jnp.exp(-jnp.abs(p1)))
-    sig = 1.0 / (1.0 + jnp.exp(-p2))
-    fields = jnp.concatenate(
-        [(parcel[1] + 1).astype(F32), soft, sig, jnp.zeros((5, rows), F32)], axis=0
-    )
-    rank = rank_ref[0:1, :]
-    share = 48 // parcel_cap
-    lane = rank + lax.rem(me, share) * parcel_cap + 64 * (lax.div(me, share) & 1)
-    goal = jnp.where(rank >= 0, parcel[0] * LANES + lane, -1)
-    spots = ones(iota((blocks * LANES, rows), 0) == goal)
-    meta = mm_nt(jnp.concatenate(split(fields, 3), axis=0), spots)
-    meta = meta[16:24] + meta[8:16] + meta[0:8]
-    own = jnp.where(lanes == 0, d0, jnp.where(lanes == 1, d1, 0.0))
-    for b in range(blocks):
-        m_ref[4 * b : 4 * b + 3, :] = meta[0:3, b * LANES : (b + 1) * LANES]
-        m_ref[4 * b + 3 : 4 * b + 4, :] = own
-
-
-def assemble_kernel(
-    blocks, tile_cap, parcel_cap, buf_ref, m0, m1, m2, m3, z_near, z_far, out_ref, z_ref
-):
-    z_ref[...] = z_near[...] + z_far[...]
+def add_kernel(near_ref, far_ref, out_ref):
+    out_ref[...] = near_ref[...] + far_ref[...]
+
+
+def assemble_kernel(blocks, tile_cap, parcel_cap, buf_ref, m0, m1, m2, m3, z_half, out_ref):
     ghost = parcel_cap + (PAIRS - 1) * tile_cap
     z = slice(4 * blocks, 4 * blocks + TILES)
     total = (m0[z, :] + m1[z, :]) + (m2[z, :] + m3[z, :])
@@ -286,7 +286,7 @@
 
 
 def sum_kernel(
-    species, other_ref, factors, d_other, strip, zh_ref, fh_ref, own_ref, d_own, sems
+    species, other_ref, factors, d_other, after0, after1, after2, after3, zh_ref, fh_ref, own_ref, d_own, sems
 ):
     half, cells = zh_ref.shape
     quarter = cells // 4
@@ -703,14 +703,12 @@
     other_species = swap(species, 1)
     other_factors = swap(factors, 1)
 
-    target, cell = parcel_block.reshape(int_row), parcel_cell.reshape(int_row)
-    packed, strips, edge_flow, strip, column, code, rank = call(
-        functools.partial(pack_rows_kernel, *sizes),
-        "pack_rows",
+    m0, strips, strip, column, code, slot = call(
+        functools.partial(pack_meta_kernel, *sizes),
+        "pack_meta",
         [
-            ((blocks, rows, LANES), F32),
+            ((4 * blocks + TILES, LANES), F32),
             ((32, STRIP), F32),
-            ((16, STRIP), F32),
             ((2, TILES, LANES), F32),
             ((2, TILES, STRIP), F32),
             ((2, TILES, STRIP), F32),
@@ -720,60 +718,72 @@
         [
             vmem((local_species, 8, cells), F32),
             vmem((local_species, 8, cells), F32),
-            vmem((8, cells), F32),
-            vmem((8, cells), F32),
+            vmem((1, local_species), F32),
             vmem((4, 1, TILES), jnp.int32),
             vmem(droplet_table.shape, F32),
-            vmem((2,) + int_row, jnp.int32),
+            vmem((3,) + int_row, jnp.int32),
             dma(11),
         ],
-        kib=13000,
+        kib=10000,
     )(
         species,
-        interface_normal_flow,
-        face_diffusion,
+        factors,
         low_partner,
         high_partner,
         low_orient,
         high_orient,
         droplet_table,
-        target,
+        parcel_block.reshape(int_row),
+        parcel_cell.reshape(int_row),
         parcel_live.reshape(int_row),
     )
-
+    m1, m2, m3 = swap(m0, 1), swap(m0, 2), swap(m0, 3)
+
+
+    packed, edge_flow = call(
+        functools.partial(pack_rows_kernel, *sizes),
+        "pack_rows",
+        [((blocks, rows, LANES), F32), ((16, STRIP), F32)],
+        slow(3) + fast(6),
+        [
+            vmem((8, cells), F32),
+            vmem((8, cells), F32),
+            vmem(droplet_table.shape, F32),
+            dma(3),
+        ],
+        kib=10000,
+    )(
+        interface_normal_flow,
+        face_diffusion,
+        droplet_table,
+        strips,
+        strip,
+        column,
+        code,
+        slot,
+        m0,
+    )
     z_half, fuel_half = call(
         sum_kernel,
         "chip_sum",
         [((layers // 2, cells), F32), ((layers // 2, cells), F32)],
-        slow(1) + fast(1) + slow(1) + fast(2),
+        slow(1) + fast(1) + slow(1) + fast(5),
         [vmem(species.shape, F32), vmem((1, local_species), F32), dma(5)],
         kib=4680,
-    )(species, other_species, factors, other_factors, strip)
+    )(species, other_species, factors, other_factors, m1, m2, m3, edge_flow)
     z_far = swap(z_half, 2)
-
-    (m0,) = call(
-        functools.partial(pack_meta_kernel, blocks, parcel_cap),
-        "pack_meta",
-        [((4 * blocks + TILES, LANES), F32)],
-        slow(4) + fast(6),
-        [
-            vmem((1, local_species), F32),
-            vmem(droplet_table.shape, F32),
-            vmem((2,) + int_row, jnp.int32),
-            dma(4),
-        ],
-        kib=6000,
-    )(factors, droplet_table, target, cell, strips, strip, column, code, rank, z_half)
-    m1, m2, m3 = swap(m0, 1), swap(m0, 2), swap(m0, 3)
     fuel_far = swap(fuel_half, 2)
 
-    ready, z_own = call(
+    (z_own,) = call(
+        add_kernel, "z_own", [((layers // 2, cells), F32)], fast(2), kib=1000
+    )(z_half, z_far)
+    (ready,) = call(
         functools.partial(assemble_kernel, *sizes),
         "assemble",
-        [((blocks, rows, LANES), F32), ((layers // 2, cells), F32)],
-        fast(7),
+        [((blocks, rows, LANES), F32)],
+        fast(6),
         kib=2880,
-    )(packed, m0, m1, m2, m3, z_half, z_far)
+    )(packed, m0, m1, m2, m3, z_half)
     z_other = swap(z_own, 1)
     got = lax.all_to_all(ready, "blk", split_axis=0, concat_axis=0, tiled=True)
 

time: 43.8 us -> 39.4 us (0.90)
  waiting for transfers between devices: 8.1 us -> 4.08 us
  starting transfers between devices: 13.2 us -> 12.7 us
    ppermute x9, waiting for transfers between devices: 8.1 us -> 3.86 us  [swap(): lax.ppermute(value, 'sp', [(i, i ^ bit) for i in range(lax.axis_size('sp'...]
    pallas_call x8 -> x9, Pallas kernels: 21.5 us -> 21.6 us  [held(): run(*(pltpu.with_memory_space_constraint(a, spec.memory_space) for a, spe...]
  transfers between devices with their start and end apart: 10 -> 10, of which waited for: 4 -> 4; matrix products, arithmetic and copies ran while one was open for 0% -> 0% of each run, Pallas kernels for 26% -> 31%
where the time goes in v3:
time: 39.4 us; the launch traced here: 39.2 us
  Pallas kernels  21.6 us (55%)
  starting transfers between devices  12.7 us (32%)
  waiting for transfers between devices  4.08 us (10%)
  between operations  0.73 us (2%)
    pallas_call x9, Pallas kernels, held(): run(*(pltpu.with_memory_space_constraint(a, spec.memory_space) for a, spe...  21.6 us
    ppermute x9, starting transfers between devices, swap(): lax.ppermute(value, 'sp', [(i, i ^ bit) for i in range(lax.axis_size('sp'...  6.91 us
    all_to_all x1, starting transfers between devices, body(): got = lax.all_to_all(ready, 'blk', split_axis=0, concat_axis=0, tiled=True)  5.82 us
    ppermute x9, waiting for transfers between devices, swap(): lax.ppermute(value, 'sp', [(i, i ^ bit) for i in range(lax.axis_size('sp'...  3.86 us
  transfers between devices with their start and end apart: 10, of which 4 were waited for; matrix products, arithmetic and copies ran while one was open for 0% of the time, Pallas kernels for 31%

profile of v3, /device:TPU:0, one launch (start us, length us, event | category | flops | bytes accessed | tf_op | source)
XLA Modules:
  0.0 39.2 jit_solution(12900666255204620774)
XLA Ops:
  0.6 0.5 %collective-permute-start.3 = (f32[2,32,4096]{2,1,0:T(8,128)}, f32[2,32,4096]{2,1,0:T(8,128)S(1)}, u32[]{:S(2)}, u32[]{:S(2)}) collective-permute-start(f32[2,32,4096]{2,1,0:T(8,128)} %species.7), channel_id=1, source_target_pairs={{0,1},{1,0},{2,3},{3,2},{4,5},{5,4},{6,7},{7,6},{8,9},{9,8},{10,11... | collective-permute-start | bytes 3145736 | tf_op jit(solution)/shard_map/ppermute | solution.py:700
  1.2 2.8 %pack_meta.1 = (f32[96,128]{1,0:T(8,128)S(1)}, f32[32,512]{1,0:T(8,128)S(1)}, f32[2,64,128]{2,1,0:T(8,128)S(1)}, f32[2,64,512]{2,1,0:T(8,128)S(1)}, f32[2,64,512]{2,1,0:T(8,128)S(1)}, /*index=5*/s32[8,256]{1,0:T(8,128)S(1)}) custom-call(f32[2,32,4096]{2,1,0:T(8,128)} %species.7, f32[1,2]{1,0:T(1,128)} %bitcast.4, s32[1,64]{1,0:T(1,128)} %low_partner.1, ...), custom_call_target="tpu_custom_call" | custom-call | bytes 10240000 | tf_op jit(solution)/shard_map/pack_meta/pallas_call | solution.py:658
  4.0 2.7 %collective-permute-start.2 = (f32[96,128]{1,0:T(8,128)S(1)}, f32[96,128]{1,0:T(8,128)S(1)}, u32[]{:S(2)}, u32[]{:S(2)}) collective-permute-start(f32[96,128]{1,0:T(8,128)S(1)} %get-tuple-element.19.z_half.m0), channel_id=1, source_target_pairs={{0,3},{1,2},{2,1},{3,0},{4,7},{5,6},{6,5},{7,4},{8,11},{9,10},{10,... | collective-permute-start | bytes 147464 | tf_op jit(solution)/shard_map/ppermute | solution.py:700
  6.7 0.0 collective-permute-start.1
  6.7 0.2 collective-permute-start
  6.8 0.3 collective-permute-start.4
  7.2 2.8 %pack_rows.1 = (f32[8,88,128]{2,1,0:T(8,128)S(1)}, f32[16,512]{1,0:T(8,128)S(1)}) custom-call(f32[3,32,4096]{2,1,0:T(8,128)} %flow.5, f32[3,32,4096]{2,1,0:T(8,128)} %diff.3, f32[256,128]{1,0:T(8,128)} %table.3, f32[32,512]{1,0:T(8,128)S(1)} %get-tuple-element.14.strips_ref, f32[2,64,128]{2,1,0:T(8,128)S(1)} %get-tuple-element.15.strip_ref, ...), custom_call_target="tpu_custom_call" | custom-call | bytes 10240000 | tf_op jit(solution)/shard_map/pack_rows/pallas_call | solution.py:658
  10.0 0.0 collective-permute-done.4.d_other
  10.0 0.0 collective-permute-done.2.after2.m3
  10.0 0.7 %collective-permute-done.1.after1.m2 = f32[96,128]{1,0:T(8,128)S(1)} collective-permute-done((f32[96,128]{1,0:T(8,128)S(1)}, f32[96,128]{1,0:T(8,128)S(1)}, u32[]{:S(2)}, u32[]{:S(2)}) %collective-permute-start.1) | collective-permute-done | bytes 49184 | tf_op jit(solution)/shard_map/ppermute | solution.py:700
  10.8 1.3 %chip_sum.1 = (f32[16,4096]{1,0:T(8,128)S(1)}, f32[16,4096]{1,0:T(8,128)S(1)}) custom-call(f32[2,32,4096]{2,1,0:T(8,128)} %species.7, f32[2,32,4096]{2,1,0:T(8,128)S(1)} %collective-permute-done.3.other_ref, f32[1,2]{1,0:T(1,128)} %bitcast.6, f32[1,2]{1,0:T(1,128)S(1)} %collective-permute-done.4.d_other, f32[96,128]{1,0:T(8,128)S(1)} %collective-permute-done.after0.m1, ...), custom_call_target="tpu_custom_call" | custom-call | bytes 4792320 | tf_op jit(solution)/shard_map/chip_sum/pallas_call | solution.py:658
  12.1 1.4 %collective-permute-start.6 = (f32[16,4096]{1,0:T(8,128)S(1)}, f32[16,4096]{1,0:T(8,128)S(1)}, u32[]{:S(2)}, u32[]{:S(2)}) collective-permute-start(f32[16,4096]{1,0:T(8,128)S(1)} %get-tuple-element.22.z_half.near_ref), channel_id=1, source_target_pairs={{0,2},{1,3},{2,0},{3,1},{4,6},{5,7},{6,4},{7,5},{8,10},{9,11},{10,... | collective-permute-start | bytes 786440 | tf_op jit(solution)/shard_map/ppermute | solution.py:700
  13.5 0.8 %assemble.1 = f32[8,88,128]{2,1,0:T(8,128)} custom-call(f32[8,88,128]{2,1,0:T(8,128)S(1)} %get-tuple-element.20.buf_ref, f32[96,128]{1,0:T(8,128)S(1)} %get-tuple-element.19.z_half.m0, f32[96,128]{1,0:T(8,128)S(1)} %collective-permute-done.after0.m1, f32[96,128]{1,0:T(8,128)S(1)} %collective-permute-done.1.after1.m2, ...), custom_call_target="tpu_custom_call" | custom-call | bytes 2949120 | tf_op jit(solution)/shard_map/assemble/pallas_call | solution.py:658
  14.3 5.8 %all-to-all-start = ((f32[8,88,128]{2,1,0:T(8,128)}), f32[8,88,128]{2,1,0:T(8,128)S(1)}, u32[]{:S(2)}, u32[]{:S(2)}) async-start(f32[8,88,128]{2,1,0:T(8,128)} %assemble.1), calls=%async_computation | async-start | bytes 720896 | tf_op jit(solution)/shard_map/all_to_all | solution.py:788
  20.1 0.1 collective-permute-start.7
  20.2 1.6 %collective-permute-start.5 = (f32[16,4096]{1,0:T(8,128)S(1)}, f32[16,4096]{1,0:T(8,128)S(1)}, u32[]{:S(2)}, u32[]{:S(2)}) collective-permute-start(f32[16,4096]{1,0:T(8,128)S(1)} %get-tuple-element.23.near_ref), channel_id=1, source_target_pairs={{0,2},{1,3},{2,0},{3,1},{4,6},{5,7},{6,4},{7,5},{8,10},{9,11},{10,... | collective-permute-start | bytes 786440 | tf_op jit(solution)/shard_map/ppermute | solution.py:700
  21.9 0.0 collective-permute-done.7.zb_ref
  21.9 5.5 %inner_flux.1 = (f32[2,32,4096]{2,1,0:T(8,128)S(1)}, f32[32,512]{1,0:T(8,128)S(1)}) custom-call(f32[3,32,4096]{2,1,0:T(8,128)} %flow.5, f32[3,32,4096]{2,1,0:T(8,128)} %diff.3, f32[32,4096]{1,0:T(8,128)} %vol.3, f32[2,32,4096]{2,1,0:T(8,128)} %species.7, f32[16,4096]{1,0:T(8,128)S(1)} %z_own.1.za_ref, f32[16,4096]{1,0:T(8,128)S(1)} %collective-permute-done.7.zb_ref, ...), custom_call_target="tpu_custom_call" | custom-call | bytes 25804800 | tf_op jit(solution)/shard_map/inner_flux/pallas_call | solution.py:658
  27.3 1.6 %collective-permute-done.5.far_ref = f32[16,4096]{1,0:T(8,128)S(1)} collective-permute-done((f32[16,4096]{1,0:T(8,128)S(1)}, f32[16,4096]{1,0:T(8,128)S(1)}, u32[]{:S(2)}, u32[]{:S(2)}) %collective-permute-start.5) | collective-permute-done | bytes 262176 | tf_op jit(solution)/shard_map/ppermute | solution.py:700
  29.0 0.1 collective-permute-start.8
  29.1 1.5 %collective-permute-done.8.other_ref = f32[16,4096]{1,0:T(8,128)S(1)} collective-permute-done((f32[16,4096]{1,0:T(8,128)S(1)}, f32[16,4096]{1,0:T(8,128)S(1)}, u32[]{:S(2)}, u32[]{:S(2)}) %collective-permute-start.8) | collective-permute-done | bytes 262176 | tf_op jit(solution)/shard_map/ppermute | solution.py:700
  30.6 0.2 fuel_parts.1.fuel_ref
  30.8 0.2 all-to-all-done.got_ref
  31.0 8.2 %final.1 = (f32[2,32,4096]{2,1,0:T(8,128)}, f32[384,128]{1,0:T(8,128)}) custom-call(f32[8,88,128]{2,1,0:T(8,128)S(1)} %all-to-all-done.got_ref, bf16[256,1024]{1,0:T(8,128)(2,1)S(1)} %fuel_parts.1.fuel_ref, f32[2,32,4096]{2,1,0:T(8,128)S(1)} %get-tuple-element.25.base_ref, f32[2,32,4096]{2,1,0:T(8,128)} %species.7, f32[32,4096]{1,0:T(8,128)} %vol.3, ...), custom_call_target="tpu_custom_call" | custom-call | bytes 33177600 | tf_op jit(solution)/shard_map/final/pallas_call | solution.py:658
  (5 shorter events, 0.1 us)
Async XLA Ops:
  0.6 10.1 %collective-permute-start.3 = (f32[2,32,4096]{2,1,0:T(8,128)}, f32[2,32,4096]{2,1,0:T(8,128)S(1)}, u32[]{:S(2)}, u32[]{:S(2)}) collective-permute-start(f32[2,32,4096]{2,1,0:T(8,128)} %species.7), channel_id=1, source_target_pairs={{0,1},{1,0},{2,3},{3,2},{4,5},{5,4},{6,7},{7,6},{8,9},{9,8},{10,11... | collective-permute-start | bytes 3145736 | tf_op jit(solution)/shard_map/ppermute | solution.py:700
  4.0 6.1 %collective-permute-start.2 = (f32[96,128]{1,0:T(8,128)S(1)}, f32[96,128]{1,0:T(8,128)S(1)}, u32[]{:S(2)}, u32[]{:S(2)}) collective-permute-start(f32[96,128]{1,0:T(8,128)S(1)} %get-tuple-element.19.z_half.m0), channel_id=1, source_target_pairs={{0,3},{1,2},{2,1},{3,0},{4,7},{5,6},{6,5},{7,4},{8,11},{9,10},{10,... | collective-permute-start | bytes 147464 | tf_op jit(solution)/shard_map/ppermute | solution.py:700
  6.7 4.1 %collective-permute-start.1 = (f32[96,128]{1,0:T(8,128)S(1)}, f32[96,128]{1,0:T(8,128)S(1)}, u32[]{:S(2)}, u32[]{:S(2)}) collective-permute-start(f32[96,128]{1,0:T(8,128)S(1)} %get-tuple-element.19.z_half.m0), channel_id=1, source_target_pairs={{0,2},{1,3},{2,0},{3,1},{4,6},{5,7},{6,4},{7,5},{8,10},{9,11},{10,... | collective-permute-start | bytes 147464 | tf_op jit(solution)/shard_map/ppermute | solution.py:700
  6.7 4.1 %collective-permute-start = (f32[96,128]{1,0:T(8,128)S(1)}, f32[96,128]{1,0:T(8,128)S(1)}, u32[]{:S(2)}, u32[]{:S(2)}) collective-permute-start(f32[96,128]{1,0:T(8,128)S(1)} %get-tuple-element.19.z_half.m0), channel_id=1, source_target_pairs={{0,1},{1,0},{2,3},{3,2},{4,5},{5,4},{6,7},{7,6},{8,9},{9,8},{10,11... | collective-permute-start | bytes 147464 | tf_op jit(solution)/shard_map/ppermute | solution.py:700
  6.8 3.2 %collective-permute-start.4 = (f32[1,2]{1,0:T(1,128)}, f32[1,2]{1,0:T(1,128)S(1)}, u32[]{:S(2)}, u32[]{:S(2)}) collective-permute-start(f32[1,2]{1,0:T(1,128)} %bitcast.5), channel_id=1, source_target_pairs={{0,1},{1,0},{2,3},{3,2},{4,5},{5,4},{6,7},{7,6},{8,9},{9,8},{10,11... | collective-permute-start | bytes 32 | tf_op jit(solution)/shard_map/ppermute | solution.py:700
  12.1 8.0 %collective-permute-start.6 = (f32[16,4096]{1,0:T(8,128)S(1)}, f32[16,4096]{1,0:T(8,128)S(1)}, u32[]{:S(2)}, u32[]{:S(2)}) collective-permute-start(f32[16,4096]{1,0:T(8,128)S(1)} %get-tuple-element.22.z_half.near_ref), channel_id=1, source_target_pairs={{0,2},{1,3},{2,0},{3,1},{4,6},{5,7},{6,4},{7,5},{8,10},{9,11},{10,... | collective-permute-start | bytes 786440 | tf_op jit(solution)/shard_map/ppermute | solution.py:700
  14.3 16.7 %all-to-all-start = ((f32[8,88,128]{2,1,0:T(8,128)}), f32[8,88,128]{2,1,0:T(8,128)S(1)}, u32[]{:S(2)}, u32[]{:S(2)}) async-start(f32[8,88,128]{2,1,0:T(8,128)} %assemble.1), calls=%async_computation | async-start | bytes 720896 | tf_op jit(solution)/shard_map/all_to_all | solution.py:788
  20.1 1.7 %collective-permute-start.7 = (f32[16,4096]{1,0:T(8,128)S(1)}, f32[16,4096]{1,0:T(8,128)S(1)}, u32[]{:S(2)}, u32[]{:S(2)}) collective-permute-start(f32[16,4096]{1,0:T(8,128)S(1)} %z_own.1.za_ref), channel_id=1, source_target_pairs={{0,1},{1,0},{2,3},{3,2},{4,5},{5,4},{6,7},{7,6},{8,9},{9,8},{10,11... | collective-permute-start | bytes 786440 | tf_op jit(solution)/shard_map/ppermute | solution.py:700
  20.2 8.7 %collective-permute-start.5 = (f32[16,4096]{1,0:T(8,128)S(1)}, f32[16,4096]{1,0:T(8,128)S(1)}, u32[]{:S(2)}, u32[]{:S(2)}) collective-permute-start(f32[16,4096]{1,0:T(8,128)S(1)} %get-tuple-element.23.near_ref), channel_id=1, source_target_pairs={{0,2},{1,3},{2,0},{3,1},{4,6},{5,7},{6,4},{7,5},{8,10},{9,11},{10,... | collective-permute-start | bytes 786440 | tf_op jit(solution)/shard_map/ppermute | solution.py:700
  29.0 1.6 %collective-permute-start.8 = (f32[16,4096]{1,0:T(8,128)S(1)}, f32[16,4096]{1,0:T(8,128)S(1)}, u32[]{:S(2)}, u32[]{:S(2)}) collective-permute-start(f32[16,4096]{1,0:T(8,128)S(1)} %fuel_half.1.own_ref), channel_id=1, source_target_pairs={{0,1},{1,0},{2,3},{3,2},{4,5},{5,4},{6,7},{7,6},{8,9},{9,8},{10,11... | collective-permute-start | bytes 786440 | tf_op jit(solution)/shard_map/ppermute | solution.py:700

commit v4 on v3

--- a/solution.py
+++ b/solution.py
@@ -131,17 +131,21 @@
     block,
     cell,
     live,
+    flow,
+    diff,
     m_ref,
     strips_ref,
     strip_ref,
     column_ref,
     code_ref,
     slot_ref,
+    table_in,
+    vel_in,
+    dif_in,
     bottom,
     top,
     d_own,
     small,
-    table_in,
     parcel,
     sems,
 ):
@@ -151,7 +155,8 @@
         + [(high_orient, small.at[2]), (low_orient, small.at[3])]
         + [(block, parcel.at[0]), (live, parcel.at[1]), (cell, parcel.at[2])]
         + [(table, table_in), (diffusivity, d_own)]
-        + [(species.at[:, layers - 8 :], top), (species.at[:, 0:8], bottom)],
+        + [(species.at[:, layers - 8 :], top), (species.at[:, 0:8], bottom)]
+        + [(flow.at[0, 0:8], vel_in), (diff.at[0, 0:8], dif_in)],
         sems,
     )
     me = lax.axis_index("blk")
@@ -211,15 +216,17 @@
         tiles += take_tiles([face], strip, column_ref[k], code_ref[k], inside)
     high, low = turn_tiles(tiles, turn)
     m_ref[4 * blocks : 4 * blocks + TILES, :] = jnp.where(lanes < 64, high, low)
+    copies[11].wait()
+    copies[12].wait()
 
 
 def pack_rows_kernel(
     blocks,
     tile_cap,
     parcel_cap,
-    flow,
-    diff,
-    table,
+    table_in,
+    vel_in,
+    dif_in,
     strips_ref,
     strip_ref,
     column_ref,
@@ -228,18 +235,9 @@
     z_half,
     out_ref,
     edge_ref,
-    vel_in,
-    dif_in,
-    table_in,
-    sems,
 ):
-    copies = begin(
-        [(flow.at[0, 0:8], vel_in), (diff.at[0, 0:8], dif_in), (table, table_in)], sems
-    )
     inside, turn = inside_table(), orient_table()
     faces = [strips_ref[8 * i : 8 * i + 8, :] for i in range(4)]
-    copies[0].wait()
-    copies[1].wait()
     vel, dif = to_strips(vel_in[0:1, :]), to_strips(dif_in[0:1, :])
     edge_ref[...] = jnp.concatenate([vel, dif], axis=0)
     tiles = []
@@ -253,8 +251,7 @@
         jnp.where(left, pltpu.roll(low0, 64, 1), low1),
         jnp.where(left, pltpu.roll(vel, 64, 1), dif),
     ]
-    copies[2].wait()
-    rows = table.shape[0]
+    rows = table_in.shape[0]
     send = ones(iota((blocks * parcel_cap, rows), 0) == slot_ref[0:1, :])
     parts = split(table_in[...], 3)
     sent = mm(send, parts[2]) + mm(send, parts[1]) + mm(send, parts[0])
@@ -263,6 +260,10 @@
         for k in range(PAIRS - 1):
             at = parcel_cap + k * tile_cap
             out_ref[b, at : at + tile_cap, :] = pairs[k][b * tile_cap : (b + 1) * tile_cap]
+
+
+def pass_kernel(*refs):
+    pass
 
 
 def add_kernel(near_ref, far_ref, out_ref):
@@ -286,25 +287,20 @@
 
 
 def sum_kernel(
-    species, other_ref, factors, d_other, after0, after1, after2, after3, zh_ref, fh_ref, own_ref, d_own, sems
+    own_ref, other_ref, factors, d_other, after0, after1, zh_ref, fh_ref, d_own, sem
 ):
     half, cells = zh_ref.shape
-    quarter = cells // 4
-    parts = [slice(i * quarter, (i + 1) * quarter) for i in range(4)]
-    copies = begin(
-        [(factors, d_own)] + [(species.at[:, :, p], own_ref.at[:, :, p]) for p in parts], sems
-    )
+    copy = pltpu.make_async_copy(factors, d_own, sem)
+    copy.start()
     first = (lax.axis_index("sp") & 1) == 0
-    copies[0].wait()
+    copy.wait()
     d0, d1, e0, e1 = d_own[0:1, 0:1], d_own[0:1, 1:2], d_other[0:1, 0:1], d_other[0:1, 1:2]
-    for copy, p in zip(copies[1:], parts):
-        copy.wait()
-        for lo in range(p.start, p.stop, LANES):
-            at = slice(lo, lo + LANES)
-            own, other = own_ref[0, :, at], other_ref[0, :, at]
-            z = d0 * own + d1 * own_ref[1, :, at] + (e0 * other + e1 * other_ref[1, :, at])
-            zh_ref[:, at] = jnp.where(first, z[0:half], z[half:])
-            fh_ref[:, at] = jnp.where(first, own[0:half], other[half:])
+    for lo in range(0, cells, LANES):
+        at = slice(lo, lo + LANES)
+        own, other = own_ref[0, :, at], other_ref[0, :, at]
+        z = d0 * own + d1 * own_ref[1, :, at] + (e0 * other + e1 * other_ref[1, :, at])
+        zh_ref[:, at] = jnp.where(first, z[0:half], z[half:])
+        fh_ref[:, at] = jnp.where(first, own[0:half], other[half:])
 
 
 def flux(velocity, diffusion, d, upper, lower, weight):
@@ -496,27 +492,52 @@
         lo = ghost + k * tile_cap
         return jnp.concatenate([got_ref[b, lo : lo + tile_cap, :] for b in range(blocks)], axis=0)
 
-    def meta(f):
-        rows = []
-        for h in range(2):
-            for g in range(groups):
-                total = None
-                for i in range(share):
-                    one = got_ref[g * share + i, at + 3 * h + f : at + 3 * h + f + 1, :]
-                    total = one if total is None else total + one
-                rows.append(total)
-        return jnp.concatenate(rows, axis=0)
-
-    chunks = 2 * groups
-    number = meta(0).astype(jnp.int32) - 1
-    soft, sig = meta(1), meta(2)
-    cell_layer = lax.shift_right_arithmetic(number, 12)
-    cell_row = (lax.shift_right_arithmetic(number, 7) & 31) * layers + cell_layer
-    cell_row = jnp.where(number >= 0, cell_row, -1)
-    number_ref[...] = jnp.maximum(cell_row, 0)
+    def meta(f, h, g):
+        total = None
+        for i in range(share):
+            lo = at + 3 * h + f
+            one = got_ref[g * share + i, lo : lo + 1, :]
+            total = one if total is None else total + one
+        return total
+
+    quad = groups // 2
+    order = [(h, g) for h in range(2) for g in range(groups)]
+    four = [
+        jnp.concatenate([meta(f, h, g) for f in range(3) for h, g in order[quad * i : quad * i + quad]], axis=0)
+        for i in range(4)
+    ]
+    lane = iota((3 * quad, LANES), 1)
+    a, b, c, d = four
+    b_low, c_high = pltpu.roll(b, 96, 1), pltpu.roll(c, 48, 1)
+    full = [
+        jnp.where(lane < 48, a, jnp.where(lane < 96, pltpu.roll(a, 112, 1), b_low)),
+        jnp.where(
+            lane < 64,
+            jnp.where(lane < 16, b_low, pltpu.roll(b, 80, 1)),
+            jnp.where(lane < 112, pltpu.roll(c, 64, 1), c_high),
+        ),
+        jnp.where(
+            lane < 32, c_high, jnp.where(lane < 80, pltpu.roll(d, 32, 1), pltpu.roll(d, 16, 1))
+        ),
+    ]
+
+    def field(f, arrays):
+        return jnp.concatenate([one[quad * f : quad * f + quad] for one in arrays], axis=0)
+
+    def locate(numbers):
+        number = numbers.astype(jnp.int32) - 1
+        layer = lax.shift_right_arithmetic(number, 12)
+        row = (lax.shift_right_arithmetic(number, 7) & 31) * layers + layer
+        used = number >= 0
+        return jnp.where(used, row, -1), jnp.where(used, number & (LANES - 1), -1)
+
+    chunks = 3 * quad
+    own_row, own_lane = locate(field(0, four[0:2]))
+    number_ref[...] = jnp.maximum(own_row, 0)
     fetch_number = pltpu.make_async_copy(number_ref, number_smem, number_sem)
     fetch_number.start()
-    cell_lane = number & (LANES - 1)
+    cell_row, cell_lane = locate(field(0, full))
+    soft, sig = field(1, full), field(2, full)
     sublane = iota((LANES, LANES), 0)
     tall = iota((tall_rows, LANES), 0)
     for c in range(chunks):
@@ -589,14 +610,11 @@
     for copy in fetch_flow:
         copy.wait()
 
-    def group(g, carry):
+    for g in range(groups):
         for i in range(size):
             where = number_smem[g, 64 * (g & 1) + i]
             for f in range(3):
-                rows_ref[f, pl.ds(64 * g + i, 1), :] = flow_ref[f, pl.ds(where, 1), :]
-        return carry
-
-    lax.fori_loop(0, groups, group, 0)
+                rows_ref[f, 64 * g + i : 64 * g + i + 1, :] = flow_ref[f, pl.ds(where, 1), :]
     index, column = iota((8, PV), 0), iota((8, PV), 1)
     spread = ones(index == 0)
     take = ones((index < 2) & (column == 0))
@@ -604,14 +622,28 @@
     into = ones(column == 3 + lax.div(index, 2 * LANES))
     drag = (iota((size, PV), 1) >= 3) & (iota((size, PV), 1) <= 5)
     keep = jnp.where(drag, 1.0 - friction_timescale, 1.0)
-    lane_of = jnp.where(number >= 0, cell_lane, -1).astype(F32)
+    lane_of = own_lane.astype(F32)
+    gone0 = jnp.concatenate(evaporated[0:quad], axis=0)
+    gone1 = jnp.concatenate(evaporated[quad : 2 * quad], axis=0)
+    lane = iota((quad, LANES), 1)
+    evaporated = jnp.concatenate(
+        [
+            jnp.where(lane < 64, gone0, pltpu.roll(gone0, 16, 1)),
+            jnp.where(
+                lane < 32,
+                pltpu.roll(gone0, 32, 1),
+                jnp.where(lane < 64, pltpu.roll(gone1, 32, 1), pltpu.roll(gone1, 48, 1)),
+            ),
+        ],
+        axis=0,
+    )
     none = jnp.zeros((6, LANES), F32)
     for h in range(groups // 2):
         a, b = 2 * h, 2 * h + 1
         lanes = jnp.where(lefts, lane_of[a : a + 1], lane_of[b : b + 1])
         lanes = jnp.concatenate([lanes, lanes, none], axis=0).astype(BF16)
         mask = mm_tn(lanes, spread) == iota((LANES, PV), 1).astype(F32)
-        gone = jnp.where(lefts, evaporated[a], evaporated[b])
+        gone = jnp.where(lefts, evaporated[a : a + 1], evaporated[b : b + 1])
         head = gone.astype(BF16).astype(F32)
         change = -mm_tn(jnp.concatenate([head, gone - head, none], axis=0).astype(BF16), take)
         fields = []
@@ -663,6 +695,17 @@
         )
 
     return held
+
+
+def after(value, *others):
+    return pl.pallas_call(
+        pass_kernel,
+        out_shape=pltpu.VMEM(value.shape, value.dtype),
+        in_specs=fast(1 + len(others)),
+        out_specs=fast()[0],
+        input_output_aliases={0: 0},
+        name="after",
+    )(*(pltpu.with_memory_space_constraint(a, pltpu.VMEM) for a in (value, *others)))
 
 
 def dma(*count):
@@ -703,7 +746,7 @@
     other_species = swap(species, 1)
     other_factors = swap(factors, 1)
 
-    m0, strips, strip, column, code, slot = call(
+    m0, strips, strip, column, code, slot, table, vel, dif = call(
         functools.partial(pack_meta_kernel, *sizes),
         "pack_meta",
         [
@@ -713,16 +756,18 @@
             ((2, TILES, STRIP), F32),
             ((2, TILES, STRIP), F32),
             ((8, parcels), jnp.int32),
+            (droplet_table.shape, F32),
+            ((8, cells), F32),
+            ((8, cells), F32),
         ],
-        slow(10),
+        slow(12),
         [
             vmem((local_species, 8, cells), F32),
             vmem((local_species, 8, cells), F32),
             vmem((1, local_species), F32),
             vmem((4, 1, TILES), jnp.int32),
-            vmem(droplet_table.shape, F32),
             vmem((3,) + int_row, jnp.int32),
-            dma(11),
+            dma(13),
         ],
         kib=10000,
     )(
@@ -736,6 +781,8 @@
         parcel_block.reshape(int_row),
         parcel_cell.reshape(int_row),
         parcel_live.reshape(int_row),
+        interface_normal_flow,
+        face_diffusion,
     )
     m1, m2, m3 = swap(m0, 1), swap(m0, 2), swap(m0, 3)
 
@@ -744,18 +791,12 @@
         functools.partial(pack_rows_kernel, *sizes),
         "pack_rows",
         [((blocks, rows, LANES), F32), ((16, STRIP), F32)],
-        slow(3) + fast(6),
-        [
-            vmem((8, cells), F32),
-            vmem((8, cells), F32),
-            vmem(droplet_table.shape, F32),
-            dma(3),
-        ],
+        fast(9),
         kib=10000,
     )(
-        interface_normal_flow,
-        face_diffusion,
-        droplet_table,
+        table,
+        vel,
+        dif,
         strips,
         strip,
         column,
@@ -767,10 +808,11 @@
         sum_kernel,
         "chip_sum",
         [((layers // 2, cells), F32), ((layers // 2, cells), F32)],
-        slow(1) + fast(1) + slow(1) + fast(5),
-        [vmem(species.shape, F32), vmem((1, local_species), F32), dma(5)],
+        fast(2) + slow(1) + fast(3),
+        [vmem((1, local_species), F32), pltpu.SemaphoreType.DMA],
         kib=4680,
-    )(species, other_species, factors, other_factors, m1, m2, m3, edge_flow)
+    )(species, other_species, factors, other_factors, m1, edge_flow)
+    z_half = after(z_half, m2, m3)
     z_far = swap(z_half, 2)
     fuel_far = swap(fuel_half, 2)
 
@@ -831,14 +873,14 @@
         [
             vmem(species.shape, F32),
             vmem((blocks * parcel_cap, PV), F32),
-            vmem((tall, 2 * groups * LANES), BF16),
-            vmem((2 * LANES, 2 * groups * LANES), BF16),
+            vmem((tall, 3 * groups // 2 * LANES), BF16),
+            vmem((2 * LANES, 3 * groups // 2 * LANES), BF16),
             vmem((8, cells), F32),
             vmem(species.shape, F32),
             vmem((layers, cells), F32),
             vmem((3, tall, LANES), F32),
-            vmem((2 * groups, LANES), jnp.int32),
-            pltpu.SMEM((2 * groups, LANES), jnp.int32),
+            vmem((groups, LANES), jnp.int32),
+            pltpu.SMEM((groups, LANES), jnp.int32),
             vmem((3, 64 * groups, PV), F32),
             dma(2, 4),
             dma(cells // LANES),

time: 39.4 us -> 36.2 us (0.919)
  Pallas kernels: 21.6 us -> 18.2 us
  waiting for transfers between devices: 4.08 us -> 4.58 us
    pallas_call x9, Pallas kernels: 21.6 us -> 18.2 us  [held(): run(*(pltpu.with_memory_space_constraint(a, spec.memory_space) for a, spe...]
    ppermute x9, waiting for transfers between devices: 3.86 us -> 4.52 us  [swap(): lax.ppermute(value, 'sp', [(i, i ^ bit) for i in range(lax.axis_size('sp'...]
  transfers between devices with their start and end apart: 10 -> 10, of which waited for: 4 -> 4; matrix products, arithmetic and copies ran while one was open for 0% -> 0% of each run, Pallas kernels for 31% -> 33%
where the time goes in v4:
time: 36.2 us; the launch traced here: 36 us
  Pallas kernels  18.2 us (50%)
  starting transfers between devices  12.5 us (35%)
  waiting for transfers between devices  4.58 us (13%)
  between operations  0.76 us (2%)
    pallas_call x9, Pallas kernels, held(): run(*(pltpu.with_memory_space_constraint(a, spec.memory_space) for a, spe...  18.2 us
    ppermute x9, starting transfers between devices, swap(): lax.ppermute(value, 'sp', [(i, i ^ bit) for i in range(lax.axis_size('sp'...  6.64 us
    all_to_all x1, starting transfers between devices, body(): got = lax.all_to_all(ready, 'blk', split_axis=0, concat_axis=0, tiled=True)  5.83 us
    ppermute x9, waiting for transfers between devices, swap(): lax.ppermute(value, 'sp', [(i, i ^ bit) for i in range(lax.axis_size('sp'...  4.52 us
  transfers between devices with their start and end apart: 10, of which 4 were waited for; matrix products, arithmetic and copies ran while one was open for 0% of the time, Pallas kernels for 33%

profile of v4, /device:TPU:0, one launch (start us, length us, event | category | flops | bytes accessed | tf_op | source)
XLA Modules:
  0.0 36.0 jit_solution(17487319702116664536)
XLA Ops:
  0.6 0.5 %collective-permute-start.3 = (f32[2,32,4096]{2,1,0:T(8,128)}, f32[2,32,4096]{2,1,0:T(8,128)S(1)}, u32[]{:S(2)}, u32[]{:S(2)}) collective-permute-start(f32[2,32,4096]{2,1,0:T(8,128)} %species.5), channel_id=1, source_target_pairs={{0,1},{1,0},{2,3},{3,2},{4,5},{5,4},{6,7},{7,6},{8,9},{9,8},{10,11... | collective-permute-start | bytes 3145736 | tf_op jit(solution)/shard_map/ppermute | solution.py:743
  1.2 2.9 %pack_meta.1 = (f32[96,128]{1,0:T(8,128)S(1)}, f32[32,512]{1,0:T(8,128)S(1)}, f32[2,64,128]{2,1,0:T(8,128)S(1)}, f32[2,64,512]{2,1,0:T(8,128)S(1)}, f32[2,64,512...) custom-call(f32[2,32,4096]{2,1,0:T(8,128)} %species.5, ...), custom_call_target="tpu_custom_call" | custom-call | bytes 10240000 | tf_op jit(solution)/shard_map/pack_meta/pallas_call | solution.py:690
  4.0 0.0 copy-start
  4.0 0.1 collective-permute-start
  4.2 2.6 %collective-permute-start.2 = (f32[96,128]{1,0:T(8,128)S(1)}, f32[96,128]{1,0:T(8,128)S(1)}, u32[]{:S(2)}, u32[]{:S(2)}) collective-permute-start(f32[96,128]{1,0:T(8,128)S(1)} %get-tuple-element.25.z_half.m0), channel_id=1, source_target_pairs={{0,3},{1,2},{2,1},{3,0},{4,7},{5,6},{6,5},{7,4},{8,11},{9,10},{10,... | collective-permute-start | bytes 147464 | tf_op jit(solution)/shard_map/ppermute | solution.py:743
  6.8 0.3 collective-permute-start.1
  7.1 0.1 collective-permute-start.4
  7.2 1.4 %pack_rows.1 = (f32[8,88,128]{2,1,0:T(8,128)S(1)}, f32[16,512]{1,0:T(8,128)S(1)}) custom-call(f32[256,128]{1,0:T(8,128)S(1)} %get-tuple-element.17.table_in, f32[8,4096]{1,0:T(8,128)S(1)} %get-tuple-element.18.vel_in, f32[8,4096]{1,0:T(8,128)S(1)} %get-tuple-element.19.dif_in, f32[32,512]{1,0:T(8,128)S(1)} %get-tuple-element.20.strips_ref, ...), custom_call_target="tpu_custom_call" | custom-call | bytes 10240000 | tf_op jit(solution)/shard_map/pack_rows/pallas_call | solution.py:690
  8.7 0.0 collective-permute-done.after0.m1
  8.7 0.9 %chip_sum.1 = (f32[16,4096]{1,0:T(8,128)S(1)}, f32[16,4096]{1,0:T(8,128)S(1)}) custom-call(f32[2,32,4096]{2,1,0:T(8,128)S(1)} %copy-done, f32[2,32,4096]{2,1,0:T(8,128)S(1)} %collective-permute-done.3.other_ref, f32[1,2]{1,0:T(1,128)} %bitcast.5, f32[1,2]{1,0:T(1,128)S(1)} %collective-permute-done.4.d_other, f32[96,128]{1,0:T(8,128)S(1)} %collective-permute-done.after0.m1, ...), custom_call_target="tpu_custom_call" | custom-call | bytes 4792320 | tf_op jit(solution)/shard_map/chip_sum/pallas_call | solution.py:690
  9.7 1.2 %collective-permute-done.1.refs_1_.m2 = f32[96,128]{1,0:T(8,128)S(1)} collective-permute-done((f32[96,128]{1,0:T(8,128)S(1)}, f32[96,128]{1,0:T(8,128)S(1)}, u32[]{:S(2)}, u32[]{:S(2)}) %collective-permute-start.1) | collective-permute-done | bytes 49184 | tf_op jit(solution)/shard_map/ppermute | solution.py:743
  10.9 1.3 %collective-permute-start.6 = (f32[16,4096]{1,0:T(8,128)S(1)}, f32[16,4096]{1,0:T(8,128)S(1)}, u32[]{:S(2)}, u32[]{:S(2)}) collective-permute-start(f32[16,4096]{1,0:T(8,128)S(1)} %after.1.z_half.near_ref), channel_id=1, source_target_pairs={{0,2},{1,3},{2,0},{3,1},{4,6},{5,7},{6,4},{7,5},{8,10},{9,11},{10,... | collective-permute-start | bytes 786440 | tf_op jit(solution)/shard_map/ppermute | solution.py:743
  12.2 0.8 %assemble.1 = f32[8,88,128]{2,1,0:T(8,128)} custom-call(f32[8,88,128]{2,1,0:T(8,128)S(1)} %get-tuple-element.26.buf_ref, f32[96,128]{1,0:T(8,128)S(1)} %get-tuple-element.25.z_half.m0, f32[96,128]{1,0:T(8,128)S(1)} %collective-permute-done.after0.m1, f32[96,128]{1,0:T(8,128)S(1)} %collective-permute-done.1.refs_1_.m2, ...), custom_call_target="tpu_custom_call" | custom-call | bytes 2949120 | tf_op jit(solution)/shard_map/assemble/pallas_call | solution.py:690
  13.0 5.8 %all-to-all-start = ((f32[8,88,128]{2,1,0:T(8,128)}), f32[8,88,128]{2,1,0:T(8,128)S(1)}, u32[]{:S(2)}, u32[]{:S(2)}) async-start(f32[8,88,128]{2,1,0:T(8,128)} %assemble.1), calls=%async_computation | async-start | bytes 720896 | tf_op jit(solution)/shard_map/all_to_all | solution.py:830
  18.9 0.1 collective-permute-start.7
  19.0 1.5 %collective-permute-start.5 = (f32[16,4096]{1,0:T(8,128)S(1)}, f32[16,4096]{1,0:T(8,128)S(1)}, u32[]{:S(2)}, u32[]{:S(2)}) collective-permute-start(f32[16,4096]{1,0:T(8,128)S(1)} %get-tuple-element.29.near_ref), channel_id=1, source_target_pairs={{0,2},{1,3},{2,0},{3,1},{4,6},{5,7},{6,4},{7,5},{8,10},{9,11},{10,... | collective-permute-start | bytes 786440 | tf_op jit(solution)/shard_map/ppermute | solution.py:743
  20.4 0.0 collective-permute-done.7.zb_ref
  20.5 5.5 %inner_flux.1 = (f32[2,32,4096]{2,1,0:T(8,128)S(1)}, f32[32,512]{1,0:T(8,128)S(1)}) custom-call(f32[3,32,4096]{2,1,0:T(8,128)} %flow.5, f32[3,32,4096]{2,1,0:T(8,128)} %diff.3, f32[32,4096]{1,0:T(8,128)} %vol.3, f32[2,32,4096]{2,1,0:T(8,128)} %species.5, f32[16,4096]{1,0:T(8,128)S(1)} %z_own.1.za_ref, f32[16,4096]{1,0:T(8,128)S(1)} %collective-permute-done.7.zb_ref, ...), custom_call_target="tpu_custom_call" | custom-call | bytes 25804800 | tf_op jit(solution)/shard_map/inner_flux/pallas_call | solution.py:690
  25.9 1.7 %collective-permute-done.5.far_ref = f32[16,4096]{1,0:T(8,128)S(1)} collective-permute-done((f32[16,4096]{1,0:T(8,128)S(1)}, f32[16,4096]{1,0:T(8,128)S(1)}, u32[]{:S(2)}, u32[]{:S(2)}) %collective-permute-start.5) | collective-permute-done | bytes 262176 | tf_op jit(solution)/shard_map/ppermute | solution.py:743
  27.7 0.1 collective-permute-start.8
  27.8 1.5 %collective-permute-done.8.other_ref = f32[16,4096]{1,0:T(8,128)S(1)} collective-permute-done((f32[16,4096]{1,0:T(8,128)S(1)}, f32[16,4096]{1,0:T(8,128)S(1)}, u32[]{:S(2)}, u32[]{:S(2)}) %collective-permute-start.8) | collective-permute-done | bytes 262176 | tf_op jit(solution)/shard_map/ppermute | solution.py:743
  29.3 0.2 fuel_parts.1.fuel_ref
  29.5 0.1 all-to-all-done.got_ref
  29.6 6.4 %final.1 = (f32[2,32,4096]{2,1,0:T(8,128)}, f32[384,128]{1,0:T(8,128)}) custom-call(f32[8,88,128]{2,1,0:T(8,128)S(1)} %all-to-all-done.got_ref, bf16[256,1024]{1,0:T(8,128)(2,1)S(1)} %fuel_parts.1.fuel_ref, f32[2,32,4096]{2,1,0:T(8,128)S(1)} %get-tuple-element.31.base_ref, f32[2,32,4096]{2,1,0:T(8,128)} %species.5, f32[32,4096]{1,0:T(8,128)} %vol.3, ...), custom_call_target="tpu_custom_call" | custom-call | bytes 33177600 | tf_op jit(solution)/shard_map/final/pallas_call | solution.py:690
  (10 shorter events, 0.1 us)
Async XLA Ops:
  0.6 8.1 %collective-permute-start.3 = (f32[2,32,4096]{2,1,0:T(8,128)}, f32[2,32,4096]{2,1,0:T(8,128)S(1)}, u32[]{:S(2)}, u32[]{:S(2)}) collective-permute-start(f32[2,32,4096]{2,1,0:T(8,128)} %species.5), channel_id=1, source_target_pairs={{0,1},{1,0},{2,3},{3,2},{4,5},{5,4},{6,7},{7,6},{8,9},{9,8},{10,11... | collective-permute-start | bytes 3145736 | tf_op jit(solution)/shard_map/ppermute | solution.py:743
  1.2 6.0 %copy-start.1 = (f32[2]{0:T(128)S(1)}, f32[2]{0:T(128)}, u32[]{:S(2)}) copy-start(f32[2]{0:T(128)} %param.17) | copy-start | bytes 28
  4.0 4.7 %copy-start = (f32[2,32,4096]{2,1,0:T(8,128)S(1)}, f32[2,32,4096]{2,1,0:T(8,128)}, u32[]{:S(2)}) copy-start(f32[2,32,4096]{2,1,0:T(8,128)} %species.5) | copy-start | bytes 3145732
  4.0 4.7 %collective-permute-start = (f32[96,128]{1,0:T(8,128)S(1)}, f32[96,128]{1,0:T(8,128)S(1)}, u32[]{:S(2)}, u32[]{:S(2)}) collective-permute-start(f32[96,128]{1,0:T(8,128)S(1)} %get-tuple-element.25.z_half.m0), channel_id=1, source_target_pairs={{0,1},{1,0},{2,3},{3,2},{4,5},{5,4},{6,7},{7,6},{8,9},{9,8},{10,11... | collective-permute-start | bytes 147464 | tf_op jit(solution)/shard_map/ppermute | solution.py:743
  4.2 5.5 %collective-permute-start.2 = (f32[96,128]{1,0:T(8,128)S(1)}, f32[96,128]{1,0:T(8,128)S(1)}, u32[]{:S(2)}, u32[]{:S(2)}) collective-permute-start(f32[96,128]{1,0:T(8,128)S(1)} %get-tuple-element.25.z_half.m0), channel_id=1, source_target_pairs={{0,3},{1,2},{2,1},{3,0},{4,7},{5,6},{6,5},{7,4},{8,11},{9,10},{10,... | collective-permute-start | bytes 147464 | tf_op jit(solution)/shard_map/ppermute | solution.py:743
  6.8 4.1 %collective-permute-start.1 = (f32[96,128]{1,0:T(8,128)S(1)}, f32[96,128]{1,0:T(8,128)S(1)}, u32[]{:S(2)}, u32[]{:S(2)}) collective-permute-start(f32[96,128]{1,0:T(8,128)S(1)} %get-tuple-element.25.z_half.m0), channel_id=1, source_target_pairs={{0,2},{1,3},{2,0},{3,1},{4,6},{5,7},{6,4},{7,5},{8,10},{9,11},{10,... | collective-permute-start | bytes 147464 | tf_op jit(solution)/shard_map/ppermute | solution.py:743
  7.1 1.5 %collective-permute-start.4 = (f32[1,2]{1,0:T(1,128)S(1)}, f32[1,2]{1,0:T(1,128)S(1)}, u32[]{:S(2)}, u32[]{:S(2)}) collective-permute-start(f32[1,2]{1,0:T(1,128)S(1)} %bitcast.6), channel_id=1, source_target_pairs={{0,1},{1,0},{2,3},{3,2},{4,5},{5,4},{6,7},{7,6},{8,9},{9,8},{10,11... | collective-permute-start | bytes 32 | tf_op jit(solution)/shard_map/ppermute | solution.py:743
  10.9 8.0 %collective-permute-start.6 = (f32[16,4096]{1,0:T(8,128)S(1)}, f32[16,4096]{1,0:T(8,128)S(1)}, u32[]{:S(2)}, u32[]{:S(2)}) collective-permute-start(f32[16,4096]{1,0:T(8,128)S(1)} %after.1.z_half.near_ref), channel_id=1, source_target_pairs={{0,2},{1,3},{2,0},{3,1},{4,6},{5,7},{6,4},{7,5},{8,10},{9,11},{10,... | collective-permute-start | bytes 786440 | tf_op jit(solution)/shard_map/ppermute | solution.py:743
  13.0 16.6 %all-to-all-start = ((f32[8,88,128]{2,1,0:T(8,128)}), f32[8,88,128]{2,1,0:T(8,128)S(1)}, u32[]{:S(2)}, u32[]{:S(2)}) async-start(f32[8,88,128]{2,1,0:T(8,128)} %assemble.1), calls=%async_computation | async-start | bytes 720896 | tf_op jit(solution)/shard_map/all_to_all | solution.py:830
  18.9 1.6 %collective-permute-start.7 = (f32[16,4096]{1,0:T(8,128)S(1)}, f32[16,4096]{1,0:T(8,128)S(1)}, u32[]{:S(2)}, u32[]{:S(2)}) collective-permute-start(f32[16,4096]{1,0:T(8,128)S(1)} %z_own.1.za_ref), channel_id=1, source_target_pairs={{0,1},{1,0},{2,3},{3,2},{4,5},{5,4},{6,7},{7,6},{8,9},{9,8},{10,11... | collective-permute-start | bytes 786440 | tf_op jit(solution)/shard_map/ppermute | solution.py:743
  19.0 8.7 %collective-permute-start.5 = (f32[16,4096]{1,0:T(8,128)S(1)}, f32[16,4096]{1,0:T(8,128)S(1)}, u32[]{:S(2)}, u32[]{:S(2)}) collective-permute-start(f32[16,4096]{1,0:T(8,128)S(1)} %get-tuple-element.29.near_ref), channel_id=1, source_target_pairs={{0,2},{1,3},{2,0},{3,1},{4,6},{5,7},{6,4},{7,5},{8,10},{9,11},{10,... | collective-permute-start | bytes 786440 | tf_op jit(solution)/shard_map/ppermute | solution.py:743
  27.7 1.6 %collective-permute-start.8 = (f32[16,4096]{1,0:T(8,128)S(1)}, f32[16,4096]{1,0:T(8,128)S(1)}, u32[]{:S(2)}, u32[]{:S(2)}) collective-permute-start(f32[16,4096]{1,0:T(8,128)S(1)} %fuel_half.1.own_ref), channel_id=1, source_target_pairs={{0,1},{1,0},{2,3},{3,2},{4,5},{5,4},{6,7},{7,6},{8,9},{9,8},{10,11... | collective-permute-start | bytes 786440 | tf_op jit(solution)/shard_map/ppermute | solution.py:743

commit v5 on v4

--- a/solution.py
+++ b/solution.py
@@ -90,7 +90,7 @@
 
 
 def take_tiles(faces, strip, column, code, inside):
-    parts = [part for face in faces for part in split(face, 3)]
+    parts = [part for face in faces for part in split(face, 2)]
     wide = mm(strip, jnp.concatenate(parts, axis=1))
     tall = jnp.concatenate(
         [(wide[:, i * STRIP : (i + 1) * STRIP] * column).astype(BF16) for i in range(len(parts))],
@@ -107,7 +107,7 @@
 def turn_tiles(tiles, table):
     turned = mm(jnp.concatenate(tiles, axis=0), table)
     turned = [turned[i * TILES : (i + 1) * TILES] for i in range(len(tiles))]
-    return [turned[i + 2] + turned[i + 1] + turned[i] for i in range(0, len(tiles), 3)]
+    return [turned[i + 1] + turned[i] for i in range(0, len(tiles), 2)]
 
 
 def begin(copies, sems):
@@ -115,6 +115,10 @@
     for one in started:
         one.start()
     return started
+
+
+def z_row(blocks):
+    return (3 * blocks // 2) // 8 * 8 + 8
 
 
 def pack_meta_kernel(
@@ -134,6 +138,7 @@
     flow,
     diff,
     m_ref,
+    factor_ref,
     strips_ref,
     strip_ref,
     column_ref,
@@ -193,18 +198,20 @@
         [(parcel[2] + 1).astype(F32), soft, sig, jnp.zeros((5, rows), F32)], axis=0
     )
     share = 48 // parcel_cap
-    lane = rank + lax.rem(me, share) * parcel_cap + 64 * (lax.div(me, share) & 1)
-    goal = jnp.where(alive, target * LANES + lane, -1)
-    spots = ones(iota((blocks * LANES, rows), 0) == goal)
+    lane = rank + lax.rem(me, share) * parcel_cap
+    goal = jnp.where(alive, target * 64 + lane, -1)
+    spots = ones(iota((blocks * 64, rows), 0) == goal)
     meta = mm_nt(jnp.concatenate(split(fields, 3), axis=0), spots)
     meta = meta[16:24] + meta[8:16] + meta[0:8]
     copies[8].wait()
     d0, d1 = d_own[0:1, 0:1], d_own[0:1, 1:2]
     lanes = iota((1, LANES), 1)
     own = jnp.where(lanes == 0, d0, jnp.where(lanes == 1, d1, 0.0))
-    for b in range(blocks):
-        m_ref[4 * b : 4 * b + 3, :] = meta[0:3, b * LANES : (b + 1) * LANES]
-        m_ref[4 * b + 3 : 4 * b + 4, :] = own
+    for k in range(blocks // 2):
+        m_ref[3 * k : 3 * k + 3, :] = meta[0:3, k * LANES : (k + 1) * LANES]
+    factor_ref[...] = jnp.broadcast_to(own, (8, LANES))
+    z_at = z_row(blocks)
+    m_ref[3 * blocks // 2 : z_at, :] = jnp.broadcast_to(own, (z_at - 3 * blocks // 2, LANES))
     copies[9].wait()
     copies[10].wait()
     top0, top1 = to_strips(top[0, 7:8, :]), to_strips(top[1, 7:8, :])
@@ -215,7 +222,7 @@
         strip = strip_ref[k][:, 0:8].astype(BF16)
         tiles += take_tiles([face], strip, column_ref[k], code_ref[k], inside)
     high, low = turn_tiles(tiles, turn)
-    m_ref[4 * blocks : 4 * blocks + TILES, :] = jnp.where(lanes < 64, high, low)
+    m_ref[z_at : z_at + TILES, :] = jnp.where(lanes < 64, high, low)
     copies[11].wait()
     copies[12].wait()
 
@@ -272,16 +279,27 @@
 
 def assemble_kernel(blocks, tile_cap, parcel_cap, buf_ref, m0, m1, m2, m3, z_half, out_ref):
     ghost = parcel_cap + (PAIRS - 1) * tile_cap
-    z = slice(4 * blocks, 4 * blocks + TILES)
+    z = slice(z_row(blocks), z_row(blocks) + TILES)
     total = (m0[z, :] + m1[z, :]) + (m2[z, :] + m3[z, :])
-    near = m0[0 : 4 * blocks, :] + pltpu.roll(m1[0 : 4 * blocks, :], 64, 1)
-    far = m2[0 : 4 * blocks, :] + pltpu.roll(m3[0 : 4 * blocks, :], 64, 1)
+    used = 3 * blocks // 2
+    right = lax.div(lax.axis_index("blk"), 48 // parcel_cap) & 1
+    here = (iota((used, LANES), 1) >> 6) == right
+    near, far = [], []
+    for out, a, b in ((near, m0, m1), (far, m2, m3)):
+        a, b = a[0:used, :], b[0:used, :]
+        a_turned, b_turned = pltpu.roll(a, 64, 1), pltpu.roll(b, 64, 1)
+        for half in range(2):
+            same = right == half
+            out.append(
+                jnp.where(here, jnp.where(same, a, a_turned), jnp.where(same, b_turned, b))
+            )
     for b in range(blocks):
         out_ref[b, 0:ghost, :] = buf_ref[b, 0:ghost, :]
         out_ref[b, ghost : ghost + tile_cap, :] = total[b * tile_cap : (b + 1) * tile_cap]
         at = ghost + tile_cap
-        out_ref[b, at : at + 3, :] = near[4 * b : 4 * b + 3]
-        out_ref[b, at + 3 : at + 6, :] = far[4 * b : 4 * b + 3]
+        row = b // 2 * 3
+        out_ref[b, at : at + 3, :] = near[b % 2][row : row + 3]
+        out_ref[b, at + 3 : at + 6, :] = far[b % 2][row : row + 3]
         if at + 6 < out_ref.shape[1]:
             out_ref[b, at + 6 :, :] = jnp.zeros((out_ref.shape[1] - at - 6, LANES), F32)
 
@@ -355,7 +373,7 @@
     left = lane < 64
     inner = row > 0
     off_wall = (lane & 63) != 0
-    ds = (m0[3:4, 0:1], m0[3:4, 1:2])
+    ds = (m0[0:1, 0:1], m0[0:1, 1:2])
     above = [jnp.zeros(shape, F32)] * 2
     for j in range(cells // LANES - 1, -1, -1):
         here = slice(j * LANES, (j + 1) * LANES)
@@ -430,14 +448,14 @@
     parts = []
     for pair, right in pairs:
         one = jnp.where((lane >= 64) if right else (lane < 64), pair, 0.0)
-        parts += split(one, 3)
+        parts += split(one, 2)
     wide = mm_nt(jnp.concatenate(parts, axis=0), inside)
     wide = [
         (wide[i * TILES : (i + 1) * TILES] * column).astype(BF16) for i in range(len(parts))
     ]
     wide = mm_tn(strip, jnp.concatenate(wide, axis=1))
     wide = [wide[:, i * STRIP : (i + 1) * STRIP] for i in range(len(parts))]
-    return [wide[3 * i + 2] + wide[3 * i + 1] + wide[3 * i] for i in range(len(pairs))]
+    return [wide[2 * i + 1] + wide[2 * i] for i in range(len(pairs))]
 
 
 def final_kernel(
@@ -557,7 +575,7 @@
     bottom_scale, top_scale = section_step * zedge_ref[16:24, :], section_step * zedge_ref[24:32, :]
     bottom_v, bottom_d = fedge_ref[0:8, :], fedge_ref[8:16, :]
     for s, (below, above) in enumerate(((below0, above0), (below1, above1))):
-        d = m0[3:4, s : s + 1]
+        d = m0[0:1, s : s + 1]
         high = strips_ref[8 * s : 8 * s + 8, :]
         low = strips_ref[16 + 8 * s : 24 + 8 * s, :]
         f_low = flux(bottom_v, bottom_d, d, low, below, z_bottom - below_z)
@@ -746,11 +764,12 @@
     other_species = swap(species, 1)
     other_factors = swap(factors, 1)
 
-    m0, strips, strip, column, code, slot, table, vel, dif = call(
+    m0, own_factors, strips, strip, column, code, slot, table, vel, dif = call(
         functools.partial(pack_meta_kernel, *sizes),
         "pack_meta",
         [
-            ((4 * blocks + TILES, LANES), F32),
+            ((z_row(blocks) + TILES, LANES), F32),
+            ((8, LANES), F32),
             ((32, STRIP), F32),
             ((2, TILES, LANES), F32),
             ((2, TILES, STRIP), F32),
@@ -850,7 +869,7 @@
         species,
         z_own,
         z_other,
-        m0,
+        own_factors,
     )
 
     (fuel_own,) = call(
@@ -900,7 +919,7 @@
         strips,
         strip,
         column,
-        m0,
+        own_factors,
     )
 
 

time: 36.2 us -> 35.6 us (0.983)
  Pallas kernels: 18.2 us -> 17.4 us
    pallas_call x9, Pallas kernels: 18.2 us -> 17.4 us  [held(): run(*(pltpu.with_memory_space_constraint(a, spec.memory_space) for a, spe...]
  transfers between devices with their start and end apart: 10 -> 10, of which waited for: 4 -> 4; matrix products, arithmetic and copies ran while one was open for 0% -> 0% of each run, Pallas kernels for 33% -> 32%
where the time goes in v5:
time: 35.6 us; the launch traced here: 35.3 us
  Pallas kernels  17.4 us (49%)
  starting transfers between devices  12.2 us (34%)
  waiting for transfers between devices  4.93 us (14%)
  between operations  0.76 us (2%)
    pallas_call x9, Pallas kernels, held(): run(*(pltpu.with_memory_space_constraint(a, spec.memory_space) for a, spe...  17.4 us
    ppermute x9, starting transfers between devices, swap(): lax.ppermute(value, 'sp', [(i, i ^ bit) for i in range(lax.axis_size('sp'...  6.38 us
    all_to_all x1, starting transfers between devices, body(): got = lax.all_to_all(ready, 'blk', split_axis=0, concat_axis=0, tiled=True)  5.83 us
    ppermute x9, waiting for transfers between devices, swap(): lax.ppermute(value, 'sp', [(i, i ^ bit) for i in range(lax.axis_size('sp'...  4.87 us
  transfers between devices with their start and end apart: 10, of which 4 were waited for; matrix products, arithmetic and copies ran while one was open for 0% of the time, Pallas kernels for 32%

profile of v5, /device:TPU:0, one launch (start us, length us, event | category | flops | bytes accessed | tf_op | source)
XLA Modules:
  0.0 35.3 jit_solution(3634116446855001801)
XLA Ops:
  0.6 0.5 %collective-permute-start.3 = (f32[2,32,4096]{2,1,0:T(8,128)}, f32[2,32,4096]{2,1,0:T(8,128)S(1)}, u32[]{:S(2)}, u32[]{:S(2)}) collective-permute-start(f32[2,32,4096]{2,1,0:T(8,128)} %species.5), channel_id=1, source_target_pairs={{0,1},{1,0},{2,3},{3,2},{4,5},{5,4},{6,7},{7,6},{8,9},{9,8},{10,11... | collective-permute-start | bytes 3145736 | tf_op jit(solution)/shard_map/ppermute | solution.py:761
  1.2 2.7 %pack_meta.1 = (f32[80,128]{1,0:T(8,128)S(1)}, f32[8,128]{1,0:T(8,128)S(1)}, f32[32,512]{1,0:T(8,128)S(1)}, f32[2,64,128]{2,1,0:T(8,128)S(1)}, f32[2,64,512]{2,1...) custom-call(f32[2,32,4096]{2,1,0:T(8,128)} %species.5, ...), custom_call_target="tpu_custom_call" | custom-call | bytes 10240000 | tf_op jit(solution)/shard_map/pack_meta/pallas_call | solution.py:708
  3.9 0.0 copy-start
  3.9 0.1 collective-permute-start
  4.0 2.6 %collective-permute-start.2 = (f32[80,128]{1,0:T(8,128)S(1)}, f32[80,128]{1,0:T(8,128)S(1)}, u32[]{:S(2)}, u32[]{:S(2)}) collective-permute-start(f32[80,128]{1,0:T(8,128)S(1)} %get-tuple-element.26.z_half.m0), channel_id=1, source_target_pairs={{0,3},{1,2},{2,1},{3,0},{4,7},{5,6},{6,5},{7,4},{8,11},{9,10},{10,... | collective-permute-start | bytes 122888 | tf_op jit(solution)/shard_map/ppermute | solution.py:761
  6.7 0.3 collective-permute-start.1
  7.0 0.1 collective-permute-start.4
  7.1 1.1 %pack_rows.1 = (f32[8,88,128]{2,1,0:T(8,128)S(1)}, f32[16,512]{1,0:T(8,128)S(1)}) custom-call(f32[256,128]{1,0:T(8,128)S(1)} %get-tuple-element.18.table_in, f32[8,4096]{1,0:T(8,128)S(1)} %get-tuple-element.19.vel_in, f32[8,4096]{1,0:T(8,128)S(1)} %get-tuple-element.20.dif_in, f32[32,512]{1,0:T(8,128)S(1)} %get-tuple-element.21.strips_ref, ...), custom_call_target="tpu_custom_call" | custom-call | bytes 10240000 | tf_op jit(solution)/shard_map/pack_rows/pallas_call | solution.py:708
  8.2 0.0 collective-permute-done.4.d_other
  8.2 0.9 %chip_sum.1 = (f32[16,4096]{1,0:T(8,128)S(1)}, f32[16,4096]{1,0:T(8,128)S(1)}) custom-call(f32[2,32,4096]{2,1,0:T(8,128)S(1)} %copy-done, f32[2,32,4096]{2,1,0:T(8,128)S(1)} %collective-permute-done.3.other_ref, f32[1,2]{1,0:T(1,128)} %bitcast.5, f32[1,2]{1,0:T(1,128)S(1)} %collective-permute-done.4.d_other, f32[80,128]{1,0:T(8,128)S(1)} %collective-permute-done.after0.m1, ...), custom_call_target="tpu_custom_call" | custom-call | bytes 4792320 | tf_op jit(solution)/shard_map/chip_sum/pallas_call | solution.py:708
  9.1 1.6 %collective-permute-done.1.refs_1_.m2 = f32[80,128]{1,0:T(8,128)S(1)} collective-permute-done((f32[80,128]{1,0:T(8,128)S(1)}, f32[80,128]{1,0:T(8,128)S(1)}, u32[]{:S(2)}, u32[]{:S(2)}) %collective-permute-start.1) | collective-permute-done | bytes 40992 | tf_op jit(solution)/shard_map/ppermute | solution.py:761
  10.7 1.1 %collective-permute-start.6 = (f32[16,4096]{1,0:T(8,128)S(1)}, f32[16,4096]{1,0:T(8,128)S(1)}, u32[]{:S(2)}, u32[]{:S(2)}) collective-permute-start(f32[16,4096]{1,0:T(8,128)S(1)} %after.1.z_half.near_ref), channel_id=1, source_target_pairs={{0,2},{1,3},{2,0},{3,1},{4,6},{5,7},{6,4},{7,5},{8,10},{9,11},{10,... | collective-permute-start | bytes 786440 | tf_op jit(solution)/shard_map/ppermute | solution.py:761
  11.7 0.8 %assemble.1 = f32[8,88,128]{2,1,0:T(8,128)} custom-call(f32[8,88,128]{2,1,0:T(8,128)S(1)} %get-tuple-element.27.buf_ref, f32[80,128]{1,0:T(8,128)S(1)} %get-tuple-element.26.z_half.m0, f32[80,128]{1,0:T(8,128)S(1)} %collective-permute-done.after0.m1, f32[80,128]{1,0:T(8,128)S(1)} %collective-permute-done.1.refs_1_.m2, ...), custom_call_target="tpu_custom_call" | custom-call | bytes 2949120 | tf_op jit(solution)/shard_map/assemble/pallas_call | solution.py:708
  12.5 5.8 %all-to-all-start = ((f32[8,88,128]{2,1,0:T(8,128)}), f32[8,88,128]{2,1,0:T(8,128)S(1)}, u32[]{:S(2)}, u32[]{:S(2)}) async-start(f32[8,88,128]{2,1,0:T(8,128)} %assemble.1), calls=%async_computation | async-start | bytes 720896 | tf_op jit(solution)/shard_map/all_to_all | solution.py:849
  18.4 0.1 collective-permute-start.7
  18.5 1.5 %collective-permute-start.5 = (f32[16,4096]{1,0:T(8,128)S(1)}, f32[16,4096]{1,0:T(8,128)S(1)}, u32[]{:S(2)}, u32[]{:S(2)}) collective-permute-start(f32[16,4096]{1,0:T(8,128)S(1)} %get-tuple-element.30.near_ref), channel_id=1, source_target_pairs={{0,2},{1,3},{2,0},{3,1},{4,6},{5,7},{6,4},{7,5},{8,10},{9,11},{10,... | collective-permute-start | bytes 786440 | tf_op jit(solution)/shard_map/ppermute | solution.py:761
  20.0 0.0 collective-permute-done.7.zb_ref
  20.0 5.5 %inner_flux.1 = (f32[2,32,4096]{2,1,0:T(8,128)S(1)}, f32[32,512]{1,0:T(8,128)S(1)}) custom-call(f32[3,32,4096]{2,1,0:T(8,128)} %flow.5, f32[3,32,4096]{2,1,0:T(8,128)} %diff.3, f32[32,4096]{1,0:T(8,128)} %vol.3, f32[2,32,4096]{2,1,0:T(8,128)} %species.5, f32[16,4096]{1,0:T(8,128)S(1)} %z_own.1.za_ref, f32[16,4096]{1,0:T(8,128)S(1)} %collective-permute-done.7.zb_ref, ...), custom_call_target="tpu_custom_call" | custom-call | bytes 25804800 | tf_op jit(solution)/shard_map/inner_flux/pallas_call | solution.py:708
  25.5 1.7 %collective-permute-done.5.far_ref = f32[16,4096]{1,0:T(8,128)S(1)} collective-permute-done((f32[16,4096]{1,0:T(8,128)S(1)}, f32[16,4096]{1,0:T(8,128)S(1)}, u32[]{:S(2)}, u32[]{:S(2)}) %collective-permute-start.5) | collective-permute-done | bytes 262176 | tf_op jit(solution)/shard_map/ppermute | solution.py:761
  27.2 0.1 collective-permute-start.8
  27.3 1.5 %collective-permute-done.8.other_ref = f32[16,4096]{1,0:T(8,128)S(1)} collective-permute-done((f32[16,4096]{1,0:T(8,128)S(1)}, f32[16,4096]{1,0:T(8,128)S(1)}, u32[]{:S(2)}, u32[]{:S(2)}) %collective-permute-start.8) | collective-permute-done | bytes 262176 | tf_op jit(solution)/shard_map/ppermute | solution.py:761
  28.8 0.2 fuel_parts.1.fuel_ref
  29.1 0.1 all-to-all-done.got_ref
  29.1 6.2 %final.1 = (f32[2,32,4096]{2,1,0:T(8,128)}, f32[384,128]{1,0:T(8,128)}) custom-call(f32[8,88,128]{2,1,0:T(8,128)S(1)} %all-to-all-done.got_ref, bf16[256,1024]{1,0:T(8,128)(2,1)S(1)} %fuel_parts.1.fuel_ref, f32[2,32,4096]{2,1,0:T(8,128)S(1)} %get-tuple-element.33.base_ref, f32[2,32,4096]{2,1,0:T(8,128)} %species.5, f32[32,4096]{1,0:T(8,128)} %vol.3, ...), custom_call_target="tpu_custom_call" | custom-call | bytes 33177600 | tf_op jit(solution)/shard_map/final/pallas_call | solution.py:708
  (10 shorter events, 0.1 us)
Async XLA Ops:
  0.6 7.6 %collective-permute-start.3 = (f32[2,32,4096]{2,1,0:T(8,128)}, f32[2,32,4096]{2,1,0:T(8,128)S(1)}, u32[]{:S(2)}, u32[]{:S(2)}) collective-permute-start(f32[2,32,4096]{2,1,0:T(8,128)} %species.5), channel_id=1, source_target_pairs={{0,1},{1,0},{2,3},{3,2},{4,5},{5,4},{6,7},{7,6},{8,9},{9,8},{10,11... | collective-permute-start | bytes 3145736 | tf_op jit(solution)/shard_map/ppermute | solution.py:761
  1.2 5.9 %copy-start.1 = (f32[2]{0:T(128)S(1)}, f32[2]{0:T(128)}, u32[]{:S(2)}) copy-start(f32[2]{0:T(128)} %param.17) | copy-start | bytes 28
  3.9 4.3 %copy-start = (f32[2,32,4096]{2,1,0:T(8,128)S(1)}, f32[2,32,4096]{2,1,0:T(8,128)}, u32[]{:S(2)}) copy-start(f32[2,32,4096]{2,1,0:T(8,128)} %species.5) | copy-start | bytes 3145732
  3.9 4.3 %collective-permute-start = (f32[80,128]{1,0:T(8,128)S(1)}, f32[80,128]{1,0:T(8,128)S(1)}, u32[]{:S(2)}, u32[]{:S(2)}) collective-permute-start(f32[80,128]{1,0:T(8,128)S(1)} %get-tuple-element.26.z_half.m0), channel_id=1, source_target_pairs={{0,1},{1,0},{2,3},{3,2},{4,5},{5,4},{6,7},{7,6},{8,9},{9,8},{10,11... | collective-permute-start | bytes 122888 | tf_op jit(solution)/shard_map/ppermute | solution.py:761
  4.0 5.1 %collective-permute-start.2 = (f32[80,128]{1,0:T(8,128)S(1)}, f32[80,128]{1,0:T(8,128)S(1)}, u32[]{:S(2)}, u32[]{:S(2)}) collective-permute-start(f32[80,128]{1,0:T(8,128)S(1)} %get-tuple-element.26.z_half.m0), channel_id=1, source_target_pairs={{0,3},{1,2},{2,1},{3,0},{4,7},{5,6},{6,5},{7,4},{8,11},{9,10},{10,... | collective-permute-start | bytes 122888 | tf_op jit(solution)/shard_map/ppermute | solution.py:761
  6.7 4.0 %collective-permute-start.1 = (f32[80,128]{1,0:T(8,128)S(1)}, f32[80,128]{1,0:T(8,128)S(1)}, u32[]{:S(2)}, u32[]{:S(2)}) collective-permute-start(f32[80,128]{1,0:T(8,128)S(1)} %get-tuple-element.26.z_half.m0), channel_id=1, source_target_pairs={{0,2},{1,3},{2,0},{3,1},{4,6},{5,7},{6,4},{7,5},{8,10},{9,11},{10,... | collective-permute-start | bytes 122888 | tf_op jit(solution)/shard_map/ppermute | solution.py:761
  7.0 1.2 %collective-permute-start.4 = (f32[1,2]{1,0:T(1,128)S(1)}, f32[1,2]{1,0:T(1,128)S(1)}, u32[]{:S(2)}, u32[]{:S(2)}) collective-permute-start(f32[1,2]{1,0:T(1,128)S(1)} %bitcast.6), channel_id=1, source_target_pairs={{0,1},{1,0},{2,3},{3,2},{4,5},{5,4},{6,7},{7,6},{8,9},{9,8},{10,11... | collective-permute-start | bytes 32 | tf_op jit(solution)/shard_map/ppermute | solution.py:761
  10.7 7.7 %collective-permute-start.6 = (f32[16,4096]{1,0:T(8,128)S(1)}, f32[16,4096]{1,0:T(8,128)S(1)}, u32[]{:S(2)}, u32[]{:S(2)}) collective-permute-start(f32[16,4096]{1,0:T(8,128)S(1)} %after.1.z_half.near_ref), channel_id=1, source_target_pairs={{0,2},{1,3},{2,0},{3,1},{4,6},{5,7},{6,4},{7,5},{8,10},{9,11},{10,... | collective-permute-start | bytes 786440 | tf_op jit(solution)/shard_map/ppermute | solution.py:761
  12.5 16.6 %all-to-all-start = ((f32[8,88,128]{2,1,0:T(8,128)}), f32[8,88,128]{2,1,0:T(8,128)S(1)}, u32[]{:S(2)}, u32[]{:S(2)}) async-start(f32[8,88,128]{2,1,0:T(8,128)} %assemble.1), calls=%async_computation | async-start | bytes 720896 | tf_op jit(solution)/shard_map/all_to_all | solution.py:849
  18.4 1.6 %collective-permute-start.7 = (f32[16,4096]{1,0:T(8,128)S(1)}, f32[16,4096]{1,0:T(8,128)S(1)}, u32[]{:S(2)}, u32[]{:S(2)}) collective-permute-start(f32[16,4096]{1,0:T(8,128)S(1)} %z_own.1.za_ref), channel_id=1, source_target_pairs={{0,1},{1,0},{2,3},{3,2},{4,5},{5,4},{6,7},{7,6},{8,9},{9,8},{10,11... | collective-permute-start | bytes 786440 | tf_op jit(solution)/shard_map/ppermute | solution.py:761
  18.5 8.7 %collective-permute-start.5 = (f32[16,4096]{1,0:T(8,128)S(1)}, f32[16,4096]{1,0:T(8,128)S(1)}, u32[]{:S(2)}, u32[]{:S(2)}) collective-permute-start(f32[16,4096]{1,0:T(8,128)S(1)} %get-tuple-element.30.near_ref), channel_id=1, source_target_pairs={{0,2},{1,3},{2,0},{3,1},{4,6},{5,7},{6,4},{7,5},{8,10},{9,11},{10,... | collective-permute-start | bytes 786440 | tf_op jit(solution)/shard_map/ppermute | solution.py:761
  27.2 1.6 %collective-permute-start.8 = (f32[16,4096]{1,0:T(8,128)S(1)}, f32[16,4096]{1,0:T(8,128)S(1)}, u32[]{:S(2)}, u32[]{:S(2)}) collective-permute-start(f32[16,4096]{1,0:T(8,128)S(1)} %fuel_half.1.own_ref), channel_id=1, source_target_pairs={{0,1},{1,0},{2,3},{3,2},{4,5},{5,4},{6,7},{7,6},{8,9},{9,8},{10,11... | collective-permute-start | bytes 786440 | tf_op jit(solution)/shard_map/ppermute | solution.py:761

commit v6 on v5

--- a/solution.py
+++ b/solution.py
@@ -558,34 +558,12 @@
     soft, sig = field(1, full), field(2, full)
     sublane = iota((LANES, LANES), 0)
     tall = iota((tall_rows, LANES), 0)
-    for c in range(chunks):
-        spots[:, c * LANES : (c + 1) * LANES] = ones(tall == cell_row[c : c + 1])
-    inside = inside_table()
-    p0, p1, p2, p3 = (pair(k) for k in range(PAIRS))
-    below0, below1, below_z = ghost_faces(
-        [(p0, 0), (p0, 1), (p3, 0)], strip_ref[1].astype(BF16)[:, 0:8], column_ref[1], inside
-    )
-    above0, above1, top_v, top_d, above_z = ghost_faces(
-        [(p1, 0), (p1, 1), (p2, 0), (p2, 1), (p3, 1)],
-        strip_ref[0].astype(BF16)[:, 0:8],
-        column_ref[0],
-        inside,
-    )
-    z_bottom, z_top = zedge_ref[0:8, :], zedge_ref[8:16, :]
-    bottom_scale, top_scale = section_step * zedge_ref[16:24, :], section_step * zedge_ref[24:32, :]
-    bottom_v, bottom_d = fedge_ref[0:8, :], fedge_ref[8:16, :]
-    for s, (below, above) in enumerate(((below0, above0), (below1, above1))):
-        d = m0[0:1, s : s + 1]
-        high = strips_ref[8 * s : 8 * s + 8, :]
-        low = strips_ref[16 + 8 * s : 24 + 8 * s, :]
-        f_low = flux(bottom_v, bottom_d, d, low, below, z_bottom - below_z)
-        f_high = flux(top_v, top_d, d, above, high, above_z - z_top)
-        edge[2 * s : 2 * s + 1, :] = from_strips(bottom_scale * f_low)
-        edge[2 * s + 1 : 2 * s + 2, :] = from_strips(top_scale * f_high)
     width = 2 * LANES
     lefts = iota((1, LANES), 1) < 64
     evaporated = []
     for c in range(0, chunks, 2):
+        for i in range(c, c + 2):
+            spots[:, i * LANES : (i + 1) * LANES] = ones(tall == cell_row[i : i + 1])
         both = mm(fuel_ref[...], spots[:, c * LANES : c * LANES + width])
         both = both[0:LANES] + both[LANES:]
         for i in range(2):
@@ -599,6 +577,28 @@
                 loads[k * LANES : (k + 1) * LANES, (c + i) * LANES : (c + i + 1) * LANES] = part
     source = mm_nt(spots[...], loads[...])
     source = source[:, 0:LANES] + source[:, LANES:]
+    inside = inside_table()
+    p0, p1, p2, p3 = (pair(k) for k in range(PAIRS))
+    below0, below1, below_z = ghost_faces(
+        [(p0, 0), (p0, 1), (p3, 0)], strip_ref[1].astype(BF16)[:, 0:8], column_ref[1], inside
+    )
+    above0, above1, top_v, top_d, above_z = ghost_faces(
+        [(p1, 0), (p1, 1), (p2, 0), (p2, 1), (p3, 1)],
+        strip_ref[0].astype(BF16)[:, 0:8],
+        column_ref[0],
+        inside,
+    )
+    z_bottom, z_top = zedge_ref[0:8, :], zedge_ref[8:16, :]
+    bottom_scale, top_scale = section_step * zedge_ref[16:24, :], section_step * zedge_ref[24:32, :]
+    bottom_v, bottom_d = fedge_ref[0:8, :], fedge_ref[8:16, :]
+    for s, (below, above) in enumerate(((below0, above0), (below1, above1))):
+        d = m0[0:1, s : s + 1]
+        high = strips_ref[8 * s : 8 * s + 8, :]
+        low = strips_ref[16 + 8 * s : 24 + 8 * s, :]
+        f_low = flux(bottom_v, bottom_d, d, low, below, z_bottom - below_z)
+        f_high = flux(top_v, top_d, d, above, high, above_z - z_top)
+        edge[2 * s : 2 * s + 1, :] = from_strips(bottom_scale * f_low)
+        edge[2 * s + 1 : 2 * s + 2, :] = from_strips(top_scale * f_high)
     row = iota((8, LANES), 0)
     delta = (jnp.where(lax.axis_index("sp") == 0, 1.0, 0.0), 0.0)
     for copy in fetch:
@@ -656,6 +656,7 @@
         axis=0,
     )
     none = jnp.zeros((6, LANES), F32)
+    lost, gathered = [], []
     for h in range(groups // 2):
         a, b = 2 * h, 2 * h + 1
         lanes = jnp.where(lefts, lane_of[a : a + 1], lane_of[b : b + 1])
@@ -663,11 +664,14 @@
         mask = mm_tn(lanes, spread) == iota((LANES, PV), 1).astype(F32)
         gone = jnp.where(lefts, evaporated[a : a + 1], evaporated[b : b + 1])
         head = gone.astype(BF16).astype(F32)
-        change = -mm_tn(jnp.concatenate([head, gone - head, none], axis=0).astype(BF16), take)
+        lost.append(mm_tn(jnp.concatenate([head, gone - head, none], axis=0).astype(BF16), take))
         fields = []
         for f in range(3):
             fields += split(jnp.where(mask, rows_ref[f, h * LANES : (h + 1) * LANES, :], 0.0), 2)
-        change = change + friction_timescale * mm(jnp.concatenate(fields, axis=1), into)
+        gathered.append(jnp.concatenate(fields, axis=1))
+    pulled = friction_timescale * mm(jnp.concatenate(gathered, axis=0), into)
+    for h in range(groups // 2):
+        change = pulled[h * LANES : (h + 1) * LANES] - lost[h]
         for i in range(2):
             g = 2 * h + i
             table = jnp.concatenate(

time: 35.6 us -> 35.3 us (level)
  no operation moved by 1% of the time
where the time goes in v6:
time: 35.3 us; the launch traced here: 35 us
  Pallas kernels  17.1 us (48%)
  starting transfers between devices  12.2 us (35%)
  waiting for transfers between devices  4.93 us (14%)
  between operations  0.76 us (2%)
    pallas_call x9, Pallas kernels, held(): run(*(pltpu.with_memory_space_constraint(a, spec.memory_space) for a, spe...  17.1 us
    ppermute x9, starting transfers between devices, swap(): lax.ppermute(value, 'sp', [(i, i ^ bit) for i in range(lax.axis_size('sp'...  6.38 us
    all_to_all x1, starting transfers between devices, body(): got = lax.all_to_all(ready, 'blk', split_axis=0, concat_axis=0, tiled=True)  5.83 us
    ppermute x9, waiting for transfers between devices, swap(): lax.ppermute(value, 'sp', [(i, i ^ bit) for i in range(lax.axis_size('sp'...  4.87 us
  transfers between devices with their start and end apart: 10, of which 4 were waited for; matrix products, arithmetic and copies ran while one was open for 0% of the time, Pallas kernels for 32%

profile of v6, /device:TPU:0, one launch (start us, length us, event | category | flops | bytes accessed | tf_op | source)
XLA Modules:
  0.0 35.0 jit_solution(16946986535604458067)
XLA Ops:
  0.6 0.5 %collective-permute-start.3 = (f32[2,32,4096]{2,1,0:T(8,128)}, f32[2,32,4096]{2,1,0:T(8,128)S(1)}, u32[]{:S(2)}, u32[]{:S(2)}) collective-permute-start(f32[2,32,4096]{2,1,0:T(8,128)} %species.5), channel_id=1, source_target_pairs={{0,1},{1,0},{2,3},{3,2},{4,5},{5,4},{6,7},{7,6},{8,9},{9,8},{10,11... | collective-permute-start | bytes 3145736 | tf_op jit(solution)/shard_map/ppermute | solution.py:765
  1.2 2.7 %pack_meta.1 = (f32[80,128]{1,0:T(8,128)S(1)}, f32[8,128]{1,0:T(8,128)S(1)}, f32[32,512]{1,0:T(8,128)S(1)}, f32[2,64,128]{2,1,0:T(8,128)S(1)}, f32[2,64,512]{2,1...) custom-call(f32[2,32,4096]{2,1,0:T(8,128)} %species.5, ...), custom_call_target="tpu_custom_call" | custom-call | bytes 10240000 | tf_op jit(solution)/shard_map/pack_meta/pallas_call | solution.py:712
  3.9 0.0 copy-start
  3.9 0.1 collective-permute-start
  4.0 2.6 %collective-permute-start.2 = (f32[80,128]{1,0:T(8,128)S(1)}, f32[80,128]{1,0:T(8,128)S(1)}, u32[]{:S(2)}, u32[]{:S(2)}) collective-permute-start(f32[80,128]{1,0:T(8,128)S(1)} %get-tuple-element.26.z_half.m0), channel_id=1, source_target_pairs={{0,3},{1,2},{2,1},{3,0},{4,7},{5,6},{6,5},{7,4},{8,11},{9,10},{10,... | collective-permute-start | bytes 122888 | tf_op jit(solution)/shard_map/ppermute | solution.py:765
  6.7 0.3 collective-permute-start.1
  7.0 0.1 collective-permute-start.4
  7.1 1.1 %pack_rows.1 = (f32[8,88,128]{2,1,0:T(8,128)S(1)}, f32[16,512]{1,0:T(8,128)S(1)}) custom-call(f32[256,128]{1,0:T(8,128)S(1)} %get-tuple-element.18.table_in, f32[8,4096]{1,0:T(8,128)S(1)} %get-tuple-element.19.vel_in, f32[8,4096]{1,0:T(8,128)S(1)} %get-tuple-element.20.dif_in, f32[32,512]{1,0:T(8,128)S(1)} %get-tuple-element.21.strips_ref, ...), custom_call_target="tpu_custom_call" | custom-call | bytes 10240000 | tf_op jit(solution)/shard_map/pack_rows/pallas_call | solution.py:712
  8.2 0.0 collective-permute-done.4.d_other
  8.2 0.9 %chip_sum.1 = (f32[16,4096]{1,0:T(8,128)S(1)}, f32[16,4096]{1,0:T(8,128)S(1)}) custom-call(f32[2,32,4096]{2,1,0:T(8,128)S(1)} %copy-done, f32[2,32,4096]{2,1,0:T(8,128)S(1)} %collective-permute-done.3.other_ref, f32[1,2]{1,0:T(1,128)} %bitcast.5, f32[1,2]{1,0:T(1,128)S(1)} %collective-permute-done.4.d_other, f32[80,128]{1,0:T(8,128)S(1)} %collective-permute-done.after0.m1, ...), custom_call_target="tpu_custom_call" | custom-call | bytes 4792320 | tf_op jit(solution)/shard_map/chip_sum/pallas_call | solution.py:712
  9.1 1.6 %collective-permute-done.1.refs_1_.m2 = f32[80,128]{1,0:T(8,128)S(1)} collective-permute-done((f32[80,128]{1,0:T(8,128)S(1)}, f32[80,128]{1,0:T(8,128)S(1)}, u32[]{:S(2)}, u32[]{:S(2)}) %collective-permute-start.1) | collective-permute-done | bytes 40992 | tf_op jit(solution)/shard_map/ppermute | solution.py:765
  10.7 1.1 %collective-permute-start.6 = (f32[16,4096]{1,0:T(8,128)S(1)}, f32[16,4096]{1,0:T(8,128)S(1)}, u32[]{:S(2)}, u32[]{:S(2)}) collective-permute-start(f32[16,4096]{1,0:T(8,128)S(1)} %after.1.z_half.near_ref), channel_id=1, source_target_pairs={{0,2},{1,3},{2,0},{3,1},{4,6},{5,7},{6,4},{7,5},{8,10},{9,11},{10,... | collective-permute-start | bytes 786440 | tf_op jit(solution)/shard_map/ppermute | solution.py:765
  11.7 0.8 %assemble.1 = f32[8,88,128]{2,1,0:T(8,128)} custom-call(f32[8,88,128]{2,1,0:T(8,128)S(1)} %get-tuple-element.27.buf_ref, f32[80,128]{1,0:T(8,128)S(1)} %get-tuple-element.26.z_half.m0, f32[80,128]{1,0:T(8,128)S(1)} %collective-permute-done.after0.m1, f32[80,128]{1,0:T(8,128)S(1)} %collective-permute-done.1.refs_1_.m2, ...), custom_call_target="tpu_custom_call" | custom-call | bytes 2949120 | tf_op jit(solution)/shard_map/assemble/pallas_call | solution.py:712
  12.5 5.8 %all-to-all-start = ((f32[8,88,128]{2,1,0:T(8,128)}), f32[8,88,128]{2,1,0:T(8,128)S(1)}, u32[]{:S(2)}, u32[]{:S(2)}) async-start(f32[8,88,128]{2,1,0:T(8,128)} %assemble.1), calls=%async_computation | async-start | bytes 720896 | tf_op jit(solution)/shard_map/all_to_all | solution.py:853
  18.4 0.1 collective-permute-start.7
  18.5 1.5 %collective-permute-start.5 = (f32[16,4096]{1,0:T(8,128)S(1)}, f32[16,4096]{1,0:T(8,128)S(1)}, u32[]{:S(2)}, u32[]{:S(2)}) collective-permute-start(f32[16,4096]{1,0:T(8,128)S(1)} %get-tuple-element.30.near_ref), channel_id=1, source_target_pairs={{0,2},{1,3},{2,0},{3,1},{4,6},{5,7},{6,4},{7,5},{8,10},{9,11},{10,... | collective-permute-start | bytes 786440 | tf_op jit(solution)/shard_map/ppermute | solution.py:765
  20.0 0.0 collective-permute-done.7.zb_ref
  20.0 5.5 %inner_flux.1 = (f32[2,32,4096]{2,1,0:T(8,128)S(1)}, f32[32,512]{1,0:T(8,128)S(1)}) custom-call(f32[3,32,4096]{2,1,0:T(8,128)} %flow.5, f32[3,32,4096]{2,1,0:T(8,128)} %diff.3, f32[32,4096]{1,0:T(8,128)} %vol.3, f32[2,32,4096]{2,1,0:T(8,128)} %species.5, f32[16,4096]{1,0:T(8,128)S(1)} %z_own.1.za_ref, f32[16,4096]{1,0:T(8,128)S(1)} %collective-permute-done.7.zb_ref, ...), custom_call_target="tpu_custom_call" | custom-call | bytes 25804800 | tf_op jit(solution)/shard_map/inner_flux/pallas_call | solution.py:712
  25.5 1.7 %collective-permute-done.5.far_ref = f32[16,4096]{1,0:T(8,128)S(1)} collective-permute-done((f32[16,4096]{1,0:T(8,128)S(1)}, f32[16,4096]{1,0:T(8,128)S(1)}, u32[]{:S(2)}, u32[]{:S(2)}) %collective-permute-start.5) | collective-permute-done | bytes 262176 | tf_op jit(solution)/shard_map/ppermute | solution.py:765
  27.2 0.1 collective-permute-start.8
  27.3 1.5 %collective-permute-done.8.other_ref = f32[16,4096]{1,0:T(8,128)S(1)} collective-permute-done((f32[16,4096]{1,0:T(8,128)S(1)}, f32[16,4096]{1,0:T(8,128)S(1)}, u32[]{:S(2)}, u32[]{:S(2)}) %collective-permute-start.8) | collective-permute-done | bytes 262176 | tf_op jit(solution)/shard_map/ppermute | solution.py:765
  28.8 0.2 fuel_parts.1.fuel_ref
  29.1 0.1 all-to-all-done.got_ref
  29.1 5.9 %final.1 = (f32[2,32,4096]{2,1,0:T(8,128)}, f32[384,128]{1,0:T(8,128)}) custom-call(f32[8,88,128]{2,1,0:T(8,128)S(1)} %all-to-all-done.got_ref, bf16[256,1024]{1,0:T(8,128)(2,1)S(1)} %fuel_parts.1.fuel_ref, f32[2,32,4096]{2,1,0:T(8,128)S(1)} %get-tuple-element.33.base_ref, f32[2,32,4096]{2,1,0:T(8,128)} %species.5, f32[32,4096]{1,0:T(8,128)} %vol.3, ...), custom_call_target="tpu_custom_call" | custom-call | bytes 33177600 | tf_op jit(solution)/shard_map/final/pallas_call | solution.py:712
  (10 shorter events, 0.1 us)
Async XLA Ops:
  0.6 7.6 %collective-permute-start.3 = (f32[2,32,4096]{2,1,0:T(8,128)}, f32[2,32,4096]{2,1,0:T(8,128)S(1)}, u32[]{:S(2)}, u32[]{:S(2)}) collective-permute-start(f32[2,32,4096]{2,1,0:T(8,128)} %species.5), channel_id=1, source_target_pairs={{0,1},{1,0},{2,3},{3,2},{4,5},{5,4},{6,7},{7,6},{8,9},{9,8},{10,11... | collective-permute-start | bytes 3145736 | tf_op jit(solution)/shard_map/ppermute | solution.py:765
  1.2 5.9 %copy-start.1 = (f32[2]{0:T(128)S(1)}, f32[2]{0:T(128)}, u32[]{:S(2)}) copy-start(f32[2]{0:T(128)} %param.17) | copy-start | bytes 28
  3.9 4.3 %copy-start = (f32[2,32,4096]{2,1,0:T(8,128)S(1)}, f32[2,32,4096]{2,1,0:T(8,128)}, u32[]{:S(2)}) copy-start(f32[2,32,4096]{2,1,0:T(8,128)} %species.5) | copy-start | bytes 3145732
  3.9 4.3 %collective-permute-start = (f32[80,128]{1,0:T(8,128)S(1)}, f32[80,128]{1,0:T(8,128)S(1)}, u32[]{:S(2)}, u32[]{:S(2)}) collective-permute-start(f32[80,128]{1,0:T(8,128)S(1)} %get-tuple-element.26.z_half.m0), channel_id=1, source_target_pairs={{0,1},{1,0},{2,3},{3,2},{4,5},{5,4},{6,7},{7,6},{8,9},{9,8},{10,11... | collective-permute-start | bytes 122888 | tf_op jit(solution)/shard_map/ppermute | solution.py:765
  4.0 5.1 %collective-permute-start.2 = (f32[80,128]{1,0:T(8,128)S(1)}, f32[80,128]{1,0:T(8,128)S(1)}, u32[]{:S(2)}, u32[]{:S(2)}) collective-permute-start(f32[80,128]{1,0:T(8,128)S(1)} %get-tuple-element.26.z_half.m0), channel_id=1, source_target_pairs={{0,3},{1,2},{2,1},{3,0},{4,7},{5,6},{6,5},{7,4},{8,11},{9,10},{10,... | collective-permute-start | bytes 122888 | tf_op jit(solution)/shard_map/ppermute | solution.py:765
  6.7 4.0 %collective-permute-start.1 = (f32[80,128]{1,0:T(8,128)S(1)}, f32[80,128]{1,0:T(8,128)S(1)}, u32[]{:S(2)}, u32[]{:S(2)}) collective-permute-start(f32[80,128]{1,0:T(8,128)S(1)} %get-tuple-element.26.z_half.m0), channel_id=1, source_target_pairs={{0,2},{1,3},{2,0},{3,1},{4,6},{5,7},{6,4},{7,5},{8,10},{9,11},{10,... | collective-permute-start | bytes 122888 | tf_op jit(solution)/shard_map/ppermute | solution.py:765
  7.0 1.2 %collective-permute-start.4 = (f32[1,2]{1,0:T(1,128)S(1)}, f32[1,2]{1,0:T(1,128)S(1)}, u32[]{:S(2)}, u32[]{:S(2)}) collective-permute-start(f32[1,2]{1,0:T(1,128)S(1)} %bitcast.6), channel_id=1, source_target_pairs={{0,1},{1,0},{2,3},{3,2},{4,5},{5,4},{6,7},{7,6},{8,9},{9,8},{10,11... | collective-permute-start | bytes 32 | tf_op jit(solution)/shard_map/ppermute | solution.py:765
  10.7 7.7 %collective-permute-start.6 = (f32[16,4096]{1,0:T(8,128)S(1)}, f32[16,4096]{1,0:T(8,128)S(1)}, u32[]{:S(2)}, u32[]{:S(2)}) collective-permute-start(f32[16,4096]{1,0:T(8,128)S(1)} %after.1.z_half.near_ref), channel_id=1, source_target_pairs={{0,2},{1,3},{2,0},{3,1},{4,6},{5,7},{6,4},{7,5},{8,10},{9,11},{10,... | collective-permute-start | bytes 786440 | tf_op jit(solution)/shard_map/ppermute | solution.py:765
  12.5 16.6 %all-to-all-start = ((f32[8,88,128]{2,1,0:T(8,128)}), f32[8,88,128]{2,1,0:T(8,128)S(1)}, u32[]{:S(2)}, u32[]{:S(2)}) async-start(f32[8,88,128]{2,1,0:T(8,128)} %assemble.1), calls=%async_computation | async-start | bytes 720896 | tf_op jit(solution)/shard_map/all_to_all | solution.py:853
  18.4 1.6 %collective-permute-start.7 = (f32[16,4096]{1,0:T(8,128)S(1)}, f32[16,4096]{1,0:T(8,128)S(1)}, u32[]{:S(2)}, u32[]{:S(2)}) collective-permute-start(f32[16,4096]{1,0:T(8,128)S(1)} %z_own.1.za_ref), channel_id=1, source_target_pairs={{0,1},{1,0},{2,3},{3,2},{4,5},{5,4},{6,7},{7,6},{8,9},{9,8},{10,11... | collective-permute-start | bytes 786440 | tf_op jit(solution)/shard_map/ppermute | solution.py:765
  18.5 8.7 %collective-permute-start.5 = (f32[16,4096]{1,0:T(8,128)S(1)}, f32[16,4096]{1,0:T(8,128)S(1)}, u32[]{:S(2)}, u32[]{:S(2)}) collective-permute-start(f32[16,4096]{1,0:T(8,128)S(1)} %get-tuple-element.30.near_ref), channel_id=1, source_target_pairs={{0,2},{1,3},{2,0},{3,1},{4,6},{5,7},{6,4},{7,5},{8,10},{9,11},{10,... | collective-permute-start | bytes 786440 | tf_op jit(solution)/shard_map/ppermute | solution.py:765
  27.2 1.6 %collective-permute-start.8 = (f32[16,4096]{1,0:T(8,128)S(1)}, f32[16,4096]{1,0:T(8,128)S(1)}, u32[]{:S(2)}, u32[]{:S(2)}) collective-permute-start(f32[16,4096]{1,0:T(8,128)S(1)} %fuel_half.1.own_ref), channel_id=1, source_target_pairs={{0,1},{1,0},{2,3},{3,2},{4,5},{5,4},{6,7},{7,6},{8,9},{9,8},{10,11... | collective-permute-start | bytes 786440 | tf_op jit(solution)/shard_map/ppermute | solution.py:765
